TPU v7x, 32 devices: a whole 2x2x4 slice. The times are simulated.
32 devices in a mesh: dp: 4 (over y, x), ctx: 4 (over z), tp: 2 (over core).
Axes of the slice: x: 2, y: 2, z: 4, core: 2. Of those that a mesh axis runs over, the one named last changes fastest.
Arguments:
- hidden_in: bfloat16 [8, 1024, 1024], P('dp', 'ctx'), may hold values from -6 to 6
- positions: int32 [8, 1024], P('dp', 'ctx'), may hold values from 0 to 1023, as said below
- gain_attn: bfloat16 [1024], P(('dp', 'ctx')), may hold values from 0.25 to 1.75
- w_qkv: bfloat16 [1024, 2, 384], P(('dp', 'ctx'), 'tp'), may hold values from -0.1875 to 0.1875
- w_attn_out: bfloat16 [512, 1024], P('tp', ('dp', 'ctx')), may hold values from -1.5 to 1.5
- w_zx: bfloat16 [1024, 2, 1536], P(('dp', 'ctx'), None, 'tp'), may hold values from -0.1875 to 0.1875
- w_bc: bfloat16 [1024, 256], P(('dp', 'ctx')), may hold values from -0.1875 to 0.1875
- w_dt: bfloat16 [1024, 24], P(('dp', 'ctx'), 'tp'), may hold values from -0.046875 to 0.046875
- conv_x: bfloat16 [4, 1536], P(None, 'tp'), may hold values from -3 to 3
- conv_bc: bfloat16 [4, 256], replicated, may hold values from -3 to 3
- a_log: float32 [24], P('tp'), may hold values from -1 to 3
- dt_bias: float32 [24], P('tp'), may hold values from -6 to -3
- d_skip: float32 [24], P('tp'), may hold values from 0.5 to 1.5
- w_mamba_out: bfloat16 [1536, 1024], P('tp', ('dp', 'ctx')), may hold values from -0.15625 to 0.15625
- gain_ffn: bfloat16 [1024], P(('dp', 'ctx')), may hold values from 0.25 to 1.75
- w_gu: bfloat16 [1024, 2, 2048], P(('dp', 'ctx'), None, 'tp'), may hold values from -0.1875 to 0.1875
- w_down: bfloat16 [2048, 1024], P('tp', ('dp', 'ctx')), may hold values from -0.125 to 0.125
- output_cotangent: bfloat16 [8, 1024, 1024], P('dp', 'ctx'), may hold values from -6 to 6
Outputs:
- block_out: bfloat16 [8, 1024, 1024], P('dp', 'ctx')
- d_hidden: bfloat16 [8, 1024, 1024], P('dp', 'ctx')
- grad_gain_attn: float32 [1024], P(('dp', 'ctx'))
- grad_w_qkv: float32 [1024, 2, 384], P(('dp', 'ctx'), 'tp')
- grad_w_attn_out: float32 [512, 1024], P('tp', ('dp', 'ctx'))
- grad_w_zx: float32 [1024, 2, 1536], P(('dp', 'ctx'), None, 'tp')
- grad_w_bc: float32 [1024, 256], P(('dp', 'ctx'))
- grad_w_dt: float32 [1024, 24], P(('dp', 'ctx'), 'tp')
- grad_conv_x: float32 [4, 1536], P(None, 'tp')
- grad_conv_bc: float32 [4, 256], replicated
- grad_a_log: float32 [24], P('tp')
- grad_dt_bias: float32 [24], P('tp')
- grad_d_skip: float32 [24], P('tp')
- grad_w_mamba_out: float32 [1536, 1024], P('tp', ('dp', 'ctx'))
- grad_gain_ffn: float32 [1024], P(('dp', 'ctx'))
- grad_w_gu: float32 [1024, 2, 2048], P(('dp', 'ctx'), None, 'tp')
- grad_w_down: float32 [2048, 1024], P('tp', ('dp', 'ctx'))
Inputs may be any that keep to these rules, and one draw needn't show every extreme that they name: Each row of 1024 tokens is packed with documents: a position of 0 starts a document and positions then rise by one. Every document but the last of a row has 60 to 800 tokens. Of the 2 rows of each index of dp, one row drawn from the seed is a single document.
All inputs are finite; a program needn't handle non-finite values.
Results may differ from a plain program's by a relative error of at most 0.02.
Values may be sent and summed in bfloat16 or wider, within the bound.
No kernel may reach another device: no remote copies, remote signals or barrier semaphores. Data moves between devices by JAX's collectives and lax.ppermute only.
A program may use at most 192 MiB of HBM per device.

v0:
```python
import math

import jax
import jax.numpy as jnp
from jax import lax
from jax.sharding import PartitionSpec as P

HD = 64
KC = 4


highest = lax.Precision.HIGHEST
rope_base = 100000000000.0


def from_behind(block, axis, distance):
    devices = range(lax.axis_size(axis))
    route = [(i - distance, i) for i in devices if i - distance in devices]
    return lax.ppermute(block, axis, route)


def carried_in(value, axis, combine, identity, reverse):
    count, index = (lax.axis_size(axis), lax.axis_index(axis))
    everything = jax.tree.map(
        lambda part, kind: lax.all_gather(part.astype(kind), axis),
        value,
        jax.tree.map(lambda a: jnp.bfloat16 if a.dtype == jnp.float32 else a.dtype, value),
    )
    start = jax.tree.map(
        lambda part, zero: jnp.broadcast_to(jnp.asarray(zero, part.dtype), part.shape),
        value,
        identity,
    )

    def hop(k, before):
        at = count - 1 - k if reverse else k
        reached = at > index if reverse else at < index
        new = combine(
            before, jax.tree.map(lambda part, own: part[at].astype(own.dtype), everything, value)
        )
        return jax.tree.map(lambda a, b: jnp.where(reached, a, b), new, before)

    return lax.fori_loop(0, count, hop, start)


def shortened(value):
    return jax.tree.map(lambda a: a.astype(jnp.bfloat16) if a.dtype == jnp.float32 else a, value)


def normed(values, gain):
    return values * lax.rsqrt(jnp.mean(values * values, axis=-1, keepdims=True) + 1e-05) * gain


def angles(pos, width):
    frequency = jnp.power(
        jnp.float32(rope_base), -jnp.arange(0, width, 2).astype(jnp.float32) / width
    )
    turned = pos.astype(jnp.float32)[..., None] * frequency
    return (jnp.cos(turned), jnp.sin(turned))


def rotate(values, cosine, sine):
    half = values.shape[-1] // 2
    first, second = (values[..., :half], values[..., half:])
    return jnp.concatenate(
        [first * cosine - second * sine, second * cosine + first * sine], axis=-1
    )


def rotate_back(grads, cosine, sine):
    half = grads.shape[-1] // 2
    first, second = (grads[..., :half], grads[..., half:])
    return jnp.concatenate(
        [first * cosine + second * sine, second * cosine - first * sine], axis=-1
    )


def conv_silu(values, tail, weights, pos):
    span = weights.shape[0]
    count = values.shape[1]
    joined = jnp.concatenate([tail, values], axis=1)
    total = jnp.zeros_like(values)
    for shift_by in range(span):
        piece = joined[:, span - 1 - shift_by : span - 1 - shift_by + count, :]
        total = (
            total + weights[shift_by] * piece * (pos >= shift_by).astype(jnp.float32)[:, :, None]
        )
    return jax.nn.silu(total)


def decay_sums(log_decay, pos):
    marks = jnp.cumsum((pos == 0).astype(jnp.int32), axis=1)
    return (jnp.cumsum(log_decay, axis=1), marks)


def stretch_end(inflow, b_vec, log_decay, pos):
    cumulated, marks = decay_sums(log_decay, pos)
    last = cumulated[:, -1, :]
    same = (marks == marks[:, -1:]).astype(jnp.float32)
    weight = jnp.exp(last[:, None, :] - cumulated) * same[:, :, None]
    ends = jnp.einsum("sthp,stn->shpn", weight[..., None] * inflow, b_vec, precision=highest)
    carry = jnp.exp(last) * (marks[:, -1] == 0).astype(jnp.float32)[:, None]
    return (ends, carry)


def stretch_inner(heads_x, inflow, b_vec, c_vec, log_decay, pos, d_skip):
    cumulated, marks = decay_sums(log_decay, pos)
    count = log_decay.shape[1]
    order = jnp.arange(count)
    valid = (order[:, None] >= order[None, :])[None] & (marks[:, :, None] == marks[:, None, :])
    differ = cumulated[:, :, None, :] - cumulated[:, None, :, :]
    mixing = jnp.exp(jnp.where(valid[..., None], differ, -1e30))
    scores = jnp.einsum("stn,srn->str", c_vec, b_vec, precision=highest)
    result = jnp.einsum("strh,srhp->sthp", mixing * scores[..., None], inflow, precision=highest)
    return result + d_skip[None, None, :, None] * heads_x


def stretch_read(c_vec, log_decay, pos, state):
    cumulated, marks = decay_sums(log_decay, pos)
    weight = jnp.exp(cumulated) * (marks == 0).astype(jnp.float32)[:, :, None]
    readout = jnp.einsum("stn,shpn->sthp", c_vec, state, precision=highest)
    return weight[..., None] * readout


def mamba_inputs(gate_input_rows, bc, dtr, tail_x, tail_bc, conv_x, conv_bc, a_log, dt_bias, pos):
    heads = a_log.shape[0]
    gate = gate_input_rows[:, :, 0, :]
    convolved = conv_silu(gate_input_rows[:, :, 1, :], tail_x, conv_x, pos)
    bc_conv = conv_silu(bc, tail_bc, conv_bc, pos)
    states = bc_conv.shape[2] // 2
    b_vec, c_vec = (bc_conv[..., :states], bc_conv[..., states:])
    step_size = jax.nn.softplus(dtr + dt_bias)
    log_decay = -jnp.exp(a_log) * step_size
    heads_x = convolved.reshape(convolved.shape[0], convolved.shape[1], heads, -1)
    inflow = heads_x * step_size[..., None]
    return (gate, heads_x, inflow, b_vec, c_vec, log_decay)


def mamba_all(
    gate_input_rows, bc, dtr, tail_x, tail_bc, conv_x, conv_bc, a_log, dt_bias, d_skip, state, pos
):
    gate, heads_x, inflow, b_vec, c_vec, log_decay = mamba_inputs(
        gate_input_rows, bc, dtr, tail_x, tail_bc, conv_x, conv_bc, a_log, dt_bias, pos
    )
    result = stretch_inner(heads_x, inflow, b_vec, c_vec, log_decay, pos, d_skip) + stretch_read(
        c_vec, log_decay, pos, state
    )
    gated = result.reshape(gate.shape) * jax.nn.silu(gate)
    ends, carry = stretch_end(inflow, b_vec, log_decay, pos)
    return (gated, ends, carry)


def link_states(earlier, later):
    return (earlier[0] * later[0], later[0][:, :, None, None] * earlier[1] + later[1])


def block_scores(q_low, key_value, key_begins, tokens, begins, number, width):
    size = q_low.shape[-1]
    piece = lax.dynamic_slice_in_dim(key_value, number * width, width, 1)
    piece_begins = lax.dynamic_slice_in_dim(key_begins, number * width, width, 1)
    key_tokens = number * width + jnp.arange(width, dtype=jnp.int32)
    scores = (
        jnp.einsum("sqrd,skd->srqk", q_low, piece[..., :size], preferred_element_type=jnp.float32)
        * 0.125
    )
    valid = (key_tokens[None, None, :] <= tokens[None, :, None]) & (
        piece_begins[:, None, :] == begins[:, :, None]
    )
    valid = valid[:, None]
    return (jnp.where(valid, scores, -1e30), valid, piece)


def attend(q_low, key_value, key_begins, tokens, begins, reach, width):
    seqs, block, per_group, size = q_low.shape
    start_state = (
        jnp.full((seqs, per_group, block), -1e30, jnp.float32),
        jnp.zeros((seqs, per_group, block), jnp.float32),
        jnp.zeros((seqs, per_group, block, size), jnp.float32),
    )

    def advance(number, running):
        best, total, accum = running
        scores, valid, piece = block_scores(
            q_low, key_value, key_begins, tokens, begins, number, width
        )
        top = jnp.maximum(best, jnp.max(scores, axis=-1))
        weights = jnp.where(valid, jnp.exp(scores - top[..., None]), 0.0)
        shrink = jnp.exp(best - top)
        total = total * shrink + jnp.sum(weights, axis=-1)
        update = jnp.einsum(
            "srqk,skd->srqd",
            weights.astype(jnp.bfloat16),
            piece[..., size:],
            preferred_element_type=jnp.float32,
        )
        return (top, total, accum * shrink[..., None] + update)

    best, total, accum = lax.fori_loop(0, reach, advance, start_state)
    result = jnp.transpose(accum / total[..., None], (0, 2, 1, 3))
    log_total = jnp.transpose(best + jnp.log(total), (0, 2, 1))
    return (result, log_total)


def attend_back(
    q_low, grad_out, log_total, row_dot, key_value, key_begins, tokens, begins, reach, width, buffer
):
    size = q_low.shape[-1]
    lse_rows = jnp.transpose(log_total, (0, 2, 1))
    dot_rows = jnp.transpose(row_dot, (0, 2, 1))

    def advance(number, running):
        grad_query, kept = running
        scores, valid, piece = block_scores(
            q_low, key_value, key_begins, tokens, begins, number, width
        )
        probs = jnp.where(valid, jnp.exp(scores - lse_rows[..., None]), 0.0)
        grad_prob = jnp.einsum(
            "sqrd,skd->srqk", grad_out, piece[..., size:], preferred_element_type=jnp.float32
        )
        grad_score = (probs * (grad_prob - dot_rows[..., None])).astype(jnp.bfloat16)
        grad_query = grad_query + jnp.einsum(
            "srqk,skd->sqrd", grad_score, piece[..., :size], preferred_element_type=jnp.float32
        )
        grad_key = (
            jnp.einsum("srqk,sqrd->skd", grad_score, q_low, preferred_element_type=jnp.float32)
            * 0.125
        )
        grad_value = jnp.einsum(
            "srqk,sqrd->skd",
            probs.astype(jnp.bfloat16),
            grad_out,
            preferred_element_type=jnp.float32,
        )
        older = lax.dynamic_slice_in_dim(kept, number * width, width, 1)
        kept = lax.dynamic_update_slice_in_dim(
            kept, older + jnp.concatenate([grad_key, grad_value], axis=-1), number * width, 1
        )
        return (grad_query, kept)

    grad_query, kept = lax.fori_loop(
        0, reach, advance, (jnp.zeros(q_low.shape, jnp.float32), buffer)
    )
    return (grad_query * 0.125, kept)


def per_device(
    hidden_in,
    positions,
    gain_attn,
    w_qkv,
    w_attn_out,
    w_zx,
    w_bc,
    w_dt,
    conv_x,
    conv_bc,
    a_log,
    dt_bias,
    d_skip,
    w_mamba_out,
    gain_ffn,
    w_gu,
    w_down,
    output_cotangent,
):
    (
        gain_a_all,
        qkv_all,
        attn_out_all,
        gate_input_every_layer,
        bc_all,
        dt_all,
        mamba_out_all,
        gain_f_all,
        gate_up_every_layer,
        down_all,
    ) = (
        lax.all_gather(gain_attn, ("dp", "ctx"), axis=0, tiled=True),
        lax.all_gather(w_qkv, ("dp", "ctx"), axis=0, tiled=True),
        lax.all_gather(w_attn_out, ("dp", "ctx"), axis=1, tiled=True),
        lax.all_gather(w_zx, ("dp", "ctx"), axis=0, tiled=True),
        lax.all_gather(w_bc, ("dp", "ctx"), axis=0, tiled=True),
        lax.all_gather(w_dt, ("dp", "ctx"), axis=0, tiled=True),
        lax.all_gather(w_mamba_out, ("dp", "ctx"), axis=1, tiled=True),
        lax.all_gather(gain_ffn, ("dp", "ctx"), axis=0, tiled=True),
        lax.all_gather(w_gu, ("dp", "ctx"), axis=0, tiled=True),
        lax.all_gather(w_down, ("dp", "ctx"), axis=1, tiled=True),
    )
    seqs, block = positions.shape
    place = lax.axis_index("ctx")
    tokens = place * block + jnp.arange(block, dtype=jnp.int32)
    begins = tokens[None, :] - positions
    x_full = hidden_in.astype(jnp.float32)
    gain_a = gain_a_all.astype(jnp.float32)
    hidden_after_mixer = normed(x_full, gain_a).astype(jnp.bfloat16)
    qkv_weight = qkv_all[:, 0, :]
    qkv = jnp.dot(hidden_after_mixer, qkv_weight, preferred_element_type=jnp.float32)
    per_group = qkv_weight.shape[1] // HD - 2
    queries = qkv[..., : per_group * HD].reshape(seqs, block, per_group, HD)
    keys = qkv[..., per_group * HD : (per_group + 1) * HD]
    values = qkv[..., (per_group + 1) * HD :]
    cosine, sine = angles(positions, HD)
    q_low = rotate(queries, cosine[:, :, None], sine[:, :, None]).astype(jnp.bfloat16)
    k_low = rotate(keys, cosine, sine).astype(jnp.bfloat16)
    v_low = values.astype(jnp.bfloat16)
    key_value, key_begins = (
        lax.all_gather(jnp.concatenate([k_low, v_low], axis=-1), "ctx", axis=1, tiled=True),
        lax.all_gather(begins, "ctx", axis=1, tiled=True),
    )
    width = math.gcd(512, key_value.shape[1])
    reach = ((place + 1) * block + width - 1) // width
    attended, log_total = attend(q_low, key_value, key_begins, tokens, begins, reach, width)
    output_reduced = attended.reshape(seqs, block, per_group * HD).astype(jnp.bfloat16)
    att = jnp.dot(output_reduced, attn_out_all, preferred_element_type=jnp.float32)
    gate_input_rows = jnp.einsum(
        "zuv,vce->zuce",
        hidden_after_mixer,
        gate_input_every_layer,
        preferred_element_type=jnp.float32,
    )
    bc = jnp.dot(hidden_after_mixer, bc_all, preferred_element_type=jnp.float32)
    dtr = jnp.dot(hidden_after_mixer, dt_all, preferred_element_type=jnp.float32)
    span = KC - 1
    tail_x, tail_bc = (
        from_behind(gate_input_rows[:, block - span :, 1, :].astype(jnp.bfloat16), "ctx", 1).astype(
            jnp.float32
        ),
        from_behind(bc[:, block - span :, :].astype(jnp.bfloat16), "ctx", 1).astype(jnp.float32),
    )
    taps_x = conv_x.astype(jnp.float32)
    taps_bc = conv_bc.astype(jnp.float32)
    gate, heads_x, inflow, b_vec, c_vec, log_decay = mamba_inputs(
        gate_input_rows, bc, dtr, tail_x, tail_bc, taps_x, taps_bc, a_log, dt_bias, positions
    )
    ends, carry = stretch_end(inflow, b_vec, log_decay, positions)
    _, state = carried_in(
        (carry, ends), "ctx", link_states, (jnp.ones_like(carry), jnp.zeros_like(ends)), False
    )
    mixed = stretch_inner(
        heads_x, inflow, b_vec, c_vec, log_decay, positions, d_skip
    ) + stretch_read(c_vec, log_decay, positions, state)
    gate_act = jax.nn.silu(gate)
    gated_reduced = (mixed.reshape(gate.shape) * gate_act).astype(jnp.bfloat16)
    mam = jnp.dot(gated_reduced, mamba_out_all, preferred_element_type=jnp.float32)
    mix = lax.psum((att + mam).astype(jnp.bfloat16), "tp").astype(jnp.float32)
    resid = x_full + mix
    gain_f = gain_f_all.astype(jnp.float32)
    hidden_after_feedforward = normed(resid, gain_f).astype(jnp.bfloat16)
    gate_up_rows = jnp.einsum(
        "xuv,vmp->xump",
        hidden_after_feedforward,
        gate_up_every_layer,
        preferred_element_type=jnp.float32,
    )
    gate_ff, up_ff = (gate_up_rows[:, :, 0], gate_up_rows[:, :, 1])
    hidden_state = (jax.nn.silu(gate_ff) * up_ff).astype(jnp.bfloat16)
    ffn = lax.psum(
        jnp.dot(hidden_state, down_all, preferred_element_type=jnp.float32).astype(jnp.bfloat16),
        "tp",
    ).astype(jnp.float32)
    block_out = (resid + ffn).astype(jnp.bfloat16)
    cotangent = output_cotangent.astype(jnp.float32)
    grad_hidden = jnp.dot(output_cotangent, down_all.T, preferred_element_type=jnp.float32)
    down_projection_gradient = jnp.einsum(
        "hcu,hci->ui", hidden_state, output_cotangent, preferred_element_type=jnp.float32
    )
    sigmoid_gate = jax.nn.sigmoid(gate_ff)
    grad_gate = grad_hidden * up_ff * (sigmoid_gate * (1.0 + gate_ff * (1.0 - sigmoid_gate)))
    grad_up = grad_hidden * gate_ff * sigmoid_gate
    gate_up_gradient_reduced = jnp.stack([grad_gate, grad_up], axis=2).astype(jnp.bfloat16)
    gate_up_gradient = jnp.einsum(
        "mxj,mxvo->jvo",
        hidden_after_feedforward,
        gate_up_gradient_reduced,
        preferred_element_type=jnp.float32,
    )
    grad_h_two = lax.psum(
        jnp.einsum(
            "bpuj,zuj->bpz",
            gate_up_gradient_reduced,
            gate_up_every_layer,
            preferred_element_type=jnp.float32,
        ).astype(jnp.bfloat16),
        "tp",
    ).astype(jnp.float32)
    _, norm_pull = jax.vjp(normed, resid, gain_f)
    grad_resid_norm, grad_gain_f = norm_pull(grad_h_two)
    grad_resid = cotangent + grad_resid_norm
    mixer_output_gradient = grad_resid.astype(jnp.bfloat16)
    attention_output_gradient = jnp.einsum(
        "pcg,pch->gh", output_reduced, mixer_output_gradient, preferred_element_type=jnp.float32
    )
    grad_mamba_out = jnp.einsum(
        "qhn,qhu->nu", gated_reduced, mixer_output_gradient, preferred_element_type=jnp.float32
    )
    grad_gated = jnp.dot(mixer_output_gradient, mamba_out_all.T, preferred_element_type=jnp.float32)
    grad_out_low = (
        jnp.dot(mixer_output_gradient, attn_out_all.T, preferred_element_type=jnp.float32)
        .astype(jnp.bfloat16)
        .reshape(seqs, block, per_group, HD)
    )

    def read_state(incoming):
        return stretch_read(c_vec, log_decay, positions, incoming).reshape(gate.shape) * gate_act

    _, read_pull = jax.vjp(read_state, state)
    (state_grad,) = read_pull(grad_gated)
    _, later_grad = carried_in(
        (carry, state_grad),
        "ctx",
        link_states,
        (jnp.ones_like(carry), jnp.zeros_like(state_grad)),
        True,
    )
    grad_carry = jnp.sum(later_grad * state, axis=(2, 3))

    def mixer(
        zx_value,
        bc_value,
        dtr_value,
        tail_one,
        tail_two,
        taps_one,
        taps_two,
        decay_value,
        bias_value,
        skip_value,
        incoming,
    ):
        return mamba_all(
            zx_value,
            bc_value,
            dtr_value,
            tail_one,
            tail_two,
            taps_one,
            taps_two,
            decay_value,
            bias_value,
            skip_value,
            incoming,
            positions,
        )

    _, mixer_pull = jax.vjp(
        mixer,
        gate_input_rows,
        bc,
        dtr,
        tail_x,
        tail_bc,
        taps_x,
        taps_bc,
        a_log,
        dt_bias,
        d_skip,
        state,
    )
    (
        grad_zx,
        grad_bc,
        grad_dtr,
        grad_tail_x,
        grad_tail_bc,
        grad_taps_x,
        grad_taps_bc,
        grad_decay,
        grad_bias,
        grad_skip,
        _,
    ) = mixer_pull((grad_gated, later_grad, grad_carry))
    back_x, back_bc = (
        from_behind(shortened(grad_tail_x), "ctx", -1).astype(grad_tail_x.dtype),
        from_behind(shortened(grad_tail_bc), "ctx", -1).astype(grad_tail_bc.dtype),
    )
    grad_zx = grad_zx.at[:, block - span :, 1, :].add(back_x)
    grad_bc = grad_bc.at[:, block - span :, :].add(back_bc)
    row_dot = jnp.sum(grad_out_low.astype(jnp.float32) * attended, axis=-1)
    buffer = jnp.zeros(key_value.shape, jnp.float32)
    grad_query, buffer = attend_back(
        q_low,
        grad_out_low,
        log_total,
        row_dot,
        key_value,
        key_begins,
        tokens,
        begins,
        reach,
        width,
        buffer,
    )
    key_grad = lax.psum_scatter(
        buffer.astype(jnp.bfloat16), "ctx", scatter_dimension=1, tiled=True
    ).astype(jnp.float32)
    grad_key, grad_value = (key_grad[..., :HD], key_grad[..., HD:])
    grad_query = rotate_back(grad_query, cosine[:, :, None], sine[:, :, None]).reshape(
        seqs, block, per_group * HD
    )
    grad_key = rotate_back(grad_key, cosine, sine)
    query_key_value_gradient_reduced = jnp.concatenate(
        [grad_query, grad_key, grad_value], axis=-1
    ).astype(jnp.bfloat16)
    query_key_value_gradient = jnp.einsum(
        "wpi,wpv->iv",
        hidden_after_mixer,
        query_key_value_gradient_reduced,
        preferred_element_type=jnp.float32,
    )[:, None, :]
    gate_input_gradient_reduced = grad_zx.astype(jnp.bfloat16)
    step_rate_gradient_reduced = grad_dtr.astype(jnp.bfloat16)
    grad_zx_weight = jnp.einsum(
        "bzw,bzfo->wfo",
        hidden_after_mixer,
        gate_input_gradient_reduced,
        preferred_element_type=jnp.float32,
    )
    grad_dt_weight = jnp.einsum(
        "nvx,nva->xa",
        hidden_after_mixer,
        step_rate_gradient_reduced,
        preferred_element_type=jnp.float32,
    )
    grad_h_part = jnp.dot(
        query_key_value_gradient_reduced, qkv_weight.T, preferred_element_type=jnp.float32
    )
    grad_h_part = grad_h_part + jnp.einsum(
        "gaqw,iqw->gai",
        gate_input_gradient_reduced,
        gate_input_every_layer,
        preferred_element_type=jnp.float32,
    )
    grad_h_part = grad_h_part + jnp.dot(
        step_rate_gradient_reduced, dt_all.T, preferred_element_type=jnp.float32
    )
    grad_h_sum, grad_bc_sum, grad_taps_bc_sum = (
        lax.psum(grad_h_part.astype(jnp.bfloat16), "tp").astype(jnp.float32),
        lax.psum(grad_bc.astype(jnp.bfloat16), "tp").astype(jnp.float32),
        lax.psum(grad_taps_bc.astype(jnp.bfloat16), "tp").astype(jnp.float32),
    )
    input_readout_gradient_reduced = grad_bc_sum.astype(jnp.bfloat16)
    grad_bc_weight = jnp.einsum(
        "aex,aej->xj",
        hidden_after_mixer,
        input_readout_gradient_reduced,
        preferred_element_type=jnp.float32,
    )
    grad_h_one = grad_h_sum + jnp.dot(
        input_readout_gradient_reduced, bc_all.T, preferred_element_type=jnp.float32
    )
    _, first_pull = jax.vjp(normed, x_full, gain_a)
    grad_x_norm, grad_gain_a = first_pull(grad_h_one)
    d_hidden = (grad_resid + grad_x_norm).astype(jnp.bfloat16)
    (
        out_gain_a,
        out_qkv,
        out_attn_out,
        out_zx,
        out_bc,
        out_dt,
        out_mamba_out,
        out_gain_f,
        out_gu,
        out_down,
    ) = (
        lax.psum_scatter(grad_gain_a, ("dp", "ctx"), scatter_dimension=0, tiled=True),
        lax.psum_scatter(query_key_value_gradient, ("dp", "ctx"), scatter_dimension=0, tiled=True),
        lax.psum_scatter(attention_output_gradient, ("dp", "ctx"), scatter_dimension=1, tiled=True),
        lax.psum_scatter(grad_zx_weight, ("dp", "ctx"), scatter_dimension=0, tiled=True),
        lax.psum_scatter(grad_bc_weight, ("dp", "ctx"), scatter_dimension=0, tiled=True),
        lax.psum_scatter(grad_dt_weight, ("dp", "ctx"), scatter_dimension=0, tiled=True),
        lax.psum_scatter(grad_mamba_out, ("dp", "ctx"), scatter_dimension=1, tiled=True),
        lax.psum_scatter(grad_gain_f, ("dp", "ctx"), scatter_dimension=0, tiled=True),
        lax.psum_scatter(gate_up_gradient, ("dp", "ctx"), scatter_dimension=0, tiled=True),
        lax.psum_scatter(down_projection_gradient, ("dp", "ctx"), scatter_dimension=1, tiled=True),
    )
    out_taps_x, out_taps_bc, out_decay, out_bias, out_skip = lax.psum(
        (grad_taps_x, grad_taps_bc_sum, grad_decay, grad_bias, grad_skip), ("dp", "ctx")
    )
    return (
        block_out,
        d_hidden,
        out_gain_a,
        out_qkv,
        out_attn_out,
        out_zx,
        out_bc,
        out_dt,
        out_taps_x,
        out_taps_bc,
        out_decay,
        out_bias,
        out_skip,
        out_mamba_out,
        out_gain_f,
        out_gu,
        out_down,
    )


def solution(mesh):
    in_specs = (
        P("dp", "ctx", None),
        P("dp", "ctx"),
        P(("dp", "ctx")),
        P(("dp", "ctx"), "tp", None),
        P("tp", ("dp", "ctx")),
        P(("dp", "ctx"), None, "tp"),
        P(("dp", "ctx"), None),
        P(("dp", "ctx"), "tp"),
        P(None, "tp"),
        P(),
        P("tp"),
        P("tp"),
        P("tp"),
        P("tp", ("dp", "ctx")),
        P(("dp", "ctx")),
        P(("dp", "ctx"), None, "tp"),
        P("tp", ("dp", "ctx")),
        P("dp", "ctx", None),
    )
    out_specs = (
        P("dp", "ctx", None),
        P("dp", "ctx", None),
        P(("dp", "ctx")),
        P(("dp", "ctx"), "tp", None),
        P("tp", ("dp", "ctx")),
        P(("dp", "ctx"), None, "tp"),
        P(("dp", "ctx"), None),
        P(("dp", "ctx"), "tp"),
        P(None, "tp"),
        P(),
        P("tp"),
        P("tp"),
        P("tp"),
        P("tp", ("dp", "ctx")),
        P(("dp", "ctx")),
        P(("dp", "ctx"), None, "tp"),
        P("tp", ("dp", "ctx")),
    )
    return jax.shard_map(
        per_device, mesh=mesh, in_specs=in_specs, out_specs=out_specs, check_vma=False
    )
```

profile of v0, /device:TPU:0, one launch (start us, length us, event | category | flops | bytes accessed | tf_op | source)
XLA Modules:
  0.0 1675.3 jit_solution(14930936025140116641)
XLA Ops:
  12.7 44.5 %all-reduce.26 = (bf16[1024]{0:T(1024)(128)(2,1)S(1)}, bf16[1024]{0:T(1024)(128)(2,1)}) all-reduce(bf16[1024]{0:T(1024)(128)(2,1)S(1)} %dynamic-update-slice.6, bf16[1024]{0:T(1024)(128)(2,1)S(1)} %dynamic-update-slice.7), channel_id=1, replica_groups=mesh['dp'=4,'ctx'=4,'tp'=2] {'dp','ctx'}, use_global_device_ids=true, to_apply=%add.21 | all-reduce | flops 2048 | bytes 8192
  59.3 45.2 %all_gather.61 = bf16[1024,256]{1,0:T(8,128)(2,1)S(1)} all-gather(bf16[64,256]{1,0:T(8,128)(2,1)} %param.36), channel_id=1, replica_groups=mesh['dp'=4,'ctx'=4,'tp'=2] {'dp','ctx'}, dimensions={0}, use_global_device_ids=true | all-gather | bytes 557056 | tf_op jit(solution)/shard_map/all_gather | solution.py:282
  107.6 36.0 %all-gather.2 = bf16[16,64,12]{1,2,0:T(8,128)(2,1)S(1)} all-gather(bf16[1,64,12]{1,2,0:T(8,128)(2,1)S(1)} %bitcast.525), channel_id=1, replica_groups=mesh['dp'=4,'ctx'=4,'tp'=2] {'dp','ctx'}, dimensions={0}, use_global_device_ids=true | all-gather | bytes 26112 | tf_op jit(solution)/shard_map/all_gather | solution.py:283
  169.6 54.8 %all_gather.56 = bf16[1024,1,384]{2,0,1:T(8,128)(2,1)S(1)} all-gather(bf16[64,1,384]{2,0,1:T(8,128)(2,1)} %param.33), channel_id=1, replica_groups=mesh['dp'=4,'ctx'=4,'tp'=2] {'dp','ctx'}, dimensions={0}, use_global_device_ids=true | all-gather | bytes 835584 | tf_op jit(solution)/shard_map/all_gather | solution.py:279
  227.2 12.0 all_gather.54
  240.8 17.0 %all_gather.57 = bf16[2,1024,128]{2,1,0:T(8,128)(2,1)S(1)} all-gather(bf16[2,256,128]{2,1,0:T(8,128)(2,1)S(1)} %pad_maximum_fusion.8), channel_id=1, replica_groups=mesh['dp'=4,'ctx'=4,'tp'=2] {'ctx'}, dimensions={1}, use_global_device_ids=true | all-gather | bytes 655360 | tf_op jit(solution)/shard_map/all_gather | solution.py:307
  268.0 49.1 %all_gather.58 = bf16[256,1024]{0,1:T(8,128)(2,1)} all-gather(bf16[256,64]{0,1:T(8,128)(2,1)} %param.34), channel_id=1, replica_groups=mesh['dp'=4,'ctx'=4,'tp'=2] {'dp','ctx'}, dimensions={1}, use_global_device_ids=true | all-gather | bytes 557056 | tf_op jit(solution)/shard_map/all_gather | solution.py:280
  357.2 15.8 all-reduce.32.cloned.1.call-done
  374.7 79.0 %all-gather.14.cloned.1.call-done = bf16[1024,2,1024]{2,0,1:T(8,128)(2,1)} async-done(((bf16[64,2,1024]{2,0,1:T(8,128)(2,1)}), bf16[1024,2,1024]{2,0,1:T(8,128)(2,1)}) %all-gather.14.cloned.1.call-update) | async-done | bytes 4194320 | tf_op jit(solution)/shard_map/all_gather | solution.py:286
  460.4 55.7 %all-gather.16.cloned.1.call-done = bf16[1024,1024]{0,1:T(8,128)(2,1)} async-done(((bf16[1024,64]{0,1:T(8,128)(2,1)}), bf16[1024,1024]{0,1:T(8,128)(2,1)}) %all-gather.16.cloned.1.call-update) | async-done | bytes 2097168 | tf_op jit(solution)/shard_map/all_gather | solution.py:287
  531.7 13.6 all-reduce.34.cloned.1.call-done
  552.2 14.3 while.61
  584.4 11.3 fusion.56
  616.1 27.1 %all-gather.20.cloned.1.call-done = bf16[8,12,64,128]{3,2,1,0:T(8,128)(2,1)} async-done(((bf16[2,12,64,128]{3,2,1,0:T(8,128)(2,1)}), bf16[8,12,64,128]{3,2,1,0:T(8,128)(2,1)}) %all-gather.20.cloned.1.call-update) | async-done | bytes 1572880 | tf_op jit(solution)/shard_map/all_gather | solution.py:25
  652.3 9.6 multiply_reduce_fusion.7
  752.2 67.1 %reduce-scatter.28.cloned.1.call-done = f32[64,12]{1,0:T(8,128)} async-done(((f32[1024,12]{1,0:T(8,128)}), f32[64,12]{1,0:T(8,128)}) %reduce-scatter.28.cloned.1.call-update) | async-done | bytes 3088
  820.7 124.2 %reduce-scatter.14.cloned.1.call-done = f32[64,1,384]{2,0,1:T(8,128)} async-done(((f32[1024,1,384]{2,0,1:T(8,128)}), f32[64,1,384]{2,0,1:T(8,128)}) %reduce-scatter.14.cloned.1.call-update) | async-done | bytes 98320 | tf_op jit(solution)/shard_map/reduce_scatter | solution.py:567
  950.3 75.7 %all-reduce.25 = (f32[1024]{0:T(1024)S(1)}, f32[4,768]{1,0:T(4,128)}, f32[4,256]{1,0:T(4,128)}, f32[12]{0:T(128)}, f32[12]{0:T(128)}, /*index=5*/f32[12]{0:T(128)}, f32[1024]{0:T(1024)S(1)}) all-reduce(f32[1024]{0:T(1024)S(1)} %get-tuple-element.723, ...), channel_id=5, replica_groups=mesh['dp'=4,'ctx'=4,'tp'=2] {'dp','ctx'}, use_global_device_ids=true, to_apply=%region_40.41.clone | all-reduce | flops 6180 | bytes 47392
  1031.4 63.9 %reduce-scatter.18.cloned.1.call-done = f32[64,2,768]{2,0,1:T(8,128)} async-done(((f32[1024,2,768]{2,0,1:T(8,128)}), f32[64,2,768]{2,0,1:T(8,128)}) %reduce-scatter.18.cloned.1.call-update) | async-done | bytes 393232 | tf_op jit(solution)/shard_map/reduce_scatter | solution.py:569
  1097.4 181.6 %reduce-scatter.24.cloned.1.call-done = f32[64,2,1024]{2,0,1:T(8,128)} async-done(((f32[1024,2,1024]{2,0,1:T(8,128)}), f32[64,2,1024]{2,0,1:T(8,128)}) %reduce-scatter.24.cloned.1.call-update) | async-done | bytes 524304 | tf_op jit(solution)/shard_map/reduce_scatter | solution.py:574
  1281.2 76.9 %reduce-scatter.16.cloned.1.call-done = f32[256,64]{0,1:T(8,128)} async-done(((f32[256,1024]{0,1:T(8,128)}), f32[256,64]{0,1:T(8,128)}) %reduce-scatter.16.cloned.1.call-update) | async-done | bytes 65552 | tf_op jit(solution)/shard_map/reduce_scatter | solution.py:568
  1358.1 133.4 %reduce-scatter.22.cloned.1.call-done = f32[768,64]{0,1:T(8,128)} async-done(((f32[768,1024]{0,1:T(8,128)}), f32[768,64]{0,1:T(8,128)}) %reduce-scatter.22.cloned.1.call-update) | async-done | bytes 196624 | tf_op jit(solution)/shard_map/reduce_scatter | solution.py:572
  1491.5 81.1 %reduce-scatter.20.cloned.1.call-done = f32[64,256]{1,0:T(8,128)} async-done(((f32[1024,256]{1,0:T(8,128)}), f32[64,256]{1,0:T(8,128)}) %reduce-scatter.20.cloned.1.call-update) | async-done | bytes 65552 | tf_op jit(solution)/shard_map/reduce_scatter | solution.py:570
  1572.5 95.5 %reduce-scatter.26.cloned.1.call-done = f32[1024,64]{0,1:T(8,128)} async-done(((f32[1024,1024]{0,1:T(8,128)}), f32[1024,64]{0,1:T(8,128)}) %reduce-scatter.26.cloned.1.call-update) | async-done | bytes 262160 | tf_op jit(solution)/shard_map/reduce_scatter | solution.py:575
  (598 shorter events, 306.5 us)
Async XLA Ops:
  7.2 144.8 %all-gather.10.cloned.1.call-start = ((), (), s32[]{:S(2)}) async-start(), calls=%async_computation.9 | async-start | bytes 3342336 | tf_op jit(solution)/shard_map/all_gather | solution.py:281
  9.0 321.4 %all-gather.18.cloned.1.call-start = ((), (), s32[]{:S(2)}) async-start(), calls=%async_computation.23 | async-start | bytes 1966080 | tf_op jit(solution)/shard_map/all_gather | solution.py:25
  105.8 44.9 %collective-permute-start.1 = (bf16[2,3,256]{2,1,0:T(4,128)(2,1)S(1)}, bf16[2,3,256]{2,1,0:T(4,128)(2,1)S(1)}, u32[]{:S(2)}, u32[]{:S(2)}) collective-permute-start(bf16[2,3,256]{2,1,0:T(4,128)(2,1)S(1)} %slice.483), channel_id=1, source_target_pairs={{0,2},{2,4},{4,6},{1,3},{3,5},{5,7},{8,10},{10,12},{12,14},{9,11},... | collective-permute-start | bytes 9224 | tf_op jit(solution)/shard_map/ppermute | solution.py:19
  149.2 435.1 %copy-start.58 = (f32[2,256,12]{1,2,0:T(8,128)}, f32[2,256,12]{1,2,0:T(8,128)S(1)}, u32[]{:S(2)}) copy-start(f32[2,256,12]{1,2,0:T(8,128)S(1)} %add_select_fusion) | copy-start | bytes 73732
  156.1 5.2 collective-permute-start
  168.1 183.1 %all-gather.12.cloned.1.call-start = ((), (), s32[]{:S(2)}) async-start(), calls=%async_computation.10 | async-start | bytes 1671168 | tf_op jit(solution)/shard_map/all_gather | solution.py:284
  168.8 204.2 %all-reduce.32.cloned.1.call-start = ((), (), s32[]{:S(2)}) async-start(), calls=%async_computation.11 | async-start | bytes 2097152 | tf_op jit(solution)/shard_map/psum | solution.py:345
  355.5 98.3 %all-gather.14.cloned.1.call-start = ((), (), s32[]{:S(2)}) async-start(), calls=%async_computation.12 | async-start | bytes 4456448 | tf_op jit(solution)/shard_map/all_gather | solution.py:286
  356.3 159.9 %all-gather.16.cloned.1.call-start = ((), (), s32[]{:S(2)}) async-start(), calls=%async_computation.13 | async-start | bytes 2228224 | tf_op jit(solution)/shard_map/all_gather | solution.py:287
  356.9 188.4 %all-reduce.34.cloned.1.call-start = ((), (), s32[]{:S(2)}) async-start(), calls=%async_computation.14 | async-start | bytes 2097152 | tf_op jit(solution)/shard_map/psum | solution.py:377
  357.1 191.4 %copy-start.83 = (f32[1024]{0:T(1024)}, f32[1024]{0:T(1024)S(1)}, u32[]{:S(2)}) copy-start(f32[1024]{0:T(1024)S(1)} %convert_element_type.284) | copy-start | bytes 12292
  526.9 80.0 %reduce-scatter.12.cloned.1.call-start = ((), (), s32[]{:S(2)}) async-start(), calls=%async_computation.15 | async-start | bytes 655360 | tf_op jit(solution)/shard_map/reduce_scatter | solution.py:493
  568.6 74.6 %all-gather.20.cloned.1.call-start = ((), (), s32[]{:S(2)}) async-start(), calls=%async_computation.24 | async-start | bytes 1966080 | tf_op jit(solution)/shard_map/all_gather | solution.py:25
  583.6 157.7 %all-reduce.36.cloned.1.call-start = ((), (), s32[]{:S(2)}) async-start(), calls=%async_computation.26 | async-start | bytes 4718592 | tf_op jit(solution)/shard_map/psum | solution.py:357
  677.9 30.7 %collective-permute-start.2 = (bf16[2,3,768]{2,1,0:T(4,128)(2,1)}, bf16[2,3,768]{2,1,0:T(4,128)(2,1)}, u32[]{:S(2)}, u32[]{:S(2)}) collective-permute-start(bf16[2,3,768]{2,1,0:T(4,128)(2,1)} %split.25), channel_id=1, source_target_pairs={{2,0},{4,2},{6,4},{3,1},{5,3},{7,5},{10,8},{12,10},{14,12},{11,9},... | collective-permute-start | bytes 27656 | tf_op jit(solution)/shard_map/ppermute | solution.py:19
  702.3 6.1 collective-permute-start.3
  716.6 102.7 %reduce-scatter.28.cloned.1.call-start = ((), (), s32[]{:S(2)}) async-start(), calls=%async_computation.25 | async-start | bytes 557056
  718.7 226.2 %reduce-scatter.14.cloned.1.call-start = ((), (), s32[]{:S(2)}) async-start(), calls=%async_computation.16 | async-start | bytes 1671168 | tf_op jit(solution)/shard_map/reduce_scatter | solution.py:567
  720.9 374.5 %reduce-scatter.18.cloned.1.call-start = ((), (), s32[]{:S(2)}) async-start(), calls=%async_computation.18 | async-start | bytes 6684672 | tf_op jit(solution)/shard_map/reduce_scatter | solution.py:569
  725.6 553.3 %reduce-scatter.24.cloned.1.call-start = ((), (), s32[]{:S(2)}) async-start(), calls=%async_computation.21 | async-start | bytes 8912896 | tf_op jit(solution)/shard_map/reduce_scatter | solution.py:574
  734.4 623.7 %reduce-scatter.16.cloned.1.call-start = ((), (), s32[]{:S(2)}) async-start(), calls=%async_computation.17 | async-start | bytes 1114112 | tf_op jit(solution)/shard_map/reduce_scatter | solution.py:568
  737.3 754.1 %reduce-scatter.22.cloned.1.call-start = ((), (), s32[]{:S(2)}) async-start(), calls=%async_computation.20 | async-start | bytes 3342336 | tf_op jit(solution)/shard_map/reduce_scatter | solution.py:572
  741.3 831.2 %reduce-scatter.20.cloned.1.call-start = ((), (), s32[]{:S(2)}) async-start(), calls=%async_computation.19 | async-start | bytes 1114112 | tf_op jit(solution)/shard_map/reduce_scatter | solution.py:570
  744.1 924.0 %reduce-scatter.26.cloned.1.call-start = ((), (), s32[]{:S(2)}) async-start(), calls=%async_computation.22 | async-start | bytes 4456448 | tf_op jit(solution)/shard_map/reduce_scatter | solution.py:575
  (153 other events, 2508.1 us)
Sparse Core Ops, SparseCore 0:
  11.3 73.0 all-gather.9
  168.2 41.9 all-gather.17
  213.1 60.5 all-gather.11
  355.6 17.3 all-reduce.31
  376.6 77.1 all-gather.13
  456.8 59.3 all-gather.15
  527.0 18.2 all-reduce.33
  568.7 36.8 reduce-scatter.11
  607.8 35.4 all-gather.19
  716.7 21.3 all-reduce.35
  741.1 78.1 reduce-scatter.27
  823.9 120.9 reduce-scatter.13
  950.2 145.1 reduce-scatter.17
  1097.5 181.4 reduce-scatter.23
  1281.6 76.4 reduce-scatter.15
  1364.3 127.1 reduce-scatter.21
  1494.2 78.2 reduce-scatter.19
  1575.2 92.7 reduce-scatter.25
where the time goes:
time: 1690 us; the launch traced here: 1680 us
  waiting for transfers between devices  1020 us (60%)
  blocking collectives  344 us (20%)
  matrix products  145 us (9%)
  other arithmetic  82.7 us (5%)
  local copies, waits for them, and re-layouts  53.7 us (3%)
  between operations  18 us (1%)
    reduce_scatter x1, waiting for transfers between devices, per_device(): lax.psum_scatter(gate_up_gradient, ('dp', 'ctx'), scatter_dimension=0, ti...  182 us
    reduce_scatter x1, waiting for transfers between devices, per_device(): lax.psum_scatter(grad_mamba_out, ('dp', 'ctx'), scatter_dimension=1, tile...  133 us
    reduce_scatter x1, waiting for transfers between devices, per_device(): lax.psum_scatter(query_key_value_gradient, ('dp', 'ctx'), scatter_dimensi...  124 us
    unnamed x2, blocking collectives  120 us
    reduce_scatter x1, waiting for transfers between devices, per_device(): lax.psum_scatter(down_projection_gradient, ('dp', 'ctx'), scatter_dimensi...  95.5 us
    reduce_scatter x1, waiting for transfers between devices, per_device(): lax.psum_scatter(grad_bc_weight, ('dp', 'ctx'), scatter_dimension=0, tile...  81.1 us
    all_gather x1, waiting for transfers between devices, per_device(): lax.all_gather(w_gu, ('dp', 'ctx'), axis=0, tiled=True)  79 us
    reduce_scatter x1, waiting for transfers between devices, per_device(): lax.psum_scatter(attention_output_gradient, ('dp', 'ctx'), scatter_dimens...  76.9 us
  transfers between devices with their start and end apart: 22, of which 15 were waited for; matrix products, arithmetic and copies ran while one was open for 11% of the time, Pallas kernels for 0%

commit v1 on v0

v1 whole, which is shorter than its diff:
```python
import functools

import jax
import jax.numpy as jnp
from jax import lax
from jax.experimental import pallas as pl
from jax.experimental.pallas import tpu as pltpu
from jax.sharding import PartitionSpec as P

HD = 64
KC = 4
TAIL = 8
LANES = 128
VMEM_LIMIT = 56 * 1024 * 1024

f32 = jnp.float32
bf16 = jnp.bfloat16
highest = lax.Precision.HIGHEST
rope_base = 100000000000.0


def small_mesh():
    return lax.axis_size("dp") == 4 and lax.axis_size("ctx") == 4


def swap(value, axis, bits):
    count = lax.axis_size(axis)
    return lax.ppermute(value, axis, [(i, i ^ bits) for i in range(count)])


def shifted(value, axis, distance):
    count = lax.axis_size(axis)
    route = [(i - distance, i) for i in range(count) if 0 <= i - distance < count]
    return lax.ppermute(value, axis, route)


def assemble(me, pieces, outs, copies):
    count = len(pieces)
    total = len(outs)

    def kernel(me_ref, *refs):
        ins = refs[:count]
        outputs = refs[count : count + total]
        sems = refs[count + total]
        place = me_ref[0]
        running = []
        for number, (piece, first, width, out, bits) in enumerate(copies):
            copy = pltpu.make_async_copy(
                ins[piece].at[:, pl.ds(first, width)],
                outputs[out].at[jnp.bitwise_xor(place, bits)],
                sems.at[number],
            )
            copy.start()
            running.append(copy)
        for copy in running:
            copy.wait()

    return pl.pallas_call(
        kernel,
        out_shape=[jax.ShapeDtypeStruct(shape, pieces[0].dtype) for shape in outs],
        in_specs=[pl.BlockSpec(memory_space=pltpu.SMEM)]
        + [pl.BlockSpec(memory_space=pl.ANY)] * count,
        out_specs=[pl.BlockSpec(memory_space=pltpu.VMEM)] * total,
        scratch_shapes=[pltpu.SemaphoreType.DMA((len(copies),))],
        compiler_params=pltpu.CompilerParams(vmem_limit_bytes=VMEM_LIMIT),
        name="assemble",
    )(me.reshape(1), *pieces)


def gather_rows(packed, widths):
    rows = packed.shape[0]
    if not small_mesh():
        whole = lax.all_gather(packed, ("dp", "ctx"), axis=0, tiled=True)
        outs, first = [], 0
        for width in widths:
            outs.append(whole[:, first : first + width])
            first += width
        return outs
    dp, ctx = lax.axis_index("dp"), lax.axis_index("ctx")
    along = [packed] + [swap(packed, "ctx", k) for k in (1, 2, 3)]
    copies, first = [], 0
    for number, width in enumerate(widths):
        copies += [(k, first, width, number, k) for k in range(4)]
        first += width
    held = assemble(ctx, along, [(4, rows, width) for width in widths], copies)
    held = [h.reshape(4 * rows, h.shape[2]) for h in held]
    pieces, copies = [], []
    if len(held) == 1:
        for k in range(4):
            pieces.append(held[0] if k == 0 else swap(held[0], "dp", k))
            copies.append((k, 0, widths[0], 0, k))
    else:
        for number, (one, two) in enumerate(((1, 2), (2, 1))):
            mine = held[number]
            near = swap(mine, "dp", one)
            for bits, piece in (
                (0, mine),
                (one, near),
                (two, swap(mine, "dp", two)),
                (3, swap(near, "dp", two)),
            ):
                copies.append((len(pieces), 0, widths[number], number, bits))
                pieces.append(piece)
    full = assemble(dp, pieces, [(4, 4 * rows, width) for width in widths], copies)
    return [w.reshape(16 * rows, w.shape[2]) for w in full]


def pick(value, index, axis):
    return lax.dynamic_index_in_dim(value, index, axis, keepdims=False)


def scatter_rows(grads):
    if not small_mesh():
        joined = jnp.concatenate(grads, axis=1) if len(grads) > 1 else grads[0]
        return lax.psum_scatter(
            joined, ("dp", "ctx"), scatter_dimension=0, tiled=True
        ).astype(f32)
    dp, ctx = lax.axis_index("dp"), lax.axis_index("ctx")
    y, x = dp // 2, dp % 2
    rows = grads[0].shape[0]
    if len(grads) == 1:
        blocks = grads[0].reshape(4, rows // 4, -1)
        total = pick(blocks, dp, 0).astype(f32)
        for k in (1, 2, 3):
            total = total + swap(pick(blocks, dp ^ k, 0), "dp", k).astype(f32)
        held = total.astype(bf16)
    else:
        parts = []
        for number, grad in enumerate(grads):
            blocks = grad.reshape(2, 2, rows // 4, -1)
            one, two = (2, 1) if number == 0 else (1, 2)
            axis = 0 if number == 0 else 1
            at, then = (y, x) if number == 0 else (x, y)
            got = swap(pick(blocks, 1 - at, axis), "dp", one)
            kept = pick(blocks, at, axis)
            send = (pick(kept, 1 - then, 0).astype(f32) + pick(got, 1 - then, 0).astype(f32)).astype(
                bf16
            )
            near = swap(send, "dp", two)
            parts.append(
                (
                    pick(kept, then, 0).astype(f32)
                    + pick(got, then, 0).astype(f32)
                    + near.astype(f32)
                ).astype(bf16)
            )
        held = jnp.concatenate(parts, axis=1)
    blocks = held.reshape(4, rows // 16, -1)
    total = pick(blocks, ctx, 0).astype(f32)
    for k in (1, 2, 3):
        total = total + swap(pick(blocks, ctx ^ k, 0), "ctx", k).astype(f32)
    return total


def sum_all(value, axes):
    for axis in axes:
        count = lax.axis_size(axis)
        if count & (count - 1):
            value = lax.psum(value, axis)
            continue
        bits = 1
        while bits < count:
            value = value + swap(value, axis, bits)
            bits *= 2
    return value


def pair_sum(value):
    if lax.axis_size("tp") != 2:
        return lax.psum(value.astype(bf16), "tp").astype(f32)
    low = value.astype(bf16)
    return low.astype(f32) + swap(low, "tp", 1).astype(f32)


def behind(value):
    count, me = lax.axis_size("ctx"), lax.axis_index("ctx")
    if count <= 4:
        return [value] + [shifted(value, "ctx", d) for d in range(1, count)]
    everything = lax.all_gather(value, "ctx")
    out = [value]
    for d in range(1, count):
        there = pick(everything, lax.rem(me - d + count, count), 0)
        out.append(jnp.where(me >= d, there, jnp.zeros_like(there)))
    return out


def chained(carry, ends, reverse):
    count, me = lax.axis_size("ctx"), lax.axis_index("ctx")
    low = ends.astype(bf16)
    if count <= 4:
        sign = -1 if reverse else 1
        total, factor = None, None
        for d in range(1, count):
            piece = shifted(low, "ctx", sign * d).astype(f32)
            if factor is None:
                total = piece
                factor = jnp.ones_like(carry[0])
            else:
                total = total + factor[:, None, :] * piece
            there = me - sign * d
            factor = factor * pick(carry, jnp.clip(there, 0, count - 1), 0)
        return total
    everything = lax.all_gather(low, "ctx")

    def hop(k, before):
        at = count - 1 - k if reverse else k
        reached = at > me if reverse else at < me
        new = pick(carry, at, 0)[:, None, :] * before + pick(everything, at, 0).astype(f32)
        return jnp.where(reached, new, before)

    return lax.fori_loop(0, count, hop, jnp.zeros(ends.shape, f32))


def dot(a, b):
    return jnp.dot(a, b, preferred_element_type=f32)


def dot_nt(a, b):
    return lax.dot_general(a, b, (((1,), (1,)), ((), ())), preferred_element_type=f32)


def sig(v):
    return 1.0 / (1.0 + jnp.exp(-v))


def conv_pre(joined, span, taps, pos, count):
    total = None
    for k in range(KC):
        piece = joined[TAIL - k : TAIL - k + count, span]
        term = taps[k : k + 1, :] * piece
        if k:
            term = term * (pos >= k).astype(f32)
        total = term if total is None else total + term
    return total


def lane_ids(shape):
    return lax.broadcasted_iota(jnp.int32, shape, 1)


def decay_parts(dtr, head_row, pos, heads):
    count = dtr.shape[0]
    lane = lane_ids(dtr.shape)
    pre = dtr + head_row[1:2, :]
    dt = jnp.where(lane < heads, jnp.maximum(pre, 0.0) + jnp.log(1.0 + jnp.exp(-jnp.abs(pre))), 0.0)
    la = -jnp.exp(head_row[0:1, :]) * dt
    marked = jnp.where(lane == LANES - 1, (pos == 0).astype(f32), la)
    row = lax.broadcasted_iota(jnp.int32, (count, count), 0)
    col = lax.broadcasted_iota(jnp.int32, (count, count), 1)
    lower = (row >= col).astype(f32)
    summed = jnp.dot(lower, marked, precision=highest, preferred_element_type=f32)
    return pre, dt, la, summed


def wide(value, lane):
    return jnp.broadcast_to(value[:, lane : lane + 1], (value.shape[0], LANES))


def pair(value, j, low_half):
    return jnp.where(low_half, wide(value, 2 * j), wide(value, 2 * j + 1))


def mixer_local_kernel(
    heads, xr_ref, xt_ref, bc_ref, bt_ref, dtr_ref, tx_ref, tb_ref, hr_ref, pos_ref,
    y_ref, e_ref, c_ref, l_ref, jx, jb,
):
    count = xr_ref.shape[1]
    pos = pos_ref[0]
    head_row = hr_ref[...]
    jx[0:TAIL, :] = xt_ref[0]
    jx[TAIL : TAIL + count, :] = xr_ref[0]
    jb[0:TAIL, :] = bt_ref[0]
    jb[TAIL : TAIL + count, :] = bc_ref[0]
    pre_b = conv_pre(jb, slice(0, 2 * LANES), tb_ref[...], pos, count)
    bc = pre_b * sig(pre_b)
    b_low = bc[:, :LANES].astype(bf16)
    c_low = bc[:, LANES:].astype(bf16)
    c_ref[0] = c_low
    bt_low = jnp.transpose(bc[:, :LANES]).astype(bf16)
    _, dt, _, summed = decay_parts(dtr_ref[0], head_row, pos, heads)
    l_ref[0] = summed
    rows = jnp.transpose(summed)
    row = lax.broadcasted_iota(jnp.int32, (count, count), 0)
    col = lax.broadcasted_iota(jnp.int32, (count, count), 1)
    marks = summed[:, LANES - 1 : LANES]
    valid = (row >= col) & (marks == rows[LANES - 1 : LANES, :])
    scores = dot_nt(c_low, b_low)
    last = summed[count - 1 : count, :]
    same = (marks == last[:, LANES - 1 : LANES]).astype(f32)
    low_half = lane_ids((count, LANES)) < HD
    for j in range(heads // 2):
        span = slice(j * LANES, (j + 1) * LANES)
        pre = conv_pre(jx, span, tx_ref[:, span], pos, count)
        xc = pre * sig(pre)
        u = xc * pair(dt, j, low_half)
        u_low = u.astype(bf16)
        results = []
        for h in (2 * j, 2 * j + 1):
            differ = summed[:, h : h + 1] - rows[h : h + 1, :]
            mixing = jnp.exp(jnp.where(valid, differ, -1e30)) * scores
            results.append(dot(mixing.astype(bf16), u_low))
        skip = pair(head_row[2:3, :], j, low_half[0:1, :])
        y_ref[0, :, span] = jnp.where(low_half, results[0], results[1]) + skip * xc
        left = jnp.exp(pair(last, j, low_half[0:1, :]) - pair(summed, j, low_half)) * same
        e_ref[0, :, span] = dot(bt_low, (left * u).astype(bf16))


def mixer_local(xr, xt, bc, bt, dtr, taps_x, taps_bc, head_row, pos, heads):
    seqs, count, width = xr.shape
    states = bc.shape[2] // 2

    def whole(a):
        return pl.BlockSpec(a.shape, lambda s: (0,) * a.ndim)

    def per_seq(a):
        return pl.BlockSpec((1,) + a.shape[1:], lambda s: (s,) + (0,) * (a.ndim - 1))

    outs = [
        jax.ShapeDtypeStruct((seqs, count, width), f32),
        jax.ShapeDtypeStruct((seqs, states, width), f32),
        jax.ShapeDtypeStruct((seqs, count, states), bf16),
        jax.ShapeDtypeStruct((seqs, count, LANES), f32),
    ]
    return pl.pallas_call(
        functools.partial(mixer_local_kernel, heads),
        grid=(seqs,),
        out_shape=outs,
        in_specs=[
            per_seq(xr), per_seq(xt), per_seq(bc), per_seq(bt), per_seq(dtr),
            whole(taps_x), whole(taps_bc), whole(head_row), per_seq(pos),
        ],
        out_specs=[per_seq(o) for o in outs],
        scratch_shapes=[
            pltpu.VMEM((count + TAIL, width), f32),
            pltpu.VMEM((count + TAIL, 2 * states), f32),
        ],
        compiler_params=pltpu.CompilerParams(vmem_limit_bytes=VMEM_LIMIT),
        name="mixer_local",
    )(xr, xt, bc, bt, dtr, taps_x, taps_bc, head_row, pos)


def mixer_back_kernel(
    heads, xr_ref, xt_ref, bc_ref, bt_ref, dtr_ref, tx_ref, tb_ref, hr_ref, pos_ref,
    dy_ref, y_ref, st_ref, de_ref, dcl_ref,
    dx_ref, dbc_ref, ddt_ref, gtx_ref, gtb_ref, gh_ref,
    jx, jb, ax, ab,
):
    count = xr_ref.shape[1]
    states = LANES
    pos = pos_ref[0]
    head_row = hr_ref[...]
    jx[0:TAIL, :] = xt_ref[0]
    jx[TAIL : TAIL + count, :] = xr_ref[0]
    jb[0:TAIL, :] = bt_ref[0]
    jb[TAIL : TAIL + count, :] = bc_ref[0]
    pre_b = conv_pre(jb, slice(0, 2 * LANES), tb_ref[...], pos, count)
    sig_b = sig(pre_b)
    bc = pre_b * sig_b
    b_low = bc[:, :states].astype(bf16)
    c_low = bc[:, states:].astype(bf16)
    pre_dt, dt, la, summed = decay_parts(dtr_ref[0], head_row, pos, heads)
    rows = jnp.transpose(summed)
    row = lax.broadcasted_iota(jnp.int32, (count, count), 0)
    col = lax.broadcasted_iota(jnp.int32, (count, count), 1)
    marks = summed[:, LANES - 1 : LANES]
    valid = (row <= col) & (marks == rows[LANES - 1 : LANES, :])
    scores = dot_nt(b_low, c_low)
    last = summed[count - 1 : count, :]
    same = (marks == last[:, LANES - 1 : LANES]).astype(f32)
    first = (marks == 0.0).astype(f32)
    low_half = lane_ids((count, LANES)) < HD
    low_row = low_half[0:1, :]
    lane = lane_ids((LANES, LANES))
    lane_row = lax.broadcasted_iota(jnp.int32, (LANES, LANES), 0)
    d_scores = jnp.zeros((count, count), f32)
    d_b = jnp.zeros((count, states), f32)
    d_c = jnp.zeros((count, states), f32)
    d_sum = jnp.zeros((count, LANES), f32)
    d_dt = jnp.zeros((count, LANES), f32)
    d_end = jnp.zeros((1, LANES), f32)
    d_skip = jnp.zeros((1, LANES), f32)
    ax[...] = jnp.zeros_like(ax)
    ab[...] = jnp.zeros_like(ab)
    for j in range(heads // 2):
        span = slice(j * LANES, (j + 1) * LANES)
        taps = tx_ref[:, span]
        pre = conv_pre(jx, span, taps, pos, count)
        sg = sig(pre)
        xc = pre * sg
        dt_wide = pair(dt, j, low_half)
        u = xc * dt_wide
        u_low = u.astype(bf16)
        dy = dy_ref[0, :, span].astype(f32)
        dy_low = dy.astype(bf16)
        state = st_ref[0, :, span].astype(bf16)
        d_state = de_ref[0, :, span].astype(bf16)
        results = []
        for i, h in enumerate((2 * j, 2 * j + 1)):
            differ = rows[h : h + 1, :] - summed[:, h : h + 1]
            decay = jnp.exp(jnp.where(valid, differ, -1e30))
            half = low_half if i == 0 else jnp.logical_not(low_half)
            u_half = jnp.where(half, u, 0.0).astype(bf16)
            d_scores = d_scores + decay * dot_nt(u_half, dy_low)
            results.append(dot((decay * scores).astype(bf16), dy_low))
        left = jnp.exp(pair(last, j, low_row) - pair(summed, j, low_half)) * same
        reads = jnp.exp(pair(summed, j, low_half)) * first
        du_end = left * dot(b_low, d_state)
        du_in = jnp.where(low_half, results[0], results[1])
        du = du_in + du_end
        d_c = d_c + dot_nt((reads * dy).astype(bf16), state)
        d_b = d_b + dot_nt((left * u).astype(bf16), d_state)
        skip = pair(head_row[2:3, :], j, low_row)
        chosen = (
            ((lane == 2 * j) & (lane_row < HD)) | ((lane == 2 * j + 1) & (lane_row >= HD))
        ).astype(f32)
        per_token = (
            dy_low.astype(f32) * (y_ref[0, :, span] - skip * xc)
            - u_low.astype(f32) * du_in
            - u * du_end
        )
        d_sum = d_sum + jnp.dot(per_token, chosen, precision=highest, preferred_element_type=f32)
        d_dt = d_dt + jnp.dot(du * xc, chosen, precision=highest, preferred_element_type=f32)
        d_end = d_end + jnp.dot(
            jnp.sum(u * du_end, axis=0, keepdims=True), chosen, precision=highest,
            preferred_element_type=f32,
        )
        d_skip = d_skip + jnp.dot(
            jnp.sum(dy * xc, axis=0, keepdims=True), chosen, precision=highest,
            preferred_element_type=f32,
        )
        d_pre = (du * dt_wide + skip * dy) * (sg * (1.0 + pre * (1.0 - sg)))
        for k in range(KC):
            masked = d_pre * (pos >= k).astype(f32) if k else d_pre
            gtx_ref[0, k : k + 1, span] = jnp.sum(
                masked * jx[TAIL - k : TAIL - k + count, span], axis=0, keepdims=True
            )
            ax[TAIL - k : TAIL - k + count, span] += taps[k : k + 1, :] * masked
    dx_ref[0] = ax[...].astype(dx_ref.dtype)
    d_b = d_b + dot(d_scores.astype(bf16), c_low)
    d_c = d_c + dot(jnp.transpose(d_scores).astype(bf16), b_low)
    d_pre = jnp.concatenate([d_b, d_c], axis=1) * (sig_b * (1.0 + pre_b * (1.0 - sig_b)))
    for k in range(KC):
        masked = d_pre * (pos >= k).astype(f32) if k else d_pre
        gtb_ref[0, k : k + 1, :] = jnp.sum(
            masked * jb[TAIL - k : TAIL - k + count, :], axis=0, keepdims=True
        )
        ab[TAIL - k : TAIL - k + count, :] += tb_ref[k : k + 1, :] * masked
    dbc_ref[0] = ab[...].astype(dbc_ref.dtype)
    token = lax.broadcasted_iota(jnp.int32, (count, LANES), 0)
    at_last = d_end + dcl_ref[0]
    d_sum = d_sum + jnp.where(token == count - 1, at_last, 0.0)
    upper = (row <= col).astype(f32)
    d_la = jnp.dot(upper, d_sum, precision=highest, preferred_element_type=f32)
    d_la = jnp.where(lane_ids(d_la.shape) < heads, d_la, 0.0)
    d_dt = d_dt - jnp.exp(head_row[0:1, :]) * d_la
    d_dtr = d_dt * sig(pre_dt)
    d_dtr = jnp.where(lane_ids(d_dtr.shape) < heads, d_dtr, 0.0)
    ddt_ref[0, 0:TAIL, :] = jnp.zeros((TAIL, LANES), ddt_ref.dtype)
    ddt_ref[0, TAIL:, :] = d_dtr.astype(ddt_ref.dtype)
    gh_ref[0, 0:1, :] = jnp.sum(d_la * la, axis=0, keepdims=True)
    gh_ref[0, 1:2, :] = jnp.sum(d_dtr, axis=0, keepdims=True)
    gh_ref[0, 2:3, :] = d_skip
    gh_ref[0, 3:8, :] = jnp.zeros((5, LANES), f32)


def mixer_back(
    xr, xt, bc, bt, dtr, taps_x, taps_bc, head_row, pos, dy, y, state, d_ends, d_carry, heads
):
    seqs, count, width = xr.shape
    states = bc.shape[2] // 2

    def whole(a):
        return pl.BlockSpec(a.shape, lambda s: (0,) * a.ndim)

    def per_seq(a):
        return pl.BlockSpec((1,) + a.shape[1:], lambda s: (s,) + (0,) * (a.ndim - 1))

    outs = [
        jax.ShapeDtypeStruct((seqs, count + TAIL, width), f32),
        jax.ShapeDtypeStruct((seqs, count + TAIL, 2 * states), f32),
        jax.ShapeDtypeStruct((seqs, count + TAIL, LANES), f32),
        jax.ShapeDtypeStruct((seqs, KC, width), f32),
        jax.ShapeDtypeStruct((seqs, KC, 2 * states), f32),
        jax.ShapeDtypeStruct((seqs, 8, LANES), f32),
    ]
    args = (xr, xt, bc, bt, dtr, taps_x, taps_bc, head_row, pos, dy, y, state, d_ends, d_carry)
    shared = (5, 6, 7)
    return pl.pallas_call(
        functools.partial(mixer_back_kernel, heads),
        grid=(seqs,),
        out_shape=outs,
        in_specs=[whole(a) if i in shared else per_seq(a) for i, a in enumerate(args)],
        out_specs=[per_seq(o) for o in outs],
        scratch_shapes=[
            pltpu.VMEM((count + TAIL, width), f32),
            pltpu.VMEM((count + TAIL, 2 * states), f32),
            pltpu.VMEM((count + TAIL, width), f32),
            pltpu.VMEM((count + TAIL, 2 * states), f32),
        ],
        compiler_params=pltpu.CompilerParams(vmem_limit_bytes=VMEM_LIMIT),
        name="mixer_back",
    )(*args)


def attention_mask(tokens, begins, key_tokens, key_begins):
    return (key_tokens[:, None, :] <= tokens[:, :, None]) & (
        key_begins[:, None, :] == begins[:, :, None]
    )


def attend_one(q, k, v, mask):
    scores = jnp.einsum("qrd,kd->rqk", q, k, preferred_element_type=f32) * 0.125
    scores = jnp.where(mask[None], scores, -1e30)
    top = jnp.max(scores, axis=-1, keepdims=True)
    weights = jnp.where(mask[None], jnp.exp(scores - top), 0.0)
    total = jnp.sum(weights, axis=-1, keepdims=True)
    out = jnp.einsum("rqk,kd->qrd", (weights / total).astype(bf16), v, preferred_element_type=f32)
    return out, (top + jnp.log(total))[..., 0]


def attend_one_back(q, k, v, mask, d_out, lse, row_dot):
    scores = jnp.einsum("qrd,kd->rqk", q, k, preferred_element_type=f32) * 0.125
    probs = jnp.where(mask[None], jnp.exp(scores - lse[..., None]), 0.0)
    d_probs = jnp.einsum("qrd,kd->rqk", d_out, v, preferred_element_type=f32)
    d_scores = (probs * (d_probs - row_dot[..., None])).astype(bf16)
    d_q = jnp.einsum("rqk,kd->qrd", d_scores, k, preferred_element_type=f32) * 0.125
    d_k = jnp.einsum("rqk,qrd->kd", d_scores, q, preferred_element_type=f32) * 0.125
    d_v = jnp.einsum("rqk,qrd->kd", probs.astype(bf16), d_out, preferred_element_type=f32)
    return d_q, jnp.concatenate([d_k, d_v], axis=-1)


def over_seqs(function, args):
    if small_mesh():
        return jax.vmap(function)(*args)
    return lax.map(lambda a: function(*a), args)


def return_to_owners(kept):
    count, me = lax.axis_size("ctx"), lax.axis_index("ctx")
    low = kept.astype(bf16)
    if count <= 4:
        total = kept[:, 0]
        for d in range(1, count):
            total = total + shifted(low[:, d], "ctx", -d).astype(f32)
        return total
    places = lax.rem(me - jnp.arange(count) + count, count)
    ordered = jnp.take(low, places, axis=1)
    seqs, _, rows, width = ordered.shape
    ordered = ordered.reshape(seqs, count * rows, width)
    return lax.psum_scatter(ordered, "ctx", scatter_dimension=1, tiled=True).astype(f32)


def turn_matrix(columns):
    source = jnp.arange(columns)[:, None]
    target = jnp.arange(columns)[None, :]
    half = HD // 2
    low = target % HD < half
    minus = low & (source == target + half)
    plus = jnp.logical_not(low) & (source == target - half)
    return plus.astype(f32) - minus.astype(f32)


def per_device(
    hidden_in,
    positions,
    gain_attn,
    w_qkv,
    w_attn_out,
    w_zx,
    w_bc,
    w_dt,
    conv_x,
    conv_bc,
    a_log,
    dt_bias,
    d_skip,
    w_mamba_out,
    gain_ffn,
    w_gu,
    w_down,
    output_cotangent,
):
    seqs, block = positions.shape
    features = hidden_in.shape[2]
    rows = w_qkv.shape[0]
    heads = a_log.shape[0]
    inner = w_zx.shape[2]
    both = w_bc.shape[1]
    states = both // 2
    columns = w_qkv.shape[2]
    per_group = columns // HD - 2
    qwidth = per_group * HD
    units = w_gu.shape[2]
    count = lax.axis_size("ctx")
    place = lax.axis_index("ctx")
    tokens_here = seqs * block

    pad = jnp.zeros((rows, LANES - heads - 2), bf16)
    first_pack = jnp.concatenate(
        [w_zx[:, 1, :], w_bc, w_dt, gain_attn[:, None], gain_ffn[:, None], pad], axis=1
    )
    second_pack = jnp.concatenate(
        [w_qkv[:, 0, :], w_zx[:, 0, :], w_attn_out.T, w_mamba_out.T], axis=1
    )
    third_pack = jnp.concatenate([w_gu[:, 0, :], w_gu[:, 1, :], w_down.T], axis=1)
    tail = shifted(hidden_in[:, block - TAIL :, :], "ctx", 1)
    (w_one,) = gather_rows(first_pack, [inner + both + LANES])
    w_two, w_three = gather_rows(second_pack, [columns + inner, qwidth + inner])
    w_four, w_five = gather_rows(third_pack, [2 * units, units])

    tokens = place * block + jnp.arange(block, dtype=jnp.int32)
    begins = tokens[None, :] - positions
    all_begins = behind(begins)
    key_begins = jnp.concatenate(
        [jnp.where(place >= d, b, -1) for d, b in enumerate(all_begins)], axis=1
    )
    key_tokens = jnp.concatenate([tokens - d * block for d in range(count)])
    key_tokens = jnp.broadcast_to(key_tokens[None], key_begins.shape)
    mask = attention_mask(
        jnp.broadcast_to(tokens[None], begins.shape), begins, key_tokens, key_begins
    )
    frequency = jnp.power(
        jnp.float32(rope_base), -jnp.arange(0, HD, 2).astype(f32) / HD
    )
    spread = jnp.tile(frequency, (qwidth + HD) * 2 // HD)
    turned = positions.astype(f32).reshape(tokens_here, 1) * spread
    cosine, sine = jnp.cos(turned), jnp.sin(turned)
    turn = turn_matrix(qwidth + HD)

    x_own = hidden_in.reshape(tokens_here, features).astype(f32)
    x_ext = jnp.concatenate([x_own, tail.reshape(seqs * TAIL, features).astype(f32)], axis=0)
    gain_a = w_one[:, inner + both + heads].astype(f32)
    gain_f = w_one[:, inner + both + heads + 1].astype(f32)
    r_ext = lax.rsqrt(jnp.mean(x_ext * x_ext, axis=-1, keepdims=True) + 1e-05)
    h_ext = (x_ext * r_ext * gain_a).astype(bf16)
    h_own = h_ext[:tokens_here]
    r_one = r_ext[:tokens_here]

    proj = dot(h_ext, w_one)
    xr, xt = (
        proj[:tokens_here, :inner].reshape(seqs, block, inner),
        proj[tokens_here:, :inner].reshape(seqs, TAIL, inner),
    )
    bc, bt = (
        proj[:tokens_here, inner : inner + both].reshape(seqs, block, both),
        proj[tokens_here:, inner : inner + both].reshape(seqs, TAIL, both),
    )
    dtr = proj[:tokens_here, inner + both :].reshape(seqs, block, LANES)
    taps_x = conv_x.astype(f32)
    taps_bc = conv_bc.astype(f32)
    head_row = jnp.zeros((8, LANES), f32)
    head_row = head_row.at[0, :heads].set(a_log).at[1, :heads].set(dt_bias).at[2, :heads].set(d_skip)
    pos = positions[:, :, None]
    y_local, ends, c_vec, summed = mixer_local(
        xr, xt, bc, bt, dtr, taps_x, taps_bc, head_row, pos, heads
    )
    last = summed[:, block - 1, :]
    own_carry = jnp.exp(last[:, :heads]) * (last[:, LANES - 1 :] == 0.0).astype(f32)
    own_carry = jnp.repeat(own_carry, HD, axis=1)
    if count <= 4:
        pieces = jnp.stack([own_carry] + [swap(own_carry, "ctx", k) for k in range(1, count)])
        carry = jnp.stack([pick(pieces, place ^ j, 0) for j in range(count)])
    else:
        carry = lax.all_gather(own_carry, "ctx")
    state = chained(carry, ends, False)

    qz = dot(h_own, w_two)
    qkv = qz[:, :columns]
    gate = qz[:, columns:].reshape(seqs, block, inner)
    rotated_in = qkv[:, : qwidth + HD]
    w_turned = dot(w_two[:, : qwidth + HD], turn.astype(bf16)).astype(bf16)
    rotated = (rotated_in * cosine + dot(h_own, w_turned) * sine).astype(bf16)
    q_low = rotated[:, :qwidth].reshape(seqs, block, per_group, HD)
    kv_low = jnp.concatenate([rotated[:, qwidth:], qkv[:, qwidth + HD :].astype(bf16)], axis=1)
    keys_values = jnp.concatenate(behind(kv_low.reshape(seqs, block, 2 * HD)), axis=1)
    keys, values = keys_values[..., :HD], keys_values[..., HD:]
    attended, lse = over_seqs(attend_one, (q_low, keys, values, mask))

    read_weight = jnp.exp(jnp.repeat(summed[:, :, :heads], HD, axis=2)) * (
        summed[:, :, LANES - 1 :] == 0.0
    ).astype(f32)
    state_low = state.astype(bf16)
    y = y_local + read_weight * jnp.einsum(
        "stn,snw->stw", c_vec, state_low, preferred_element_type=f32
    )
    sig_gate = jax.nn.sigmoid(gate)
    silu_gate = gate * sig_gate
    gated = (y * silu_gate).astype(bf16)
    mixer_out = jnp.concatenate(
        [attended.reshape(tokens_here, qwidth).astype(bf16), gated.reshape(tokens_here, inner)],
        axis=1,
    )
    resid = x_own + pair_sum(dot_nt(mixer_out, w_three))

    r_two = lax.rsqrt(jnp.mean(resid * resid, axis=-1, keepdims=True) + 1e-05)
    h_two = (resid * r_two * gain_f).astype(bf16)
    gate_up = dot(h_two, w_four)
    gate_ff, up_ff = gate_up[:, :units], gate_up[:, units:]
    sig_ff = jax.nn.sigmoid(gate_ff)
    silu_ff = gate_ff * sig_ff
    hidden_state = (silu_ff * up_ff).astype(bf16)
    ffn = pair_sum(dot_nt(hidden_state, w_five))
    block_out = (resid + ffn).astype(bf16).reshape(seqs, block, features)

    e_low = output_cotangent.reshape(tokens_here, features)
    d_hidden_state = dot(e_low, w_five)
    d_gate_up = jnp.concatenate(
        [
            d_hidden_state * up_ff * (sig_ff * (1.0 + gate_ff * (1.0 - sig_ff))),
            d_hidden_state * silu_ff,
        ],
        axis=1,
    ).astype(bf16)

    def tn(a, b):
        return lax.dot_general(a, b, (((0,), (0,)), ((), ())), preferred_element_type=f32)

    d_h_two_part = dot_nt(d_gate_up, w_four).astype(bf16)
    d_h_two = pair_sum(d_h_two_part)
    ffn_grads = scatter_rows([tn(h_two, d_gate_up).astype(bf16), tn(e_low, hidden_state).astype(bf16)])
    grad_gain_f = jnp.sum(d_h_two_part.astype(f32) * resid * r_two, axis=0)
    scaled = d_h_two * gain_f
    d_resid = (
        e_low.astype(f32)
        + r_two * scaled
        - resid * (r_two * r_two * r_two) * jnp.mean(resid * scaled, axis=-1, keepdims=True)
    )
    d_mix = d_resid.astype(bf16)

    d_mixer_out = dot(d_mix, w_three)
    d_att = d_mixer_out[:, :qwidth].astype(bf16).reshape(seqs, block, per_group, HD)
    d_gated = d_mixer_out[:, qwidth:].reshape(seqs, block, inner)
    d_y = d_gated * silu_gate
    d_z = (d_gated * y * (sig_gate * (1.0 + gate * (1.0 - sig_gate)))).astype(bf16)
    state_grad = jnp.einsum(
        "stn,stw->snw", c_vec, (read_weight * d_y).astype(bf16), preferred_element_type=f32
    )
    later_grad = chained(carry, state_grad, True)

    row_dot = jnp.transpose(jnp.sum(d_att.astype(f32) * attended, axis=-1), (0, 2, 1))
    d_q, kept = over_seqs(
        attend_one_back, (q_low, keys, values, mask, d_att, lse, row_dot)
    )
    d_kv = return_to_owners(kept.reshape(seqs, count, block, 2 * HD)).reshape(tokens_here, 2 * HD)
    d_rot = jnp.concatenate([d_q.reshape(tokens_here, qwidth), d_kv[:, :HD]], axis=1)
    d_qk = d_rot * cosine + jnp.dot(d_rot * sine, turn.T, precision=lax.Precision.HIGH)
    d_two = jnp.concatenate(
        [d_qk.astype(bf16), d_kv[:, HD:].astype(bf16), d_z.reshape(tokens_here, inner)], axis=1
    )
    two_grads = scatter_rows([tn(h_own, d_two).astype(bf16), tn(d_mix, mixer_out).astype(bf16)])

    d_carry = jnp.sum((later_grad * state).reshape(seqs, states, heads, HD), axis=(1, 3))
    d_carry = d_carry * own_carry.reshape(seqs, heads, HD)[:, :, 0]
    d_carry = jnp.pad(d_carry, ((0, 0), (0, LANES - heads)))[:, None, :]
    d_x, d_bc, d_dtr, g_taps_x, g_taps_bc, g_heads = mixer_back(
        xr, xt, bc, bt, dtr, taps_x, taps_bc, head_row, pos,
        d_y, y, state_low, later_grad.astype(bf16), d_carry, heads,
    )
    d_one = jnp.concatenate([d_x, d_bc, d_dtr], axis=2).astype(bf16)
    d_one = jnp.concatenate(
        [
            d_one[:, TAIL:].reshape(tokens_here, -1),
            d_one[:, :TAIL].reshape(seqs * TAIL, -1),
        ],
        axis=0,
    )
    one_grads = scatter_rows([tn(h_ext, d_one).astype(bf16)])

    d_tail = dot_nt(d_one[tokens_here:], w_one)
    d_tail = shifted(pair_sum(d_tail).astype(bf16), "ctx", -1).astype(f32)
    d_h_part = (dot_nt(d_two, w_two) + dot_nt(d_one[:tokens_here], w_one)).astype(bf16)
    d_h = pair_sum(d_h_part).reshape(seqs, block, features)
    d_h = d_h.at[:, block - TAIL :, :].add(d_tail.reshape(seqs, TAIL, features))
    d_h = d_h.reshape(tokens_here, features)
    grad_gain_a = jnp.sum(d_h * x_own * r_one, axis=0)
    scaled = d_h * gain_a
    d_hidden = (
        d_resid
        + r_one * scaled
        - x_own * (r_one * r_one * r_one) * jnp.mean(x_own * scaled, axis=-1, keepdims=True)
    )
    d_hidden = d_hidden.astype(bf16).reshape(seqs, block, features)

    over_pair = jnp.concatenate([jnp.sum(g_taps_bc, axis=0).reshape(-1), grad_gain_f])
    over_pair = sum_all(over_pair, ("tp",))
    over_rest = jnp.concatenate(
        [
            jnp.sum(g_taps_x, axis=0).reshape(-1),
            jnp.sum(g_heads, axis=0)[:3, :heads].reshape(-1),
            grad_gain_a,
            over_pair,
        ]
    )
    total = sum_all(over_rest, ("dp", "ctx"))
    sizes = (KC * inner, heads, heads, heads, features, KC * both, features)
    small, first = [], 0
    for size in sizes:
        small.append(total[first : first + size])
        first += size
    g_tx, g_decay, g_bias, g_skip, g_gain_a, g_tb, g_gain_f = small
    shard = lax.axis_index("dp") * count + place

    def own_rows(vector):
        return lax.dynamic_slice_in_dim(vector, shard * rows, rows, 0)

    bc_grad = one_grads[:, inner : inner + both]
    bc_grad = sum_all(bc_grad, ("tp",))
    zx_grad = jnp.stack(
        [two_grads[:, columns : columns + inner], one_grads[:, :inner]], axis=1
    )
    return (
        block_out,
        d_hidden,
        own_rows(g_gain_a),
        two_grads[:, None, :columns],
        two_grads[:, columns + inner : columns + inner + qwidth].T,
        zx_grad,
        bc_grad,
        one_grads[:, inner + both : inner + both + heads],
        g_tx.reshape(KC, inner),
        g_tb.reshape(KC, both),
        g_decay,
        g_bias,
        g_skip,
        two_grads[:, columns + inner + qwidth :].T,
        own_rows(g_gain_f),
        jnp.stack([ffn_grads[:, :units], ffn_grads[:, units : 2 * units]], axis=1),
        ffn_grads[:, 2 * units :].T,
    )


def solution(mesh):
    in_specs = (
        P("dp", "ctx", None),
        P("dp", "ctx"),
        P(("dp", "ctx")),
        P(("dp", "ctx"), "tp", None),
        P("tp", ("dp", "ctx")),
        P(("dp", "ctx"), None, "tp"),
        P(("dp", "ctx"), None),
        P(("dp", "ctx"), "tp"),
        P(None, "tp"),
        P(),
        P("tp"),
        P("tp"),
        P("tp"),
        P("tp", ("dp", "ctx")),
        P(("dp", "ctx")),
        P(("dp", "ctx"), None, "tp"),
        P("tp", ("dp", "ctx")),
        P("dp", "ctx", None),
    )
    out_specs = (
        P("dp", "ctx", None),
        P("dp", "ctx", None),
        P(("dp", "ctx")),
        P(("dp", "ctx"), "tp", None),
        P("tp", ("dp", "ctx")),
        P(("dp", "ctx"), None, "tp"),
        P(("dp", "ctx"), None),
        P(("dp", "ctx"), "tp"),
        P(None, "tp"),
        P(),
        P("tp"),
        P("tp"),
        P("tp"),
        P("tp", ("dp", "ctx")),
        P(("dp", "ctx")),
        P(("dp", "ctx"), None, "tp"),
        P("tp", ("dp", "ctx")),
    )
    return jax.shard_map(
        per_device, mesh=mesh, in_specs=in_specs, out_specs=out_specs, check_vma=False
    )
```

time: 1690 us -> 571 us (0.34)
  waiting for transfers between devices: 1020 us -> 175 us
  blocking collectives: 344 us -> 0 us
  starting transfers between devices: 9.66 us -> 124 us
  matrix products: 145 us -> 69.9 us
  Pallas kernels: 0 us -> 45.1 us
  local copies, waits for them, and re-layouts: 53.7 us -> 75 us
    reduce_scatter x8 -> x0, waiting for transfers between devices: 757 us -> none  [the longest x1 182 us: per_device(): lax.psum_scatter(gate_up_gradient, ('dp', 'ctx'), scatter_dimension=0, ti...]
    all_gather x7 -> x0, blocking collectives: 222 us -> none  [the longest x1 54.8 us: per_device(): lax.all_gather(w_qkv, ('dp', 'ctx'), axis=0, tiled=True)]
    ppermute x4 -> x75, waiting for transfers between devices: 4.34 us -> 175 us  [the longest x58 159 us: swap(): return lax.ppermute(value, axis, [(i, i ^ bits) for i in range(count)])]
    all_gather x6 -> x0, waiting for transfers between devices: 162 us -> none  [the longest x1 79 us: per_device(): lax.all_gather(w_gu, ('dp', 'ctx'), axis=0, tiled=True)]
    unnamed x2 -> x0, blocking collectives: 120 us -> none
    ppermute x4 -> x75, starting transfers between devices: 8.09 us -> 124 us  [the longest x58 84.9 us: swap(): return lax.ppermute(value, axis, [(i, i ^ bits) for i in range(count)])]
    dot_general x43 -> x26, matrix products: 145 us -> 69.9 us  [the longest x6 16.8 us: dot(): return jnp.dot(a, b, preferred_element_type=f32)]
    unnamed x19 -> x0, waiting for transfers between devices: 68.5 us -> none
  transfers between devices with their start and end apart: 22 -> 75, of which waited for: 15 -> 24; matrix products, arithmetic and copies ran while one was open for 11% -> 34% of each run, Pallas kernels for 0% -> 8%
where the time goes in v1:
time: 571 us; the launch traced here: 561 us
  waiting for transfers between devices  175 us (31%)
  starting transfers between devices  124 us (22%)
  local copies, waits for them, and re-layouts  75 us (13%)
  matrix products  69.9 us (12%)
  other arithmetic  69.6 us (12%)
  Pallas kernels  45.1 us (8%)
    ppermute x58, waiting for transfers between devices, swap(): return lax.ppermute(value, axis, [(i, i ^ bits) for i in range(count)])  159 us
    ppermute x58, starting transfers between devices, swap(): return lax.ppermute(value, axis, [(i, i ^ bits) for i in range(count)])  84.9 us
    ppermute x17, starting transfers between devices, shifted(): return lax.ppermute(value, axis, route)  38.8 us
    pallas_call x6, Pallas kernels, assemble(): pl.pallas_call(kernel, out_shape=[jax.ShapeDtypeStruct(shape, pieces[0].d...  19.9 us
    pallas_call x1, Pallas kernels, mixer_back(): pl.pallas_call(functools.partial(mixer_back_kernel, heads), grid=(seqs,),...  17.6 us
    dot_general x6, matrix products, dot(): return jnp.dot(a, b, preferred_element_type=f32)  16.8 us
    unnamed x223, local copies, waits for them, and re-layouts  16.4 us
    ppermute x17, waiting for transfers between devices, shifted(): return lax.ppermute(value, axis, route)  15.8 us
  transfers between devices with their start and end apart: 75, of which 24 were waited for; matrix products, arithmetic and copies ran while one was open for 34% of the time, Pallas kernels for 8%

profile of v1, /device:TPU:0, one launch (start us, length us, event | category | flops | bytes accessed | tf_op | source)
XLA Modules:
  0.0 561.3 jit_solution(5292217229895484299)
XLA Ops:
  2.0 7.5 %collective-permute-start.21 = (s32[2,256]{1,0:T(2,128)S(1)}, s32[2,256]{1,0:T(2,128)}, u32[]{:S(2)}, u32[]{:S(2)}) collective-permute-start(s32[2,256]{1,0:T(2,128)S(1)} %get-tuple-element.161), channel_id=1, source_target_pairs={{0,6},{1,7},{8,14},{9,15},{16,22},{17,23},{24,30},{25,31}} | collective-permute-start | bytes 6152 | tf_op jit(solution)/shard_map/ppermute | solution.py:34
  44.0 12.2 %collective-permute-start.7 = (bf16[64,2176]{1,0:T(8,128)(2,1)}, bf16[64,2176]{1,0:T(8,128)(2,1)S(1)}, u32[]{:S(2)}, u32[]{:S(2)}) collective-permute-start(bf16[64,2176]{1,0:T(8,128)(2,1)} %pad_maximum_fusion.15.refs_0_), channel_id=1, source_target_pairs={{0,2},{2,0},{4,6},{6,4},{1,3},{3,1},{5,7},{7,5},{8,10},{10,8},{12,... | collective-permute-start | bytes 835592 | tf_op jit(solution)/shard_map/ppermute | solution.py:28
  62.6 10.3 %collective-permute-done.7.refs_1_ = bf16[64,2176]{1,0:T(8,128)(2,1)S(1)} collective-permute-done((bf16[64,2176]{1,0:T(8,128)(2,1)}, bf16[64,2176]{1,0:T(8,128)(2,1)S(1)}, u32[]{:S(2)}, u32[]{:S(2)}) %collective-permute-start.7) | collective-permute-done | bytes 278560 | tf_op jit(solution)/shard_map/ppermute | solution.py:28
  96.1 7.6 %mixer_local.1 = (f32[2,256,768]{2,1,0:T(8,128)}, f32[2,128,768]{2,1,0:T(8,128)}, bf16[2,256,128]{2,1,0:T(8,128)(2,1)}, f32[2,256,128]{2,1,0:T(8,128)}) custom-call(f32[2,256,768]{2,1,0:T(8,128)} %bitcast.346, f32[2,8,768]{2,1,0:T(8,128)} %slice_bitcast_fusion.17.xt_ref, f32[2,256,256]{2,1,0:T(8,128)} %bitcast.358, ...), custom_call_target="tpu_custom_call" | custom-call | tf_op jit(solution)/shard_map/mixer_local/pallas_call | solution.py:324
  124.0 8.7 %collective-permute-done.23 = f32[2,768]{1,0:T(2,128)} collective-permute-done((f32[2,768]{1,0:T(2,128)}, f32[2,768]{1,0:T(2,128)}, u32[]{:S(2)}, u32[]{:S(2)}) %collective-permute-start.23) | collective-permute-done | bytes 6176 | tf_op jit(solution)/shard_map/ppermute | solution.py:28
  145.8 7.4 %collective-permute-done.14.refs_6_ = bf16[256,1024]{1,0:T(8,128)(2,1)S(1)} collective-permute-done((bf16[256,1024]{1,0:T(8,128)(2,1)}, bf16[256,1024]{1,0:T(8,128)(2,1)S(1)}, u32[]{:S(2)}, u32[]{:S(2)}) %collective-permute-start.14) | collective-permute-done | bytes 524320 | tf_op jit(solution)/shard_map/ppermute | solution.py:28
  155.8 8.7 %collective-permute-done.15.refs_7_ = bf16[256,1024]{1,0:T(8,128)(2,1)S(1)} collective-permute-done((bf16[256,1024]{1,0:T(8,128)(2,1)}, bf16[256,1024]{1,0:T(8,128)(2,1)S(1)}, u32[]{:S(2)}, u32[]{:S(2)}) %collective-permute-start.15) | collective-permute-done | bytes 524320 | tf_op jit(solution)/shard_map/ppermute | solution.py:28
  179.0 6.3 %fusion.27 = bf16[512,320]{1,0:T(8,128)(2,1)} fusion(bf16[528,1024]{1,0:T(8,128)(2,1)} %copy-done.34, bf16[1024,1152]{1,0:T(8,128)(2,1)} %bitcast.441, f32[512,1152]{1,0:T(8,128)} %copy-done.31, f32[320]{0:T(512)} %mul.374, f32[512]{0:T(512)} %bitcast.431, s32[320]{0:T(512)} %get-tuple-element.224, s32[320]{0:T(512)} %get-tuple-element.225, ...), kind=kOutput, calls=%fused_computation.73 | convolution fusion | flops 547225600 | bytes 2958336 | tf_op jit(solution)/shard_map/dot_general | solution.py:215
  221.0 11.5 %collective-permute-done.36.refs_6_ = bf16[256,1024]{1,0:T(8,128)(2,1)S(1)} collective-permute-done((bf16[256,1024]{1,0:T(8,128)(2,1)}, bf16[256,1024]{1,0:T(8,128)(2,1)S(1)}, u32[]{:S(2)}, u32[]{:S(2)}) %collective-permute-start.36) | collective-permute-done | bytes 524320 | tf_op jit(solution)/shard_map/ppermute | solution.py:28
  232.5 11.0 %collective-permute-done.37.refs_7_ = bf16[256,1024]{1,0:T(8,128)(2,1)} collective-permute-done((bf16[256,1024]{1,0:T(8,128)(2,1)}, bf16[256,1024]{1,0:T(8,128)(2,1)}, u32[]{:S(2)}, u32[]{:S(2)}) %collective-permute-start.37) | collective-permute-done | bytes 524320 | tf_op jit(solution)/shard_map/ppermute | solution.py:28
  282.7 5.5 fusion.30
  328.1 7.2 %fusion.28 = bf16[512,320]{1,0:T(8,128)(2,1)} fusion(f32[512,64]{1,0:T(8,128)S(1)} %bitcast.398, f32[512,256]{1,0:T(8,128)S(1)} %reshape.614, f32[320]{0:T(512)S(1)} %copy-done.93, f32[512]{0:T(512)S(1)} %bitcast.432, s32[320]{0:T(512)S(1)} %copy-done.96, s32[320]{0:T(512)S(1)} %copy-done.97, pred[320]{0:T(512)(128)(4,1)S(1)} %copy-done.104, ...), kind=kOutput, calls=%fused_computation.74 | convolution fusion | flops 316600320 | bytes 989568 | tf_op jit(solution)/shard_map/dot_general | solution.py:746
  342.1 9.8 %collective-permute-done.44 = bf16[2,128,768]{2,1,0:T(8,128)(2,1)} collective-permute-done((bf16[2,128,768]{2,1,0:T(8,128)(2,1)S(1)}, bf16[2,128,768]{2,1,0:T(8,128)(2,1)}, u32[]{:S(2)}, u32[]{:S(2)}) %collective-permute-start.44) | collective-permute-done | bytes 393248 | tf_op jit(solution)/shard_map/ppermute | solution.py:34
  355.3 17.6 %mixer_back.1 = (f32[2,264,768]{2,1,0:T(8,128)}, f32[2,264,256]{2,1,0:T(8,128)}, f32[2,264,128]{2,1,0:T(8,128)}, f32[2,4,768]{2,1,0:T(4,128)}, f32[2,4,256]{2,1,0:T(4,128)}, /*index=5*/f32[2,8,128]{2,1,0:T(8,128)}) custom-call(f32[2,256,768]{2,1,0:T(8,128)} %bitcast.347, f32[2,8,768]{2,1,0:T(8,128)} %slice_bitcast_fusion.17.xt_ref, ...), custom_call_target="tpu_custom_call" | custom-call | tf_op jit(solution)/shard_map/mixer_back/pallas_call | solution.py:488
  396.4 7.4 %collective-permute-done.61 = bf16[256,1152]{1,0:T(8,128)(2,1)S(1)} collective-permute-done((bf16[256,1152]{1,0:T(8,128)(2,1)}, bf16[256,1152]{1,0:T(8,128)(2,1)S(1)}, u32[]{:S(2)}, u32[]{:S(2)}) %collective-permute-start.61) | collective-permute-done | bytes 589856 | tf_op jit(solution)/shard_map/ppermute | solution.py:28
  403.8 13.6 %collective-permute-done.63 = bf16[256,1152]{1,0:T(8,128)(2,1)S(1)} collective-permute-done((bf16[256,1152]{1,0:T(8,128)(2,1)}, bf16[256,1152]{1,0:T(8,128)(2,1)S(1)}, u32[]{:S(2)}, u32[]{:S(2)}) %collective-permute-start.63) | collective-permute-done | bytes 589856 | tf_op jit(solution)/shard_map/ppermute | solution.py:28
  418.7 9.0 %collective-permute-start.64 = (bf16[64,1152]{1,0:T(8,128)(2,1)S(1)}, bf16[64,1152]{1,0:T(8,128)(2,1)S(1)}, u32[]{:S(2)}, u32[]{:S(2)}) collective-permute-start(bf16[64,1152]{1,0:T(8,128)(2,1)S(1)} %get-tuple-element.187), channel_id=1, source_target_pairs={{0,2},{2,0},{4,6},{6,4},{1,3},{3,1},{5,7},{7,5},{8,10},{10,8},{12,... | collective-permute-start | bytes 442376 | tf_op jit(solution)/shard_map/ppermute | solution.py:28
  432.1 6.3 %collective-permute-done.56 = bf16[2,256,1024]{2,1,0:T(8,128)(2,1)S(1)} collective-permute-done((bf16[2,256,1024]{2,1,0:T(8,128)(2,1)}, bf16[2,256,1024]{2,1,0:T(8,128)(2,1)S(1)}, u32[]{:S(2)}, u32[]{:S(2)}) %collective-permute-start.56) | collective-permute-done | bytes 1048608 | tf_op jit(solution)/shard_map/ppermute | solution.py:28
  449.3 5.7 %collective-permute-done.48 = bf16[16,1024]{1,0:T(8,128)(2,1)} collective-permute-done((bf16[16,1024]{1,0:T(8,128)(2,1)}, bf16[16,1024]{1,0:T(8,128)(2,1)}, u32[]{:S(2)}, u32[]{:S(2)}) %collective-permute-start.48) | collective-permute-done | bytes 32800 | tf_op jit(solution)/shard_map/ppermute | solution.py:34
  459.6 9.5 %collective-permute-done.50 = f32[6180]{0:T(1024)S(1)} collective-permute-done((f32[6180]{0:T(1024)S(1)}, f32[6180]{0:T(1024)S(1)}, u32[]{:S(2)}, u32[]{:S(2)}) %collective-permute-start.50) | collective-permute-done | bytes 24752 | tf_op jit(solution)/shard_map/ppermute | solution.py:28
  477.9 8.9 %collective-permute-start.52 = (f32[6180]{0:T(1024)S(1)}, f32[6180]{0:T(1024)S(1)}, u32[]{:S(2)}, u32[]{:S(2)}) collective-permute-start(f32[6180]{0:T(1024)S(1)} %add.436), channel_id=1, source_target_pairs={{0,2},{2,0},{4,6},{6,4},{1,3},{3,1},{5,7},{7,5},{8,10},{10,8},{12,... | collective-permute-start | bytes 74168 | tf_op jit(solution)/shard_map/ppermute | solution.py:28
  509.5 7.0 %collective-permute-done.58 = bf16[64,2176]{1,0:T(8,128)(2,1)S(1)} collective-permute-done((bf16[64,2176]{1,0:T(8,128)(2,1)S(1)}, bf16[64,2176]{1,0:T(8,128)(2,1)S(1)}, u32[]{:S(2)}, u32[]{:S(2)}) %collective-permute-start.58) | collective-permute-done | bytes 278560 | tf_op jit(solution)/shard_map/ppermute | solution.py:28
  516.6 28.3 %collective-permute-done.59 = bf16[64,2176]{1,0:T(8,128)(2,1)S(1)} collective-permute-done((bf16[64,2176]{1,0:T(8,128)(2,1)S(1)}, bf16[64,2176]{1,0:T(8,128)(2,1)S(1)}, u32[]{:S(2)}, u32[]{:S(2)}) %collective-permute-start.59) | collective-permute-done | bytes 278560 | tf_op jit(solution)/shard_map/ppermute | solution.py:28
  548.1 10.5 %collective-permute-done.73 = bf16[64,3072]{1,0:T(8,128)(2,1)S(1)} collective-permute-done((bf16[64,3072]{1,0:T(8,128)(2,1)S(1)}, bf16[64,3072]{1,0:T(8,128)(2,1)S(1)}, u32[]{:S(2)}, u32[]{:S(2)}) %collective-permute-start.73) | collective-permute-done | bytes 393248 | tf_op jit(solution)/shard_map/ppermute | solution.py:28
  (551 shorter events, 320.7 us)
Async XLA Ops:
  39.7 37.1 %collective-permute-start.6 = (bf16[256,1152]{1,0:T(8,128)(2,1)}, bf16[256,1152]{1,0:T(8,128)(2,1)S(1)}, u32[]{:S(2)}, u32[]{:S(2)}) collective-permute-start(bf16[256,1152]{1,0:T(8,128)(2,1)} %bitcast.366), channel_id=1, source_target_pairs={{0,24},{8,16},{16,8},{24,0},{1,25},{9,17},{17,9},{25,1},{2,26},{10... | collective-permute-start | bytes 1769480 | tf_op jit(solution)/shard_map/ppermute | solution.py:28
  42.2 37.1 %collective-permute-start.5 = (bf16[256,1152]{1,0:T(8,128)(2,1)}, bf16[256,1152]{1,0:T(8,128)(2,1)S(1)}, u32[]{:S(2)}, u32[]{:S(2)}) collective-permute-start(bf16[256,1152]{1,0:T(8,128)(2,1)} %bitcast.367), channel_id=1, source_target_pairs={{0,16},{8,24},{16,0},{24,8},{1,17},{9,25},{17,1},{25,9},{2,18},{10... | collective-permute-start | bytes 1769480 | tf_op jit(solution)/shard_map/ppermute | solution.py:28
  42.7 38.1 %collective-permute-start.4 = (bf16[256,1152]{1,0:T(8,128)(2,1)}, bf16[256,1152]{1,0:T(8,128)(2,1)S(1)}, u32[]{:S(2)}, u32[]{:S(2)}) collective-permute-start(bf16[256,1152]{1,0:T(8,128)(2,1)} %bitcast.368), channel_id=1, source_target_pairs={{0,8},{8,0},{16,24},{24,16},{1,9},{9,1},{17,25},{25,17},{2,10},{10... | collective-permute-start | bytes 1769480 | tf_op jit(solution)/shard_map/ppermute | solution.py:28
  59.7 46.8 %collective-permute-start.31 = (bf16[64,3072]{1,0:T(8,128)(2,1)S(1)}, bf16[64,3072]{1,0:T(8,128)(2,1)}, u32[]{:S(2)}, u32[]{:S(2)}) collective-permute-start(bf16[64,3072]{1,0:T(8,128)(2,1)S(1)} %pad_maximum_fusion.13.refs_0_), channel_id=1, source_target_pairs={{0,6},{2,4},{4,2},{6,0},{1,7},{3,5},{5,3},{7,1},{8,14},{10,12},{12... | collective-permute-start | bytes 1179656 | tf_op jit(solution)/shard_map/ppermute | solution.py:28
  72.9 35.4 %collective-permute-start.30 = (bf16[64,3072]{1,0:T(8,128)(2,1)S(1)}, bf16[64,3072]{1,0:T(8,128)(2,1)}, u32[]{:S(2)}, u32[]{:S(2)}) collective-permute-start(bf16[64,3072]{1,0:T(8,128)(2,1)S(1)} %pad_maximum_fusion.13.refs_0_), channel_id=1, source_target_pairs={{0,4},{2,6},{4,0},{6,2},{1,5},{3,7},{5,1},{7,3},{8,12},{10,14},{12... | collective-permute-start | bytes 1179656 | tf_op jit(solution)/shard_map/ppermute | solution.py:28
  76.8 31.4 %collective-permute-start.29 = (bf16[64,3072]{1,0:T(8,128)(2,1)S(1)}, bf16[64,3072]{1,0:T(8,128)(2,1)}, u32[]{:S(2)}, u32[]{:S(2)}) collective-permute-start(bf16[64,3072]{1,0:T(8,128)(2,1)S(1)} %pad_maximum_fusion.13.refs_0_), channel_id=1, source_target_pairs={{0,2},{2,0},{4,6},{6,4},{1,3},{3,1},{5,7},{7,5},{8,10},{10,8},{12,... | collective-permute-start | bytes 1179656 | tf_op jit(solution)/shard_map/ppermute | solution.py:28
  79.3 58.9 %collective-permute-start.13 = (bf16[256,1024]{1,0:T(8,128)(2,1)}, bf16[256,1024]{1,0:T(8,128)(2,1)}, u32[]{:S(2)}, u32[]{:S(2)}) collective-permute-start(bf16[256,1024]{1,0:T(8,128)(2,1)} %bitcast.399), channel_id=1, source_target_pairs={{0,16},{8,24},{16,0},{24,8},{1,17},{9,25},{17,1},{25,9},{2,18},{10... | collective-permute-start | bytes 1572872 | tf_op jit(solution)/shard_map/ppermute | solution.py:28
  80.8 58.5 %collective-permute-start.10 = (bf16[256,1152]{1,0:T(8,128)(2,1)}, bf16[256,1152]{1,0:T(8,128)(2,1)}, u32[]{:S(2)}, u32[]{:S(2)}) collective-permute-start(bf16[256,1152]{1,0:T(8,128)(2,1)} %bitcast.394), channel_id=1, source_target_pairs={{0,8},{8,0},{16,24},{24,16},{1,9},{9,1},{17,25},{25,17},{2,10},{10... | collective-permute-start | bytes 1769480 | tf_op jit(solution)/shard_map/ppermute | solution.py:28
  143.1 89.4 %collective-permute-start.33 = (bf16[256,2048]{1,0:T(8,128)(2,1)}, bf16[256,2048]{1,0:T(8,128)(2,1)}, u32[]{:S(2)}, u32[]{:S(2)}) collective-permute-start(bf16[256,2048]{1,0:T(8,128)(2,1)} %bitcast.390), channel_id=1, source_target_pairs={{0,16},{8,24},{16,0},{24,8},{1,17},{9,25},{17,1},{25,9},{2,18},{10... | collective-permute-start | bytes 3145736 | tf_op jit(solution)/shard_map/ppermute | solution.py:28
  153.3 46.7 %collective-permute-start.32 = (bf16[256,2048]{1,0:T(8,128)(2,1)}, bf16[256,2048]{1,0:T(8,128)(2,1)}, u32[]{:S(2)}, u32[]{:S(2)}) collective-permute-start(bf16[256,2048]{1,0:T(8,128)(2,1)} %bitcast.391), channel_id=1, source_target_pairs={{0,8},{8,0},{16,24},{24,16},{1,9},{9,1},{17,25},{25,17},{2,10},{10... | collective-permute-start | bytes 3145736 | tf_op jit(solution)/shard_map/ppermute | solution.py:28
  200.5 42.9 %collective-permute-start.34 = (bf16[256,2048]{1,0:T(8,128)(2,1)}, bf16[256,2048]{1,0:T(8,128)(2,1)S(1)}, u32[]{:S(2)}, u32[]{:S(2)}) collective-permute-start(bf16[256,2048]{1,0:T(8,128)(2,1)} %collective-permute-done.32.refs_1_), channel_id=1, source_target_pairs={{0,16},{8,24},{16,0},{24,8},{1,17},{9,25},{17,1},{25,9},{2,18},{10... | collective-permute-start | bytes 3145736 | tf_op jit(solution)/shard_map/ppermute | solution.py:28
  217.6 32.4 %collective-permute-start.28 = (bf16[512,1024]{1,0:T(8,128)(2,1)}, bf16[512,1024]{1,0:T(8,128)(2,1)}, u32[]{:S(2)}, u32[]{:S(2)}) collective-permute-start(bf16[512,1024]{1,0:T(8,128)(2,1)} %convolution_convert_fusion.6), channel_id=1, source_target_pairs={{0,1},{1,0},{2,3},{3,2},{4,5},{5,4},{6,7},{7,6},{8,9},{9,8},{10,11... | collective-permute-start | bytes 3145736 | tf_op jit(solution)/shard_map/ppermute | solution.py:28
  268.1 50.9 %collective-permute-start.70 = (bf16[2,256,1024]{2,1,0:T(8,128)(2,1)}, bf16[2,256,1024]{2,1,0:T(8,128)(2,1)}, u32[]{:S(2)}, u32[]{:S(2)}) collective-permute-start(bf16[2,256,1024]{2,1,0:T(8,128)(2,1)} %dynamic-slice_bitcast_fusion.2), channel_id=1, source_target_pairs={{0,8},{8,0},{16,24},{24,16},{1,9},{9,1},{17,25},{25,17},{2,10},{10... | collective-permute-start | bytes 3145736 | tf_op jit(solution)/shard_map/ppermute | solution.py:28
  270.7 157.2 %collective-permute-start.68 = (bf16[2,256,2048]{2,1,0:T(8,128)(2,1)}, bf16[2,256,2048]{2,1,0:T(8,128)(2,1)}, u32[]{:S(2)}, u32[]{:S(2)}) collective-permute-start(bf16[2,256,2048]{2,1,0:T(8,128)(2,1)} %dynamic-slice_bitcast_fusion), channel_id=1, source_target_pairs={{0,16},{8,24},{16,0},{24,8},{1,17},{9,25},{17,1},{25,9},{2,18},{10... | collective-permute-start | bytes 6291464 | tf_op jit(solution)/shard_map/ppermute | solution.py:28
  325.1 67.8 %collective-permute-start.71 = (bf16[256,1024]{1,0:T(8,128)(2,1)}, bf16[256,1024]{1,0:T(8,128)(2,1)}, u32[]{:S(2)}, u32[]{:S(2)}) collective-permute-start(bf16[256,1024]{1,0:T(8,128)(2,1)} %fusion.47), channel_id=1, source_target_pairs={{0,16},{8,24},{16,0},{24,8},{1,17},{9,25},{17,1},{25,9},{2,18},{10... | collective-permute-start | bytes 1572872 | tf_op jit(solution)/shard_map/ppermute | solution.py:28
  392.9 45.5 %collective-permute-start.56 = (bf16[2,256,1024]{2,1,0:T(8,128)(2,1)}, bf16[2,256,1024]{2,1,0:T(8,128)(2,1)S(1)}, u32[]{:S(2)}, u32[]{:S(2)}) collective-permute-start(bf16[2,256,1024]{2,1,0:T(8,128)(2,1)} %dynamic-slice_bitcast_fusion.3), channel_id=1, source_target_pairs={{0,8},{8,0},{16,24},{24,16},{1,9},{9,1},{17,25},{25,17},{2,10},{10... | collective-permute-start | bytes 3145736 | tf_op jit(solution)/shard_map/ppermute | solution.py:28
  403.8 43.5 %collective-permute-start.46 = (bf16[512,1024]{1,0:T(8,128)(2,1)}, bf16[512,1024]{1,0:T(8,128)(2,1)}, u32[]{:S(2)}, u32[]{:S(2)}) collective-permute-start(bf16[512,1024]{1,0:T(8,128)(2,1)} %add_convert_fusion), channel_id=1, source_target_pairs={{0,1},{1,0},{2,3},{3,2},{4,5},{5,4},{6,7},{7,6},{8,9},{9,8},{10,11... | collective-permute-start | bytes 3145736 | tf_op jit(solution)/shard_map/ppermute | solution.py:28
  438.4 32.2 %collective-permute-start.54 = (bf16[2,256,1152]{2,1,0:T(8,128)(2,1)}, bf16[2,256,1152]{2,1,0:T(8,128)(2,1)}, u32[]{:S(2)}, u32[]{:S(2)}) collective-permute-start(bf16[2,256,1152]{2,1,0:T(8,128)(2,1)} %dynamic-slice_bitcast_fusion.1), channel_id=1, source_target_pairs={{0,16},{8,24},{16,0},{24,8},{1,17},{9,25},{17,1},{25,9},{2,18},{10... | collective-permute-start | bytes 3538952 | tf_op jit(solution)/shard_map/ppermute | solution.py:28
  443.6 52.9 %collective-permute-start.57 = (bf16[256,1024]{1,0:T(8,128)(2,1)}, bf16[256,1024]{1,0:T(8,128)(2,1)}, u32[]{:S(2)}, u32[]{:S(2)}) collective-permute-start(bf16[256,1024]{1,0:T(8,128)(2,1)} %fusion.50), channel_id=1, source_target_pairs={{0,16},{8,24},{16,0},{24,8},{1,17},{9,25},{17,1},{25,9},{2,18},{10... | collective-permute-start | bytes 1572872 | tf_op jit(solution)/shard_map/ppermute | solution.py:28
  444.1 59.4 %collective-permute-start.69 = (bf16[256,2048]{1,0:T(8,128)(2,1)}, bf16[256,2048]{1,0:T(8,128)(2,1)}, u32[]{:S(2)}, u32[]{:S(2)}) collective-permute-start(bf16[256,2048]{1,0:T(8,128)(2,1)} %fusion.14), channel_id=1, source_target_pairs={{0,8},{8,0},{16,24},{24,16},{1,9},{9,1},{17,25},{25,17},{2,10},{10... | collective-permute-start | bytes 3145736 | tf_op jit(solution)/shard_map/ppermute | solution.py:28
  502.4 42.5 %collective-permute-start.59 = (bf16[64,2176]{1,0:T(8,128)(2,1)S(1)}, bf16[64,2176]{1,0:T(8,128)(2,1)S(1)}, u32[]{:S(2)}, u32[]{:S(2)}) collective-permute-start(bf16[64,2176]{1,0:T(8,128)(2,1)S(1)} %get-tuple-element.183), channel_id=1, source_target_pairs={{0,4},{2,6},{4,0},{6,2},{1,5},{3,7},{5,1},{7,3},{8,12},{10,14},{12... | collective-permute-start | bytes 835592 | tf_op jit(solution)/shard_map/ppermute | solution.py:28
  506.3 41.9 %collective-permute-start.72 = (bf16[64,3072]{1,0:T(8,128)(2,1)S(1)}, bf16[64,3072]{1,0:T(8,128)(2,1)S(1)}, u32[]{:S(2)}, u32[]{:S(2)}) collective-permute-start(bf16[64,3072]{1,0:T(8,128)(2,1)S(1)} %get-tuple-element.176), channel_id=1, source_target_pairs={{0,2},{2,0},{4,6},{6,4},{1,3},{3,1},{5,7},{7,5},{8,10},{10,8},{12,... | collective-permute-start | bytes 1179656 | tf_op jit(solution)/shard_map/ppermute | solution.py:28
  509.2 39.0 %collective-permute-start.74 = (bf16[64,3072]{1,0:T(8,128)(2,1)S(1)}, bf16[64,3072]{1,0:T(8,128)(2,1)S(1)}, u32[]{:S(2)}, u32[]{:S(2)}) collective-permute-start(bf16[64,3072]{1,0:T(8,128)(2,1)S(1)} %get-tuple-element.177), channel_id=1, source_target_pairs={{0,6},{2,4},{4,2},{6,0},{1,7},{3,5},{5,3},{7,1},{8,14},{10,12},{12... | collective-permute-start | bytes 1179656 | tf_op jit(solution)/shard_map/ppermute | solution.py:28
  516.5 42.0 %collective-permute-start.73 = (bf16[64,3072]{1,0:T(8,128)(2,1)S(1)}, bf16[64,3072]{1,0:T(8,128)(2,1)S(1)}, u32[]{:S(2)}, u32[]{:S(2)}) collective-permute-start(bf16[64,3072]{1,0:T(8,128)(2,1)S(1)} %get-tuple-element.178), channel_id=1, source_target_pairs={{0,4},{2,6},{4,0},{6,2},{1,5},{3,7},{5,1},{7,3},{8,12},{10,14},{12... | collective-permute-start | bytes 1179656 | tf_op jit(solution)/shard_map/ppermute | solution.py:28
  (157 other events, 2139.2 us)

commit v2 on v1

v2 whole, which is shorter than its diff:
```python
import functools

import jax
import jax.numpy as jnp
from jax import lax
from jax.experimental import pallas as pl
from jax.experimental.pallas import tpu as pltpu
from jax.sharding import PartitionSpec as P

HD = 64
KC = 4
TAIL = 16
LANES = 128
VMEM_LIMIT = 56 * 1024 * 1024

f32 = jnp.float32
bf16 = jnp.bfloat16
highest = lax.Precision.HIGHEST
rope_base = 100000000000.0


def small_mesh():
    return lax.axis_size("dp") == 4 and lax.axis_size("ctx") == 4


def swap(value, axis, bits):
    count = lax.axis_size(axis)
    return lax.ppermute(value, axis, [(i, i ^ bits) for i in range(count)])


def shifted(value, axis, distance):
    count = lax.axis_size(axis)
    route = [(i - distance, i) for i in range(count) if 0 <= i - distance < count]
    return lax.ppermute(value, axis, route)


def place_blocks(pieces, outs, copies):
    count = len(pieces)
    total = len(outs)
    where = jnp.stack([lax.axis_index("dp"), lax.axis_index("ctx")]).astype(jnp.int32)

    def kernel(where_ref, *refs):
        ins = refs[:count]
        outputs = refs[count : count + total]
        sems = refs[count + total]
        running = []
        for number, (piece, first, width, out, axis, bits, to) in enumerate(copies):
            target = outputs[out]
            if axis is None:
                target = target.at[:, pl.ds(to, width)]
            else:
                target = target.at[jnp.bitwise_xor(where_ref[axis], bits), :, pl.ds(to, width)]
            copy = pltpu.make_async_copy(
                ins[piece].at[:, pl.ds(first, width)], target, sems.at[number]
            )
            copy.start()
            running.append(copy)
        for copy in running:
            copy.wait()

    return pl.pallas_call(
        kernel,
        out_shape=[jax.ShapeDtypeStruct(shape, pieces[0].dtype) for shape in outs],
        in_specs=[pl.BlockSpec(memory_space=pltpu.SMEM)]
        + [pl.BlockSpec(memory_space=pl.ANY)] * count,
        out_specs=[pl.BlockSpec(memory_space=pltpu.VMEM)] * total,
        scratch_shapes=[pltpu.SemaphoreType.DMA((len(copies),))],
        compiler_params=pltpu.CompilerParams(vmem_limit_bytes=VMEM_LIMIT),
        name="place_blocks",
    )(where, *pieces)


class Placing:
    def __init__(self):
        self.pieces, self.outs, self.copies = [], [], []

    def out(self, *shape):
        self.outs.append(shape)
        return len(self.outs) - 1

    def add(self, piece, out, axis=None, bits=0, to=0, first=0, width=None):
        for number, known in enumerate(self.pieces):
            if known is piece:
                break
        else:
            number = len(self.pieces)
            self.pieces.append(piece)
        width = piece.shape[1] if width is None else width
        self.copies.append((number, first, width, out, axis, bits, to))

    def after(self, *arrays):
        self.pieces.extend(arrays)

    def run(self):
        return place_blocks(self.pieces, self.outs, self.copies)


def along_ctx(packed):
    return [packed] + [swap(packed, "ctx", k) for k in (1, 2, 3)]


def along_dp(held, one, two):
    near = swap(held, "dp", one)
    return [(0, held), (one, near), (two, swap(held, "dp", two)), (3, swap(near, "dp", two))]


def gather_all(first, second, third, with_first):
    rows = first.shape[0]
    if not small_mesh():
        def whole(piece):
            return lax.all_gather(piece, ("dp", "ctx"), axis=0, tiled=True)

        w_two, w_three = [whole(jnp.concatenate(p, axis=1)) for p in second]
        w_four, w_five = [
            whole(
                jnp.concatenate(
                    [p for p, out, _ in sorted(third[0] + third[1], key=lambda t: t[2]) if out == o],
                    axis=1,
                )
            )
            for o in (0, 1)
        ]
        return with_first(whole(first)), w_two, w_three, w_four, w_five, []

    def flat(held):
        return held.reshape(held.shape[0] * held.shape[1], held.shape[2])

    wide_one = first.shape[1]
    wide_two = [sum(p.shape[1] for p in part) for part in second]
    wide_half = [sum(p.shape[1] for p, _, _ in half) for half in third]
    work = Placing()
    held_out = work.out(4, rows, wide_one)
    pack_out = work.out(rows, sum(wide_two))
    for k, piece in enumerate(along_ctx(first)):
        work.add(piece, held_out, 1, k)
    to = 0
    for piece in second[0] + second[1]:
        work.add(piece, pack_out, to=to)
        to += piece.shape[1]
    held_one, packed_two = work.run()
    held_one = flat(held_one)
    work = Placing()
    full = work.out(4, 4 * rows, wide_one)
    held_out = [work.out(4, rows, w) for w in wide_two]
    pack_out = work.out(rows, sum(wide_half))
    for k in range(4):
        work.add(held_one if k == 0 else swap(held_one, "dp", k), full, 0, k)
    for k, piece in enumerate(along_ctx(packed_two)):
        work.add(piece, held_out[0], 1, k, width=wide_two[0])
        work.add(piece, held_out[1], 1, k, first=wide_two[0], width=wide_two[1])
    to = 0
    for piece, _, _ in third[0] + third[1]:
        work.add(piece, pack_out, to=to)
        to += piece.shape[1]
    w_one, held_a, held_b, packed_three = work.run()
    made = with_first(flat(w_one))
    work = Placing()
    fulls = [work.out(4, 4 * rows, w) for w in wide_two]
    held_out = [work.out(4, rows, w) for w in wide_half]
    for bits, piece in along_dp(flat(held_a), 1, 2):
        work.add(piece, fulls[0], 0, bits)
    for bits, piece in along_dp(flat(held_b), 2, 1):
        work.add(piece, fulls[1], 0, bits)
    for k, piece in enumerate(along_ctx(packed_three)):
        work.add(piece, held_out[0], 1, k, width=wide_half[0])
        work.add(piece, held_out[1], 1, k, first=wide_half[0], width=wide_half[1])
    work.after(made[-1])
    w_two, w_three, held_a, held_b = work.run()
    work = Placing()
    ends = [0, 0]
    for part in third[0] + third[1]:
        ends[part[1]] += part[0].shape[1]
    fulls = [work.out(4, 4 * rows, w) for w in ends]
    nears = []
    for half, held, order in ((third[0], held_a, (1, 2)), (third[1], held_b, (2, 1))):
        blocks = along_dp(flat(held), *order)
        nears += [blocks[1][1], blocks[2][1]]
        for bits, piece in blocks:
            column = 0
            for part, out, to in half:
                work.add(piece, fulls[out], 0, bits, to=to, first=column, width=part.shape[1])
                column += part.shape[1]
    w_four, w_five = work.run()
    return made, flat(w_two), flat(w_three), flat(w_four), flat(w_five), nears


def pick(value, index, axis):
    return lax.dynamic_index_in_dim(value, index, axis, keepdims=False)


class Scatter:
    def __init__(self, grads):
        self.grads = grads
        self.staged = small_mesh()
        self.got, self.near, self.along = [], [], []
        if not self.staged:
            return
        self.dp, self.ctx = lax.axis_index("dp"), lax.axis_index("ctx")
        self.y, self.x = self.dp // 2, self.dp % 2
        rows = grads[0][0].shape[0]
        if len(grads) == 1:
            self.blocks = grads[0][0].reshape(4, rows // 4, -1)
            self.got = [swap(pick(self.blocks, self.dp ^ k, 0), "dp", k) for k in (1, 2, 3)]
            return
        self.kept = []
        for number, group in enumerate(grads):
            one, axis, at = (2, 0, self.y) if number == 0 else (1, 1, self.x)

            def part(index):
                return jnp.concatenate(
                    [pick(g.reshape(2, 2, rows // 4, -1), index, axis) for g in group], axis=2
                )

            self.got.append(swap(part(1 - at), "dp", one))
            self.kept.append(part(at))

    def second(self):
        if not self.staged or len(self.grads) == 1:
            return
        for number in range(2):
            then, two = (self.x, 1) if number == 0 else (self.y, 2)
            kept, got = self.kept[number], self.got[number]
            send = (
                pick(kept, 1 - then, 0).astype(f32) + pick(got, 1 - then, 0).astype(f32)
            ).astype(bf16)
            self.near.append(swap(send, "dp", two))

    def third(self):
        if not self.staged:
            return
        if len(self.grads) == 1:
            total = pick(self.blocks, self.dp, 0).astype(f32)
            for piece in self.got:
                total = total + piece.astype(f32)
            held = total.astype(bf16)
        else:
            parts = []
            for number in range(2):
                then = self.x if number == 0 else self.y
                parts.append(
                    (
                        pick(self.kept[number], then, 0).astype(f32)
                        + pick(self.got[number], then, 0).astype(f32)
                        + self.near[number].astype(f32)
                    ).astype(bf16)
                )
            held = jnp.concatenate(parts, axis=1)
        self.held = held.reshape(4, held.shape[0] // 4, -1)
        self.along = [swap(pick(self.held, self.ctx ^ k, 0), "ctx", k) for k in (1, 2, 3)]

    def result(self):
        if not self.staged:
            parts = [g for group in self.grads for g in group]
            joined = jnp.concatenate(parts, axis=1) if len(parts) > 1 else parts[0]
            return lax.psum_scatter(
                joined, ("dp", "ctx"), scatter_dimension=0, tiled=True
            ).astype(f32)
        total = pick(self.held, self.ctx, 0).astype(f32)
        for piece in self.along:
            total = total + piece.astype(f32)
        return total


def sum_all(value, axes):
    for axis in axes:
        count = lax.axis_size(axis)
        if count & (count - 1):
            value = lax.psum(value, axis)
            continue
        bits = 1
        while bits < count:
            value = value + swap(value, axis, bits)
            bits *= 2
    return value


def pair_sum(value):
    if lax.axis_size("tp") != 2:
        return lax.psum(value.astype(bf16), "tp").astype(f32)
    low = value.astype(bf16)
    return low.astype(f32) + swap(low, "tp", 1).astype(f32)


def chain_pieces(pack, reverse):
    count, me = lax.axis_size("ctx"), lax.axis_index("ctx")
    if count <= 4:
        sign = -1 if reverse else 1
        return [shifted(pack, "ctx", sign * d) for d in range(1, count)]
    everything = lax.all_gather(pack, "ctx")
    states = pack.shape[1] - TAIL

    def hop(k, before):
        at = count - 1 - k if reverse else k
        reached = at > me if reverse else at < me
        there = pick(everything, at, 0).astype(f32)
        new = there[:, states : states + 1] * before + there[:, :states]
        return jnp.where(reached, new, before)

    start = jnp.zeros((pack.shape[0], states, pack.shape[2]), f32)
    total = lax.fori_loop(0, count, hop, start).astype(bf16)
    return [jnp.pad(total, ((0, 0), (0, TAIL), (0, 0)))]


def dot(a, b):
    return jnp.dot(a, b, preferred_element_type=f32)


def dot_nt(a, b):
    return lax.dot_general(a, b, (((1,), (1,)), ((), ())), preferred_element_type=f32)


def sig(v):
    return 1.0 / (1.0 + jnp.exp(-v))


def conv_pre(joined, span, taps, pos, count):
    total = None
    for k in range(KC):
        piece = joined[TAIL - k : TAIL - k + count, span]
        term = taps[k : k + 1, :] * piece
        if k:
            term = term * (pos >= k).astype(f32)
        total = term if total is None else total + term
    return total


def lane_ids(shape):
    return lax.broadcasted_iota(jnp.int32, shape, 1)


def decay_parts(dtr, head_row, pos, heads):
    count = dtr.shape[0]
    lane = lane_ids(dtr.shape)
    pre = dtr + head_row[1:2, :]
    dt = jnp.where(lane < heads, jnp.maximum(pre, 0.0) + jnp.log(1.0 + jnp.exp(-jnp.abs(pre))), 0.0)
    la = -jnp.exp(head_row[0:1, :]) * dt
    marked = jnp.where(lane == LANES - 1, (pos == 0).astype(f32), la)
    row = lax.broadcasted_iota(jnp.int32, (count, count), 0)
    col = lax.broadcasted_iota(jnp.int32, (count, count), 1)
    lower = (row >= col).astype(f32)
    summed = jnp.dot(lower, marked, precision=highest, preferred_element_type=f32)
    return pre, dt, la, summed


def wide(value, lane):
    return jnp.broadcast_to(value[:, lane : lane + 1], (value.shape[0], LANES))


def pair(value, j, low_half):
    return jnp.where(low_half, wide(value, 2 * j), wide(value, 2 * j + 1))


def spec_whole(a):
    return pl.BlockSpec(a.shape, lambda s: (0,) * a.ndim)


def spec_rows(a, rows, base=0):
    return pl.BlockSpec((rows, a.shape[1]), lambda s: (base + s, 0))


def spec_seq(a):
    return pl.BlockSpec((1,) + a.shape[1:], lambda s: (s,) + (0,) * (a.ndim - 1))


def spec_any():
    return pl.BlockSpec(memory_space=pl.ANY)


def params():
    return pltpu.CompilerParams(vmem_limit_bytes=VMEM_LIMIT)


def cost(microseconds):
    return pl.CostEstimate(
        flops=int(microseconds * 1e8), bytes_accessed=int(microseconds * 3e5), transcendentals=0
    )


def chained_state(pieces, span, states):
    total, factor = None, None
    for piece in pieces:
        there = piece[0, :states, span].astype(f32)
        decay = piece[0, states : states + 1, span].astype(f32)
        if total is None:
            total, factor = there, decay
        else:
            total = total + factor * there
            factor = factor * decay
    return total


def mixer_local_kernel(
    heads, inner, both, proj_ref, tail_ref, tx_ref, tb_ref, hr_ref, pos_ref,
    y_ref, pack_ref, c_ref, l_ref, jx, jb,
):
    count = proj_ref.shape[0]
    states = both // 2
    pos = pos_ref[...]
    head_row = hr_ref[...]
    jx[0:TAIL, :] = tail_ref[:, :inner]
    jx[TAIL : TAIL + count, :] = proj_ref[:, :inner]
    jb[0:TAIL, :] = tail_ref[:, inner : inner + both]
    jb[TAIL : TAIL + count, :] = proj_ref[:, inner : inner + both]
    pre_b = conv_pre(jb, slice(0, both), tb_ref[...], pos, count)
    bc = pre_b * sig(pre_b)
    b_low = bc[:, :states].astype(bf16)
    c_low = bc[:, states:].astype(bf16)
    c_ref[...] = c_low
    bt_low = jnp.transpose(bc[:, :states]).astype(bf16)
    _, dt, _, summed = decay_parts(proj_ref[:, inner + both :], head_row, pos, heads)
    l_ref[...] = summed
    rows = jnp.transpose(summed)
    row = lax.broadcasted_iota(jnp.int32, (count, count), 0)
    col = lax.broadcasted_iota(jnp.int32, (count, count), 1)
    marks = summed[:, LANES - 1 : LANES]
    valid = (row >= col) & (marks == rows[LANES - 1 : LANES, :])
    scores = dot_nt(c_low, b_low)
    last = summed[count - 1 : count, :]
    same = (marks == last[:, LANES - 1 : LANES]).astype(f32)
    carry = jnp.exp(last) * (last[:, LANES - 1 : LANES] == 0.0).astype(f32)
    low_half = lane_ids((count, LANES)) < HD
    low_row = low_half[0:1, :]
    for j in range(heads // 2):
        span = slice(j * LANES, (j + 1) * LANES)
        pre = conv_pre(jx, span, tx_ref[:, span], pos, count)
        xc = pre * sig(pre)
        u = xc * pair(dt, j, low_half)
        u_low = u.astype(bf16)
        results = []
        for h in (2 * j, 2 * j + 1):
            differ = summed[:, h : h + 1] - rows[h : h + 1, :]
            mixing = jnp.exp(jnp.where(valid, differ, -1e30)) * scores
            results.append(dot(mixing.astype(bf16), u_low))
        skip = pair(head_row[2:3, :], j, low_row)
        y_ref[:, span] = jnp.where(low_half, results[0], results[1]) + skip * xc
        left = jnp.exp(pair(last, j, low_row) - pair(summed, j, low_half)) * same
        pack_ref[0, :states, span] = dot(bt_low, (left * u).astype(bf16)).astype(bf16)
        pack_ref[0, states:, span] = jnp.broadcast_to(pair(carry, j, low_row), (TAIL, LANES)).astype(bf16)


def mixer_local(proj, taps_x, taps_bc, head_row, pos, heads, seqs, count):
    inner, both = taps_x.shape[1], taps_bc.shape[1]
    states = both // 2
    outs = [
        jax.ShapeDtypeStruct((seqs * count, inner), f32),
        jax.ShapeDtypeStruct((seqs, states + TAIL, inner), bf16),
        jax.ShapeDtypeStruct((seqs * count, states), bf16),
        jax.ShapeDtypeStruct((seqs * count, LANES), f32),
    ]
    return pl.pallas_call(
        functools.partial(mixer_local_kernel, heads, inner, both),
        grid=(seqs,),
        out_shape=outs,
        in_specs=[
            spec_rows(proj, count),
            spec_rows(proj, TAIL, seqs * count // TAIL),
            spec_whole(taps_x), spec_whole(taps_bc), spec_whole(head_row), spec_rows(pos, count),
        ],
        out_specs=[
            spec_rows(outs[0], count), spec_seq(outs[1]), spec_rows(outs[2], count),
            spec_rows(outs[3], count),
        ],
        scratch_shapes=[
            pltpu.VMEM((count + TAIL, inner), f32),
            pltpu.VMEM((count + TAIL, both), f32),
        ],
        compiler_params=params(),
        cost_estimate=cost(8),
        name="mixer_local",
    )(proj, proj, taps_x, taps_bc, head_row, pos)


def mixer_read_kernel(
    heads, pieces, first, y0_ref, c_ref, l_ref, qz_ref, att_ref, *refs
):
    packs = refs[:pieces]
    y_ref, out_ref, state_ref = refs[-3:]
    count = y0_ref.shape[0]
    states = c_ref.shape[1]
    qwidth = att_ref.shape[1]
    summed = l_ref[...]
    alive = (summed[:, LANES - 1 : LANES] == 0.0).astype(f32)
    low_half = lane_ids((count, LANES)) < HD
    out_ref[:, :qwidth] = att_ref[...]
    for j in range(heads // 2):
        span = slice(j * LANES, (j + 1) * LANES)
        state = chained_state(packs, span, states).astype(bf16)
        state_ref[0, :, span] = state
        reads = jnp.exp(pair(summed, j, low_half)) * alive
        y = y0_ref[:, span] + reads * dot(c_ref[...], state)
        y_ref[:, span] = y
        gate = qz_ref[:, first + j * LANES : first + (j + 1) * LANES]
        out_ref[:, qwidth + j * LANES : qwidth + (j + 1) * LANES] = (y * gate * sig(gate)).astype(bf16)


def mixer_read(y_local, c_vec, summed, qz, att, packs, extra, heads, seqs, count, first):
    inner, states = y_local.shape[1], c_vec.shape[1]
    outs = [
        jax.ShapeDtypeStruct((seqs * count, inner), f32),
        jax.ShapeDtypeStruct((seqs * count, att.shape[1] + inner), bf16),
        jax.ShapeDtypeStruct((seqs, states, inner), bf16),
    ]
    args = (y_local, c_vec, summed, qz, att)
    return pl.pallas_call(
        functools.partial(mixer_read_kernel, heads, len(packs), first),
        grid=(seqs,),
        out_shape=outs,
        in_specs=[spec_rows(a, count) for a in args]
        + [spec_seq(p) for p in packs]
        + [spec_any()] * len(extra),
        out_specs=[spec_rows(outs[0], count), spec_rows(outs[1], count), spec_seq(outs[2])],
        compiler_params=params(),
        cost_estimate=cost(4),
        name="mixer_read",
    )(*args, *packs, *extra)


def gate_back_kernel(
    heads, first, qwidth, d_ref, y_ref, qz_ref, c_ref, l_ref,
    dy_ref, dz_ref, datt_ref, pack_ref,
):
    count = y_ref.shape[0]
    states = c_ref.shape[1]
    summed = l_ref[...]
    alive = (summed[:, LANES - 1 : LANES] == 0.0).astype(f32)
    last = summed[count - 1 : count, :]
    carry = jnp.exp(last) * (last[:, LANES - 1 : LANES] == 0.0).astype(f32)
    low_half = lane_ids((count, LANES)) < HD
    low_row = low_half[0:1, :]
    ct_low = jnp.transpose(c_ref[...].astype(f32)).astype(bf16)
    datt_ref[...] = d_ref[:, :qwidth].astype(bf16)
    for j in range(heads // 2):
        span = slice(j * LANES, (j + 1) * LANES)
        gate = qz_ref[:, first + j * LANES : first + (j + 1) * LANES]
        d_gated = d_ref[:, qwidth + j * LANES : qwidth + (j + 1) * LANES]
        sg = sig(gate)
        dy = d_gated * (gate * sg)
        dy_ref[:, span] = dy
        dz_ref[:, span] = (
            d_gated * y_ref[:, span] * (sg * (1.0 + gate * (1.0 - sg)))
        ).astype(bf16)
        reads = jnp.exp(pair(summed, j, low_half)) * alive
        pack_ref[0, :states, span] = dot(ct_low, (reads * dy).astype(bf16)).astype(bf16)
        pack_ref[0, states:, span] = jnp.broadcast_to(pair(carry, j, low_row), (TAIL, LANES)).astype(bf16)


def gate_back(d_mixer, y, qz, c_vec, summed, heads, seqs, count, first, qwidth):
    inner, states = y.shape[1], c_vec.shape[1]
    outs = [
        jax.ShapeDtypeStruct((seqs * count, inner), f32),
        jax.ShapeDtypeStruct((seqs * count, inner), bf16),
        jax.ShapeDtypeStruct((seqs * count, qwidth), bf16),
        jax.ShapeDtypeStruct((seqs, states + TAIL, inner), bf16),
    ]
    args = (d_mixer, y, qz, c_vec, summed)
    return pl.pallas_call(
        functools.partial(gate_back_kernel, heads, first, qwidth),
        grid=(seqs,),
        out_shape=outs,
        in_specs=[spec_rows(a, count) for a in args],
        out_specs=[spec_rows(o, count) for o in outs[:3]] + [spec_seq(outs[3])],
        compiler_params=params(),
        cost_estimate=cost(5),
        name="gate_back",
    )(*args)


def mixer_back_kernel(
    heads, inner, both, pieces, extra, proj_ref, tail_ref, tx_ref, tb_ref, hr_ref, pos_ref,
    dy_ref, y_ref, st_ref, *refs
):
    packs = refs[:pieces]
    main_ref, side_ref, gtx_ref, gtb_ref, gh_ref, jx, jb, ax, ab = refs[pieces + extra :]
    count = proj_ref.shape[0]
    states = both // 2
    pos = pos_ref[...]
    head_row = hr_ref[...]
    jx[0:TAIL, :] = tail_ref[:, :inner]
    jx[TAIL : TAIL + count, :] = proj_ref[:, :inner]
    jb[0:TAIL, :] = tail_ref[:, inner : inner + both]
    jb[TAIL : TAIL + count, :] = proj_ref[:, inner : inner + both]
    pre_b = conv_pre(jb, slice(0, both), tb_ref[...], pos, count)
    sig_b = sig(pre_b)
    bc = pre_b * sig_b
    b_low = bc[:, :states].astype(bf16)
    c_low = bc[:, states:].astype(bf16)
    pre_dt, dt, la, summed = decay_parts(proj_ref[:, inner + both :], head_row, pos, heads)
    rows = jnp.transpose(summed)
    row = lax.broadcasted_iota(jnp.int32, (count, count), 0)
    col = lax.broadcasted_iota(jnp.int32, (count, count), 1)
    marks = summed[:, LANES - 1 : LANES]
    valid = (row <= col) & (marks == rows[LANES - 1 : LANES, :])
    scores = dot_nt(b_low, c_low)
    last = summed[count - 1 : count, :]
    carry = jnp.exp(last) * (last[:, LANES - 1 : LANES] == 0.0).astype(f32)
    same = (marks == last[:, LANES - 1 : LANES]).astype(f32)
    first = (marks == 0.0).astype(f32)
    low_half = lane_ids((count, LANES)) < HD
    low_row = low_half[0:1, :]
    lane = lane_ids((LANES, LANES))
    lane_row = lax.broadcasted_iota(jnp.int32, (LANES, LANES), 0)
    d_scores = jnp.zeros((count, count), f32)
    d_b = jnp.zeros((count, states), f32)
    d_c = jnp.zeros((count, states), f32)
    d_sum = jnp.zeros((count, LANES), f32)
    d_dt = jnp.zeros((count, LANES), f32)
    d_rows = jnp.zeros((8, LANES), f32)
    ax[...] = jnp.zeros_like(ax)
    ab[...] = jnp.zeros_like(ab)
    for j in range(heads // 2):
        span = slice(j * LANES, (j + 1) * LANES)
        taps = tx_ref[:, span]
        pre = conv_pre(jx, span, taps, pos, count)
        sg = sig(pre)
        xc = pre * sg
        dt_wide = pair(dt, j, low_half)
        u = xc * dt_wide
        u_low = u.astype(bf16)
        dy = dy_ref[:, span]
        dy_low = dy.astype(bf16)
        state = st_ref[0, :, span]
        later = chained_state(packs, span, states)
        d_state = later.astype(bf16)
        results = []
        for i, h in enumerate((2 * j, 2 * j + 1)):
            differ = rows[h : h + 1, :] - summed[:, h : h + 1]
            decay = jnp.exp(jnp.where(valid, differ, -1e30))
            half = low_half if i == 0 else jnp.logical_not(low_half)
            u_half = jnp.where(half, u, 0.0).astype(bf16)
            d_scores = d_scores + decay * dot_nt(u_half, dy_low)
            results.append(dot((decay * scores).astype(bf16), dy_low))
        left = jnp.exp(pair(last, j, low_row) - pair(summed, j, low_half)) * same
        reads = jnp.exp(pair(summed, j, low_half)) * first
        du_end = left * dot(b_low, d_state)
        du_in = jnp.where(low_half, results[0], results[1])
        du = du_in + du_end
        d_c = d_c + dot_nt((reads * dy).astype(bf16), state)
        d_b = d_b + dot_nt((left * u).astype(bf16), d_state)
        skip = pair(head_row[2:3, :], j, low_row)
        chosen = (
            ((lane == 2 * j) & (lane_row < HD)) | ((lane == 2 * j + 1) & (lane_row >= HD))
        ).astype(f32)
        per_token = (
            dy_low.astype(f32) * (y_ref[:, span] - skip * xc)
            - u_low.astype(f32) * du_in
            - u * du_end
        )
        d_sum = d_sum + jnp.dot(per_token, chosen, precision=highest, preferred_element_type=f32)
        d_dt = d_dt + jnp.dot(du * xc, chosen, precision=highest, preferred_element_type=f32)
        sums = jnp.concatenate(
            [
                jnp.sum(u * du_end, axis=0, keepdims=True),
                jnp.sum(dy * xc, axis=0, keepdims=True),
                jnp.sum(later * state.astype(f32), axis=0, keepdims=True),
                jnp.zeros((5, LANES), f32),
            ],
            axis=0,
        )
        d_rows = d_rows + jnp.dot(sums, chosen, precision=highest, preferred_element_type=f32)
        d_pre = (du * dt_wide + skip * dy) * (sg * (1.0 + pre * (1.0 - sg)))
        for k in range(KC):
            masked = d_pre * (pos >= k).astype(f32) if k else d_pre
            gtx_ref[0, k : k + 1, span] = jnp.sum(
                masked * jx[TAIL - k : TAIL - k + count, span], axis=0, keepdims=True
            )
            ax[TAIL - k : TAIL - k + count, span] += taps[k : k + 1, :] * masked
    main_ref[:, :inner] = ax[TAIL:, :].astype(bf16)
    side_ref[:, :inner] = ax[:TAIL, :].astype(bf16)
    d_b = d_b + dot(d_scores.astype(bf16), c_low)
    d_c = d_c + dot(jnp.transpose(d_scores).astype(bf16), b_low)
    d_pre = jnp.concatenate([d_b, d_c], axis=1) * (sig_b * (1.0 + pre_b * (1.0 - sig_b)))
    for k in range(KC):
        masked = d_pre * (pos >= k).astype(f32) if k else d_pre
        gtb_ref[0, k : k + 1, :] = jnp.sum(
            masked * jb[TAIL - k : TAIL - k + count, :], axis=0, keepdims=True
        )
        ab[TAIL - k : TAIL - k + count, :] += tb_ref[k : k + 1, :] * masked
    main_ref[:, inner : inner + both] = ab[TAIL:, :].astype(bf16)
    side_ref[:, inner : inner + both] = ab[:TAIL, :].astype(bf16)
    token = lax.broadcasted_iota(jnp.int32, (count, LANES), 0)
    at_last = d_rows[0:1, :] + d_rows[2:3, :] * carry
    d_sum = d_sum + jnp.where(token == count - 1, at_last, 0.0)
    upper = (row <= col).astype(f32)
    d_la = jnp.dot(upper, d_sum, precision=highest, preferred_element_type=f32)
    d_la = jnp.where(lane_ids(d_la.shape) < heads, d_la, 0.0)
    d_dt = d_dt - jnp.exp(head_row[0:1, :]) * d_la
    d_dtr = d_dt * sig(pre_dt)
    d_dtr = jnp.where(lane_ids(d_dtr.shape) < heads, d_dtr, 0.0)
    main_ref[:, inner + both :] = d_dtr.astype(bf16)
    side_ref[:, inner + both :] = jnp.zeros((TAIL, LANES), bf16)
    gh_ref[0, 0:1, :] = jnp.sum(d_la * la, axis=0, keepdims=True)
    gh_ref[0, 1:2, :] = jnp.sum(d_dtr, axis=0, keepdims=True)
    gh_ref[0, 2:3, :] = d_rows[1:2, :]
    gh_ref[0, 3:8, :] = jnp.zeros((5, LANES), f32)


def mixer_back(
    number, made, proj, taps_x, taps_bc, head_row, pos, dy, y, state, packs, extra, heads, seqs, count
):
    inner, both = taps_x.shape[1], taps_bc.shape[1]
    width = proj.shape[1]
    outs = [
        jax.ShapeDtypeStruct((seqs * count, width), bf16),
        jax.ShapeDtypeStruct((seqs * TAIL, width), bf16),
        jax.ShapeDtypeStruct((1, KC, inner), f32),
        jax.ShapeDtypeStruct((1, KC, both), f32),
        jax.ShapeDtypeStruct((1, 8, LANES), f32),
    ]

    def rows_of(a, rows, block):
        return pl.BlockSpec((rows, a.shape[1]), lambda i: (block, 0))

    def seq_of(a):
        return pl.BlockSpec((1,) + a.shape[1:], lambda i: (number,) + (0,) * (a.ndim - 1))

    extra = list(made) + list(extra)
    first = 9 + len(packs)
    return pl.pallas_call(
        functools.partial(mixer_back_kernel, heads, inner, both, len(packs), len(extra)),
        grid=(1,),
        out_shape=outs,
        in_specs=[
            rows_of(proj, count, number),
            rows_of(proj, TAIL, seqs * count // TAIL + number),
            spec_whole(taps_x), spec_whole(taps_bc), spec_whole(head_row),
            rows_of(pos, count, number), rows_of(dy, count, number), rows_of(y, count, number),
            seq_of(state),
        ]
        + [seq_of(p) for p in packs]
        + [spec_any()] * len(extra),
        out_specs=[rows_of(outs[0], count, number), rows_of(outs[1], TAIL, number)]
        + [spec_seq(o) for o in outs[2:]],
        scratch_shapes=[
            pltpu.VMEM((count + TAIL, inner), f32),
            pltpu.VMEM((count + TAIL, both), f32),
            pltpu.VMEM((count + TAIL, inner), f32),
            pltpu.VMEM((count + TAIL, both), f32),
        ],
        input_output_aliases={first: 0, first + 1: 1} if made else {},
        compiler_params=params(),
        cost_estimate=cost(9),
        name="mixer_back",
    )(proj, proj, taps_x, taps_bc, head_row, pos, dy, y, state, *packs, *extra)


def half_turned(v):
    first = lane_ids(v.shape) % HD < HD // 2
    return jnp.where(
        first, -pltpu.roll(v, LANES - HD // 2, 1), pltpu.roll(v, HD // 2, 1)
    )


def rope_kernel(qwidth, qz_ref, cos_ref, sin_ref, q_ref, kv_ref):
    cosine, sine = cos_ref[...], sin_ref[...]
    for j in range(qwidth // LANES):
        v = qz_ref[:, j * LANES : (j + 1) * LANES]
        q_ref[:, j * LANES : (j + 1) * LANES] = (v * cosine + half_turned(v) * sine).astype(bf16)
    v = qz_ref[:, qwidth : qwidth + LANES]
    turned = v * cosine + half_turned(v) * sine
    kv_ref[...] = jnp.where(lane_ids(v.shape) < HD, turned, v).astype(bf16)


def rope(qz, cosine, sine, qwidth, seqs, count):
    outs = [
        jax.ShapeDtypeStruct((seqs * count, qwidth), bf16),
        jax.ShapeDtypeStruct((seqs * count, 2 * HD), bf16),
    ]
    return pl.pallas_call(
        functools.partial(rope_kernel, qwidth),
        grid=(seqs,),
        out_shape=outs,
        in_specs=[
            pl.BlockSpec((count, qwidth + LANES), lambda s: (s, 0)),
            spec_rows(cosine, count), spec_rows(sine, count),
        ],
        out_specs=[spec_rows(o, count) for o in outs],
        compiler_params=params(),
        cost_estimate=cost(2),
        name="rope",
    )(qz, cosine, sine)


def to_low(v, r, low_half):
    v = v.astype(f32)
    return jnp.where(low_half, v if r % 2 == 0 else pltpu.roll(v, HD, 1), 0.0)


def to_high(v, r, low_half):
    v = v.astype(f32)
    return jnp.where(low_half, 0.0, v if r % 2 else pltpu.roll(v, HD, 1))


def key_masks(pos, count, blocks):
    row = lax.broadcasted_iota(jnp.int32, (count, count), 0)
    col = lax.broadcasted_iota(jnp.int32, (count, count), 1)
    start = row - pos
    masks = []
    for d in range(blocks):
        mask = col - d * count >= start
        masks.append(mask & (col <= row) if d == 0 else mask)
    return masks


def attend_kernel(per_group, blocks, q_ref, pos_ref, *refs):
    kv = refs[:blocks]
    o_ref, lse_ref = refs[blocks:]
    count = q_ref.shape[0]
    masks = key_masks(pos_ref[...], count, blocks)
    low_half = lane_ids((count, LANES)) < HD
    lane = lane_ids((count, LANES))
    lse = jnp.zeros((count, LANES), f32)
    halves = []
    for r in range(per_group):
        span = slice(r // 2 * LANES, (r // 2 + 1) * LANES)
        q = to_low(q_ref[:, span], r, low_half).astype(bf16)
        scores = [
            jnp.where(masks[d], dot_nt(q, kv[d][...]) * 0.125, -1e30) for d in range(blocks)
        ]
        top = jnp.max(scores[0], axis=1, keepdims=True)
        for d in range(1, blocks):
            top = jnp.maximum(top, jnp.max(scores[d], axis=1, keepdims=True))
        weights = [jnp.exp(v - top) for v in scores]
        total = jnp.sum(weights[0], axis=1, keepdims=True)
        for d in range(1, blocks):
            total = total + jnp.sum(weights[d], axis=1, keepdims=True)
        scale = 1.0 / total
        out = dot((weights[0] * scale).astype(bf16), kv[0][...])
        for d in range(1, blocks):
            out = out + dot((weights[d] * scale).astype(bf16), kv[d][...])
        lse = jnp.where(lane == r, top + jnp.log(total), lse)
        halves.append(out)
        if r % 2:
            o_ref[:, span] = jnp.where(low_half, pltpu.roll(halves[r - 1], HD, 1), out).astype(bf16)
    lse_ref[...] = lse


def attend(q, pos, kv, seqs, count):
    per_group = q.shape[1] // HD
    outs = [
        jax.ShapeDtypeStruct(q.shape, bf16),
        jax.ShapeDtypeStruct((q.shape[0], LANES), f32),
    ]
    return pl.pallas_call(
        functools.partial(attend_kernel, per_group, len(kv)),
        grid=(seqs,),
        out_shape=outs,
        in_specs=[spec_rows(a, count) for a in (q, pos, *kv)],
        out_specs=[spec_rows(o, count) for o in outs],
        compiler_params=params(),
        cost_estimate=cost(8),
        name="attend",
    )(q, pos, *kv)


def attend_back_kernel(per_group, blocks, q_ref, pos_ref, do_ref, lse_ref, cos_ref, sin_ref, *refs):
    kv = refs[:blocks]
    dq_ref = refs[blocks]
    dkv = refs[blocks + 1 :]
    count = q_ref.shape[0]
    masks = key_masks(pos_ref[...], count, blocks)
    low_half = lane_ids((count, LANES)) < HD
    cosine, sine = cos_ref[...], sin_ref[...]
    totals = [jnp.zeros((LANES, count), f32) for _ in range(blocks)]
    halves = []
    for r in range(per_group):
        span = slice(r // 2 * LANES, (r // 2 + 1) * LANES)
        q = to_low(q_ref[:, span], r, low_half)
        do = to_high(do_ref[:, span], r, low_half)
        q_turned = (jnp.transpose(q) * 0.125).astype(bf16)
        do_turned = jnp.transpose(do).astype(bf16)
        q, do = q.astype(bf16), do.astype(bf16)
        lse = lse_ref[:, r : r + 1]
        probs, d_probs = [], []
        row_dot = None
        for d in range(blocks):
            scores = jnp.where(masks[d], dot_nt(q, kv[d][...]) * 0.125, -1e30)
            probs.append(jnp.exp(scores - lse))
            d_probs.append(dot_nt(do, kv[d][...]))
            part = jnp.sum(probs[d] * d_probs[d], axis=1, keepdims=True)
            row_dot = part if row_dot is None else row_dot + part
        dq = None
        for d in range(blocks):
            d_scores = (probs[d] * (d_probs[d] - row_dot)).astype(bf16)
            part = dot(d_scores, kv[d][...])
            dq = part if dq is None else dq + part
            totals[d] = (
                totals[d] + dot(q_turned, d_scores) + dot(do_turned, probs[d].astype(bf16))
            )
        halves.append(dq * 0.125)
        if r % 2:
            both = jnp.where(low_half, halves[r - 1], pltpu.roll(halves[r], HD, 1))
            dq_ref[:, span] = (both * cosine - half_turned(both) * sine).astype(bf16)
    for d in range(blocks):
        dkv[d][...] = jnp.transpose(totals[d]).astype(dkv[d].dtype)


def attend_back(q, pos, d_out, lse, cosine, sine, kv, seqs, count):
    per_group = q.shape[1] // HD
    outs = [jax.ShapeDtypeStruct(q.shape, bf16)] + [
        jax.ShapeDtypeStruct(kv[0].shape, bf16 if d else f32) for d in range(len(kv))
    ]
    args = (q, pos, d_out, lse, cosine, sine, *kv)
    return pl.pallas_call(
        functools.partial(attend_back_kernel, per_group, len(kv)),
        grid=(seqs,),
        out_shape=outs,
        in_specs=[spec_rows(a, count) for a in args],
        out_specs=[spec_rows(o, count) for o in outs],
        compiler_params=params(),
        cost_estimate=cost(14),
        name="attend_back",
    )(*args)


def join_back_kernel(pieces, dq_ref, dz_ref, cos_ref, sin_ref, *refs):
    out_ref = refs[-1]
    qwidth = dq_ref.shape[1]
    total = refs[0][...].astype(f32)
    for piece in refs[1:pieces]:
        total = total + piece[...].astype(f32)
    turned = total * cos_ref[...] - half_turned(total) * sin_ref[...]
    out_ref[:, :qwidth] = dq_ref[...]
    out_ref[:, qwidth : qwidth + LANES] = jnp.where(
        lane_ids(total.shape) < HD, turned, total
    ).astype(bf16)
    out_ref[:, qwidth + LANES :] = dz_ref[...]


def join_back(dq, dz, cosine, sine, pieces, extra, seqs, count):
    out = jax.ShapeDtypeStruct((dq.shape[0], dq.shape[1] + LANES + dz.shape[1]), bf16)
    args = (dq, dz, cosine, sine, *pieces)
    return pl.pallas_call(
        functools.partial(join_back_kernel, len(pieces)),
        grid=(seqs,),
        out_shape=out,
        in_specs=[spec_rows(a, count) for a in args] + [spec_any()] * len(extra),
        out_specs=spec_rows(out, count),
        compiler_params=params(),
        cost_estimate=cost(2),
        name="join_back",
    )(*args, *extra)


def attend_one(q, k, v, mask):
    scores = jnp.einsum("qrd,kd->rqk", q, k, preferred_element_type=f32) * 0.125
    scores = jnp.where(mask[None], scores, -1e30)
    top = jnp.max(scores, axis=-1, keepdims=True)
    weights = jnp.where(mask[None], jnp.exp(scores - top), 0.0)
    total = jnp.sum(weights, axis=-1, keepdims=True)
    out = jnp.einsum("rqk,kd->qrd", (weights / total).astype(bf16), v, preferred_element_type=f32)
    return out, jnp.transpose((top + jnp.log(total))[..., 0])


def attend_one_back(q, k, v, mask, d_out, lse):
    scores = jnp.einsum("qrd,kd->rqk", q, k, preferred_element_type=f32) * 0.125
    probs = jnp.where(mask[None], jnp.exp(scores - jnp.transpose(lse)[..., None]), 0.0)
    d_probs = jnp.einsum("qrd,kd->rqk", d_out, v, preferred_element_type=f32)
    row_dot = jnp.sum(probs * d_probs, axis=-1, keepdims=True)
    d_scores = (probs * (d_probs - row_dot)).astype(bf16)
    d_q = jnp.einsum("rqk,kd->qrd", d_scores, k, preferred_element_type=f32) * 0.125
    d_k = jnp.einsum("rqk,qrd->kd", d_scores, q, preferred_element_type=f32) * 0.125
    d_v = jnp.einsum("rqk,qrd->kd", probs.astype(bf16), d_out, preferred_element_type=f32)
    return d_q, jnp.concatenate([d_k, d_v], axis=-1)


class Attention:
    def __init__(self, q, kv, pos, seqs, count):
        self.q, self.pos, self.seqs, self.count = q, pos, seqs, count
        self.blocks = lax.axis_size("ctx")
        self.few = self.blocks <= 4
        if self.few:
            self.kv = [kv] + [shifted(kv, "ctx", d) for d in range(1, self.blocks)]
            return
        me = lax.axis_index("ctx")
        shaped = lax.all_gather(kv.reshape(seqs, count, -1), "ctx", axis=1, tiled=True)
        self.all_kv = shaped
        keys = jnp.arange(shaped.shape[1])
        tokens = me * count + jnp.arange(count)
        starts = tokens[None, :] - pos.reshape(seqs, count)
        self.mask = (keys[None, None, :] <= tokens[None, :, None]) & (
            keys[None, None, :] >= starts[:, :, None]
        )

    def heads_of(self, v):
        return v.reshape(self.seqs, self.count, -1, HD)

    def forward(self):
        if self.few:
            out, self.lse = attend(self.q, self.pos, self.kv, self.seqs, self.count)
            return out
        keys, values = self.all_kv[..., :HD], self.all_kv[..., HD:]
        out, self.lse = lax.map(
            lambda a: attend_one(*a), (self.heads_of(self.q), keys, values, self.mask)
        )
        return out.astype(bf16).reshape(self.q.shape)

    def backward(self, d_out, cosine, sine):
        if self.few:
            dq, own, *rest = attend_back(
                self.q, self.pos, d_out, self.lse, cosine, sine, self.kv, self.seqs, self.count
            )
            return dq, [own] + [
                shifted(piece, "ctx", -d) for d, piece in enumerate(rest, start=1)
            ]
        keys, values = self.all_kv[..., :HD], self.all_kv[..., HD:]
        dq, kept = lax.map(
            lambda a: attend_one_back(*a),
            (self.heads_of(self.q), keys, values, self.mask, self.heads_of(d_out), self.lse),
        )
        dq = dq.reshape(self.q.shape)
        cos_q = jnp.tile(cosine, (1, dq.shape[1] // LANES))
        sin_q = jnp.tile(sine, (1, dq.shape[1] // LANES))
        dq = dq * cos_q - jnp.dot(dq, turn_matrix(dq.shape[1]), precision=highest) * sin_q
        total = lax.psum_scatter(kept.astype(bf16), "ctx", scatter_dimension=1, tiled=True)
        return dq.astype(bf16), [total.astype(f32).reshape(-1, 2 * HD)]


def turn_matrix(columns):
    source = jnp.arange(columns)[:, None]
    target = jnp.arange(columns)[None, :]
    half = HD // 2
    low = target % HD < half
    minus = low & (source == target + half)
    plus = jnp.logical_not(low) & (source == target - half)
    return plus.astype(f32) - minus.astype(f32)


def per_device(
    hidden_in,
    positions,
    gain_attn,
    w_qkv,
    w_attn_out,
    w_zx,
    w_bc,
    w_dt,
    conv_x,
    conv_bc,
    a_log,
    dt_bias,
    d_skip,
    w_mamba_out,
    gain_ffn,
    w_gu,
    w_down,
    output_cotangent,
):
    seqs, block = positions.shape
    features = hidden_in.shape[2]
    rows = w_qkv.shape[0]
    heads = a_log.shape[0]
    inner = w_zx.shape[2]
    both = w_bc.shape[1]
    columns = w_qkv.shape[2]
    qwidth = columns - 2 * HD
    units = w_gu.shape[2]
    count = lax.axis_size("ctx")
    place = lax.axis_index("ctx")
    here = seqs * block

    pad = jnp.zeros((rows, LANES - heads - 2), bf16)
    first_pack = jnp.concatenate(
        [w_zx[:, 1, :], w_bc, w_dt, gain_attn[:, None], gain_ffn[:, None], pad], axis=1
    )
    tail = shifted(hidden_in[:, block - TAIL :, :], "ctx", 1)
    down = w_down.T
    half = units // 2
    pos = positions.reshape(here, 1)
    frequency = jnp.power(jnp.float32(rope_base), -jnp.arange(0, HD, 2).astype(f32) / HD)
    turned = pos.astype(f32) * jnp.tile(frequency, 2 * LANES // HD)
    cosine, sine = jnp.cos(turned), jnp.sin(turned)

    x_own = hidden_in.reshape(here, features).astype(f32)
    x_ext = jnp.concatenate([x_own, tail.reshape(seqs * TAIL, features).astype(f32)], axis=0)
    r_ext = lax.rsqrt(jnp.mean(x_ext * x_ext, axis=-1, keepdims=True) + 1e-05)
    r_one = r_ext[:here]
    taps_x = conv_x.astype(f32)
    taps_bc = conv_bc.astype(f32)
    head_row = jnp.pad(
        jnp.stack([a_log, dt_bias, d_skip]), ((0, 5), (0, LANES - heads))
    )

    def with_first(w_one):
        gain_a = w_one[:, inner + both + heads].astype(f32)
        h_ext = (x_ext * r_ext * gain_a).astype(bf16)
        proj = dot(h_ext, w_one)
        local = mixer_local(proj, taps_x, taps_bc, head_row, pos, heads, seqs, block)
        return w_one, gain_a, h_ext, proj, local, local[1]

    made, w_two, w_three, w_four, w_five, nears = gather_all(
        first_pack,
        ([w_qkv[:, 0, :], w_zx[:, 0, :]], [w_attn_out.T, w_mamba_out.T]),
        (
            [(w_gu[:, 0, :], 0, 0), (down[:, :half], 1, 0)],
            [(w_gu[:, 1, :], 0, units), (down[:, half:], 1, half)],
        ),
        with_first,
    )
    w_one, gain_a, h_ext, proj, (y_local, pack, c_vec, summed), _ = made
    gain_f = w_one[:, inner + both + heads + 1].astype(f32)
    h_own = h_ext[:here]
    packs = chain_pieces(pack, False)

    qz = dot(h_own, w_two)
    q_low, kv_low = rope(qz, cosine, sine, qwidth, seqs, block)
    attention = Attention(q_low, kv_low, pos, seqs, block)
    attended = attention.forward()

    y, mixer_out, state = mixer_read(
        y_local, c_vec, summed, qz, attended, packs, nears, heads, seqs, block, columns
    )
    resid = x_own + pair_sum(dot_nt(mixer_out, w_three))

    r_two = lax.rsqrt(jnp.mean(resid * resid, axis=-1, keepdims=True) + 1e-05)
    h_two = (resid * r_two * gain_f).astype(bf16)
    gate_up = dot(h_two, w_four)
    gate_ff, up_ff = gate_up[:, :units], gate_up[:, units:]
    sig_ff = jax.nn.sigmoid(gate_ff)
    silu_ff = gate_ff * sig_ff
    hidden_state = (silu_ff * up_ff).astype(bf16)
    ffn = pair_sum(dot_nt(hidden_state, w_five))
    block_out = (resid + ffn).astype(bf16).reshape(seqs, block, features)

    e_low = output_cotangent.reshape(here, features)
    d_hidden_state = dot(e_low, w_five)
    d_gate_up = jnp.concatenate(
        [
            d_hidden_state * up_ff * (sig_ff * (1.0 + gate_ff * (1.0 - sig_ff))),
            d_hidden_state * silu_ff,
        ],
        axis=1,
    ).astype(bf16)

    def tn(a, b):
        return lax.dot_general(a, b, (((0,), (0,)), ((), ())), preferred_element_type=f32)

    d_h_two_part = dot_nt(d_gate_up, w_four).astype(bf16)
    d_h_two = pair_sum(d_h_two_part)
    g_four, g_five = tn(h_two, d_gate_up).astype(bf16), tn(e_low, hidden_state).astype(bf16)
    ffn_sum = Scatter(
        [[g_four[:, :units], g_five[:, :half]], [g_four[:, units:], g_five[:, half:]]]
    )
    grad_gain_f = jnp.sum(d_h_two_part.astype(f32) * resid * r_two, axis=0)
    scaled = d_h_two * gain_f
    d_resid = (
        e_low.astype(f32)
        + r_two * scaled
        - resid * (r_two * r_two * r_two) * jnp.mean(resid * scaled, axis=-1, keepdims=True)
    )
    d_mix = d_resid.astype(bf16)

    d_mixer = dot(d_mix, w_three)
    d_y, d_z, d_att, d_pack = gate_back(
        d_mixer, y, qz, c_vec, summed, heads, seqs, block, columns, qwidth
    )
    later_packs = chain_pieces(d_pack, True)
    d_q, d_kv = attention.backward(d_att, cosine, sine)
    d_two = join_back(d_q, d_z, cosine, sine, d_kv, ffn_sum.got, seqs, block)
    two_sum = Scatter([[tn(h_own, d_two).astype(bf16)], [tn(d_mix, mixer_out).astype(bf16)]])
    ffn_sum.second()
    ffn_sum.third()
    d_main, d_side, small_grads = None, None, []
    for number in range(seqs):
        extra = []
        if number == 0:
            extra = ffn_sum.near
        if number == seqs - 1:
            extra = ffn_sum.along + two_sum.got
        d_main, d_side, *rest = mixer_back(
            number, (d_main, d_side) if number else (), proj, taps_x, taps_bc, head_row, pos,
            d_y, y, state, later_packs, extra, heads, seqs, block,
        )
        small_grads.append(rest)
    g_taps_x, g_taps_bc, g_heads = [sum(g[i] for g in small_grads) for i in range(3)]
    two_sum.second()
    one_sum = Scatter([[(tn(h_own, d_main) + tn(h_ext[here:], d_side)).astype(bf16)]])
    two_sum.third()
    one_sum.third()
    ffn_grads, two_grads, one_grads = ffn_sum.result(), two_sum.result(), one_sum.result()
    ffn_gate, ffn_up = ffn_grads[:, :units], ffn_grads[:, units + half : 2 * units + half]
    ffn_down = jnp.concatenate(
        [ffn_grads[:, units : units + half], ffn_grads[:, 2 * units + half :]], axis=1
    )

    d_tail = dot_nt(d_side, w_one)
    d_h_part = (dot_nt(d_two, w_two) + dot_nt(d_main, w_one)).astype(bf16)
    grad_gain_a = jnp.sum(d_h_part.astype(f32) * x_own * r_one, axis=0) + jnp.sum(
        d_tail * x_ext[here:] * r_ext[here:], axis=0
    )
    d_tail = shifted(pair_sum(d_tail).astype(bf16), "ctx", -1).astype(f32)
    d_h = pair_sum(d_h_part).reshape(seqs, block, features)
    d_h = d_h + jnp.pad(d_tail.reshape(seqs, TAIL, features), ((0, 0), (block - TAIL, 0), (0, 0)))
    d_h = d_h.reshape(here, features)
    scaled = d_h * gain_a
    d_hidden = (
        d_resid
        + r_one * scaled
        - x_own * (r_one * r_one * r_one) * jnp.mean(x_own * scaled, axis=-1, keepdims=True)
    )
    d_hidden = d_hidden.astype(bf16).reshape(seqs, block, features)

    over_pair = jnp.concatenate(
        [grad_gain_a, jnp.sum(g_taps_bc, axis=0).reshape(-1), grad_gain_f]
    )
    over_pair = sum_all(over_pair, ("tp",))
    over_rest = jnp.concatenate(
        [
            jnp.sum(g_taps_x, axis=0).reshape(-1),
            jnp.sum(g_heads, axis=0)[:3, :heads].reshape(-1),
            over_pair,
        ]
    )
    total = sum_all(over_rest, ("dp", "ctx"))
    sizes = (KC * inner, heads, heads, heads, features, KC * both, features)
    small, first = [], 0
    for size in sizes:
        small.append(total[first : first + size])
        first += size
    g_tx, g_decay, g_bias, g_skip, g_gain_a, g_tb, g_gain_f = small
    shard = lax.axis_index("dp") * count + place

    def own_rows(vector):
        return lax.dynamic_slice_in_dim(vector, shard * rows, rows, 0)

    bc_grad = one_grads[:, inner : inner + both]
    bc_grad = sum_all(bc_grad, ("tp",))
    zx_grad = jnp.stack(
        [two_grads[:, columns : columns + inner], one_grads[:, :inner]], axis=1
    )
    return (
        block_out,
        d_hidden,
        own_rows(g_gain_a),
        two_grads[:, None, :columns],
        two_grads[:, columns + inner : columns + inner + qwidth].T,
        zx_grad,
        bc_grad,
        one_grads[:, inner + both : inner + both + heads],
        g_tx.reshape(KC, inner),
        g_tb.reshape(KC, both),
        g_decay,
        g_bias,
        g_skip,
        two_grads[:, columns + inner + qwidth :].T,
        own_rows(g_gain_f),
        jnp.stack([ffn_gate, ffn_up], axis=1),
        ffn_down.T,
    )


def solution(mesh):
    in_specs = (
        P("dp", "ctx", None),
        P("dp", "ctx"),
        P(("dp", "ctx")),
        P(("dp", "ctx"), "tp", None),
        P("tp", ("dp", "ctx")),
        P(("dp", "ctx"), None, "tp"),
        P(("dp", "ctx"), None),
        P(("dp", "ctx"), "tp"),
        P(None, "tp"),
        P(),
        P("tp"),
        P("tp"),
        P("tp"),
        P("tp", ("dp", "ctx")),
        P(("dp", "ctx")),
        P(("dp", "ctx"), None, "tp"),
        P("tp", ("dp", "ctx")),
        P("dp", "ctx", None),
    )
    out_specs = (
        P("dp", "ctx", None),
        P("dp", "ctx", None),
        P(("dp", "ctx")),
        P(("dp", "ctx"), "tp", None),
        P("tp", ("dp", "ctx")),
        P(("dp", "ctx"), None, "tp"),
        P(("dp", "ctx"), None),
        P(("dp", "ctx"), "tp"),
        P(None, "tp"),
        P(),
        P("tp"),
        P("tp"),
        P("tp"),
        P("tp", ("dp", "ctx")),
        P(("dp", "ctx")),
        P(("dp", "ctx"), None, "tp"),
        P("tp", ("dp", "ctx")),
    )
    return jax.shard_map(
        per_device, mesh=mesh, in_specs=in_specs, out_specs=out_specs, check_vma=False
    )
```

time: 571 us -> 464 us (0.81)
  waiting for transfers between devices: 175 us -> 129 us
  local copies, waits for them, and re-layouts: 75 us -> 38 us
  Pallas kernels: 45.1 us -> 77.8 us
  matrix products: 69.9 us -> 41.5 us
  other arithmetic: 69.6 us -> 41.7 us
    ppermute x58 -> x55, waiting for transfers between devices: 159 us -> 122 us  [swap(): return lax.ppermute(value, axis, [(i, i ^ bits) for i in range(count)])]
    pallas_call x8 -> x13, Pallas kernels: 45.1 us -> 77.8 us  [the longest x2 20 us: mixer_back(): pl.pallas_call(functools.partial(mixer_back_kernel, heads, inner, both, l...]
    dot_general x9 -> x0, matrix products: 29.4 us -> none  [the longest x1 7.21 us: per_device(): jnp.dot(d_rot * sine, turn.T, precision=lax.Precision.HIGH)]
    reshape x12 -> x0, local copies, waits for them, and re-layouts: 14.3 us -> none  [the longest x2 5.2 us: per_device(): kept.reshape(seqs, count, block, 2 * HD)]
    convert_element_type x16 -> x11, other arithmetic: 29.4 us -> 15.5 us  [the longest x4 6.74 us: second(): send = (pick(kept, 1 - then, 0).astype(f32) + pick(got, 1 - then, 0).asty...]
    ppermute x17 -> x14, waiting for transfers between devices: 15.8 us -> 6.94 us  [shifted(): return lax.ppermute(value, axis, route)]
    slice x14 -> x8, local copies, waits for them, and re-layouts: 11.1 us -> 5.21 us  [the longest x1 1.48 us: per_device(): w_gu[:, 1, :]]
    ppermute x58 -> x55, starting transfers between devices: 84.9 us -> 88.2 us  [swap(): return lax.ppermute(value, axis, [(i, i ^ bits) for i in range(count)])]
  transfers between devices with their start and end apart: 75 -> 69, of which waited for: 24 -> 22; matrix products, arithmetic and copies ran while one was open for 34% -> 18% of each run, Pallas kernels for 8% -> 13%
where the time goes in v2:
time: 464 us; the launch traced here: 455 us
  waiting for transfers between devices  129 us (28%)
  starting transfers between devices  124 us (27%)
  Pallas kernels  77.8 us (17%)
  other arithmetic  41.7 us (9%)
  matrix products  41.5 us (9%)
  local copies, waits for them, and re-layouts  38 us (8%)
    ppermute x55, waiting for transfers between devices, swap(): return lax.ppermute(value, axis, [(i, i ^ bits) for i in range(count)])  122 us
    ppermute x55, starting transfers between devices, swap(): return lax.ppermute(value, axis, [(i, i ^ bits) for i in range(count)])  88.2 us
    ppermute x14, starting transfers between devices, shifted(): return lax.ppermute(value, axis, route)  36.2 us
    pallas_call x2, Pallas kernels, mixer_back(): pl.pallas_call(functools.partial(mixer_back_kernel, heads, inner, both, l...  20 us
    pallas_call x4, Pallas kernels, place_blocks(): pl.pallas_call(kernel, out_shape=[jax.ShapeDtypeStruct(shape, pieces[0].d...  19.8 us
    unnamed x189, local copies, waits for them, and re-layouts  16.7 us
    dot_general x6, matrix products, dot_nt(): lax.dot_general(a, b, (((1,), (1,)), ((), ())), preferred_element_type=f32)  14.9 us
    dot_general x5, matrix products, dot(): return jnp.dot(a, b, preferred_element_type=f32)  14.8 us
  transfers between devices with their start and end apart: 69, of which 22 were waited for; matrix products, arithmetic and copies ran while one was open for 18% of the time, Pallas kernels for 13%

profile of v2, /device:TPU:0, one launch (start us, length us, event | category | flops | bytes accessed | tf_op | source)
XLA Modules:
  0.0 455.0 jit_solution(8908512755619153239)
XLA Ops:
  14.5 8.0 %collective-permute-done.2.refs_2_ = bf16[64,1152]{1,0:T(8,128)(2,1)S(1)} collective-permute-done((bf16[64,1152]{1,0:T(8,128)(2,1)S(1)}, bf16[64,1152]{1,0:T(8,128)(2,1)S(1)}, u32[]{:S(2)}, u32[]{:S(2)}) %collective-permute-start.2) | collective-permute-done | bytes 147488 | tf_op jit(solution)/shard_map/ppermute | solution.py:28
  33.7 6.9 %collective-permute-done.7.refs_5_ = bf16[64,2176]{1,0:T(8,128)(2,1)} collective-permute-done((bf16[64,2176]{1,0:T(8,128)(2,1)}, bf16[64,2176]{1,0:T(8,128)(2,1)}, u32[]{:S(2)}, u32[]{:S(2)}) %collective-permute-start.7) | collective-permute-done | bytes 278560 | tf_op jit(solution)/shard_map/ppermute | solution.py:28
  44.8 9.9 %collective-permute-done.8.refs_6_ = bf16[64,2176]{1,0:T(8,128)(2,1)S(1)} collective-permute-done((bf16[64,2176]{1,0:T(8,128)(2,1)}, bf16[64,2176]{1,0:T(8,128)(2,1)S(1)}, u32[]{:S(2)}, u32[]{:S(2)}) %collective-permute-start.8) | collective-permute-done | bytes 278560 | tf_op jit(solution)/shard_map/ppermute | solution.py:28
  76.8 9.0 %collective-permute-done.16.refs_9_ = bf16[64,3072]{1,0:T(8,128)(2,1)} collective-permute-done((bf16[64,3072]{1,0:T(8,128)(2,1)}, bf16[64,3072]{1,0:T(8,128)(2,1)}, u32[]{:S(2)}, u32[]{:S(2)}) %collective-permute-start.16) | collective-permute-done | bytes 393248 | tf_op jit(solution)/shard_map/ppermute | solution.py:28
  88.1 10.2 %collective-permute-start.18 = (bf16[64,3072]{1,0:T(8,128)(2,1)}, bf16[64,3072]{1,0:T(8,128)(2,1)S(1)}, u32[]{:S(2)}, u32[]{:S(2)}) collective-permute-start(bf16[64,3072]{1,0:T(8,128)(2,1)} %get-tuple-element.67.refs_8_), channel_id=1, source_target_pairs={{0,6},{2,4},{4,2},{6,0},{1,7},{3,5},{5,3},{7,1},{8,14},{10,12},{12... | collective-permute-start | bytes 1179656 | tf_op jit(solution)/shard_map/ppermute | solution.py:28
  101.4 7.3 %mixer_local.1 = (f32[512,768]{1,0:T(8,128)}, bf16[2,144,768]{2,1,0:T(8,128)(2,1)}, bf16[512,128]{1,0:T(8,128)(2,1)}, f32[512,128]{1,0:T(8,128)}) custom-call(f32[544,1152]{1,0:T(8,128)} %fusion.58.proj_ref.tail_ref, f32[544,1152]{1,0:T(8,128)} %fusion.58.proj_ref.tail_ref, f32[4,768]{1,0:T(4,128)} %convert_element_type.346.tx_ref, ...), custom_call_target="tpu_custom_call" | custom-call | flops 800000000 | bytes 2400000 | tf_op jit(solution)/shard_map/mixer_local/pallas_call | solution.py:450
  110.1 6.1 %collective-permute-start.23 = (bf16[2,144,768]{2,1,0:T(8,128)(2,1)}, bf16[2,144,768]{2,1,0:T(8,128)(2,1)S(1)}, u32[]{:S(2)}, u32[]{:S(2)}) collective-permute-start(bf16[2,144,768]{2,1,0:T(8,128)(2,1)} %get-tuple-element.68.refs_12_), channel_id=1, source_target_pairs={{0,4},{2,6},{1,5},{3,7},{8,12},{10,14},{9,13},{11,15},{16,20},{18,... | collective-permute-start | bytes 1327112 | tf_op jit(solution)/shard_map/ppermute | solution.py:34
  117.1 6.1 %place_blocks.6 = (bf16[4,256,1152]{2,1,0:T(8,128)(2,1)}, bf16[4,256,1024]{2,1,0:T(8,128)(2,1)}, bf16[4,64,1536]{2,1,0:T(8,128)(2,1)}, bf16[4,64,1536]{2,1,0:T(8,128)(2,1)}) custom-call(s32[2]{0:T(128)} %pad_add_fusion.where_ref, bf16[256,1152]{1,0:T(8,128)(2,1)} %bitcast.20.refs_0_, bf16[256,1152]{1,0:T(8,128)(2,1)} %collective-permute-done.10.refs_1_, ...), custom_call_target="tpu_custom_call" | custom-call | tf_op jit(solution)/shard_map/place_blocks/pallas_call | solution.py:61
  135.8 7.7 %collective-permute-start.20 = (bf16[512,128]{1,0:T(8,128)(2,1)}, bf16[512,128]{1,0:T(8,128)(2,1)S(1)}, u32[]{:S(2)}, u32[]{:S(2)}) collective-permute-start(bf16[512,128]{1,0:T(8,128)(2,1)} %get-tuple-element.71.refs_0_), channel_id=1, source_target_pairs={{0,4},{2,6},{1,5},{3,7},{8,12},{10,14},{9,13},{11,15},{16,20},{18,... | collective-permute-start | bytes 393224 | tf_op jit(solution)/shard_map/ppermute | solution.py:34
  153.0 6.5 %collective-permute-start.24 = (bf16[2,144,768]{2,1,0:T(8,128)(2,1)S(1)}, bf16[2,144,768]{2,1,0:T(8,128)(2,1)S(1)}, u32[]{:S(2)}, u32[]{:S(2)}) collective-permute-start(bf16[2,144,768]{2,1,0:T(8,128)(2,1)S(1)} %copy-done.46), channel_id=1, source_target_pairs={{0,6},{1,7},{8,14},{9,15},{16,22},{17,23},{24,30},{25,31}} | collective-permute-start | bytes 1327112 | tf_op jit(solution)/shard_map/ppermute | solution.py:34
  159.6 7.2 %attend.1 = (bf16[512,256]{1,0:T(8,128)(2,1)}, f32[512,128]{1,0:T(8,128)}) custom-call(bf16[512,256]{1,0:T(8,128)(2,1)} %get-tuple-element.70.q_ref, s32[512,1]{1,0:T(8,128)} %bitcast.245, bf16[512,128]{1,0:T(8,128)(2,1)} %get-tuple-element.71.refs_0_, bf16[512,128]{1,0:T(8,128)(2,1)} %copy-done.85, bf16[512,128]{1,0:T(8,128)(2,1)} %copy-done.86, ...), custom_call_target="tpu_custom_call" | custom-call | flops 800000000 | bytes 2400000 | tf_op jit(solution)/shard_map/attend/pallas_call | solution.py:843
  177.2 6.9 %collective-permute-start.30 = (bf16[256,1536]{1,0:T(8,128)(2,1)S(1)}, bf16[256,1536]{1,0:T(8,128)(2,1)}, u32[]{:S(2)}, u32[]{:S(2)}) collective-permute-start(bf16[256,1536]{1,0:T(8,128)(2,1)S(1)} %copy-done.15), channel_id=1, source_target_pairs={{0,16},{8,24},{16,0},{24,8},{1,17},{9,25},{17,1},{25,9},{2,18},{10... | collective-permute-start | bytes 2359304 | tf_op jit(solution)/shard_map/ppermute | solution.py:28
  185.7 16.7 %collective-permute-done.30.refs_3_ = bf16[256,1536]{1,0:T(8,128)(2,1)} collective-permute-done((bf16[256,1536]{1,0:T(8,128)(2,1)S(1)}, bf16[256,1536]{1,0:T(8,128)(2,1)}, u32[]{:S(2)}, u32[]{:S(2)}) %collective-permute-start.30) | collective-permute-done | bytes 786464 | tf_op jit(solution)/shard_map/ppermute | solution.py:28
  203.9 6.2 %place_blocks.7 = (bf16[4,256,2048]{2,1,0:T(8,128)(2,1)}, bf16[4,256,1024]{2,1,0:T(8,128)(2,1)}) custom-call(s32[2]{0:T(128)} %pad_add_fusion.where_ref, bf16[256,1536]{1,0:T(8,128)(2,1)} %bitcast.267, bf16[256,1536]{1,0:T(8,128)(2,1)} %copy-done.14, bf16[256,1536]{1,0:T(8,128)(2,1)} %copy-done.16, bf16[256,1536]{1,0:T(8,128)(2,1)} %collective-permute-done.30.refs_3_, ...), custom_call_target="tpu_custom_call" | custom-call | tf_op jit(solution)/shard_map/place_blocks/pallas_call | solution.py:61
  242.0 9.5 %attend_back.1 = (bf16[512,256]{1,0:T(8,128)(2,1)}, f32[512,128]{1,0:T(8,128)}, bf16[512,128]{1,0:T(8,128)(2,1)}, bf16[512,128]{1,0:T(8,128)(2,1)}, bf16[512,128]{1,0:T(8,128)(2,1)}) custom-call(bf16[512,256]{1,0:T(8,128)(2,1)} %get-tuple-element.70.q_ref, s32[512,1]{1,0:T(8,128)} %bitcast.246, bf16[512,256]{1,0:T(8,128)(2,1)} %get-tuple-element.80.do_ref, ...), custom_call_target="tpu_custom_call" | custom-call | flops 1400000000 | bytes 4200000 | tf_op jit(solution)/shard_map/attend_back/pallas_call | solution.py:903
  259.0 7.4 %collective-permute-done.38.refs_5_ = bf16[2,256,1536]{2,1,0:T(8,128)(2,1)} collective-permute-done((bf16[2,256,1536]{2,1,0:T(8,128)(2,1)}, bf16[2,256,1536]{2,1,0:T(8,128)(2,1)}, u32[]{:S(2)}, u32[]{:S(2)}) %collective-permute-start.38) | collective-permute-done | bytes 1572896 | tf_op jit(solution)/shard_map/ppermute | solution.py:28
  283.6 9.2 %collective-permute-done.48.refs_9_ = bf16[2,256,1024]{2,1,0:T(8,128)(2,1)} collective-permute-done((bf16[2,256,1024]{2,1,0:T(8,128)(2,1)}, bf16[2,256,1024]{2,1,0:T(8,128)(2,1)}, u32[]{:S(2)}, u32[]{:S(2)}) %collective-permute-start.48) | collective-permute-done | bytes 1048608 | tf_op jit(solution)/shard_map/ppermute | solution.py:28
  298.9 8.6 %collective-permute-done.42.refs_3_ = bf16[256,1536]{1,0:T(8,128)(2,1)} collective-permute-done((bf16[256,1536]{1,0:T(8,128)(2,1)}, bf16[256,1536]{1,0:T(8,128)(2,1)}, u32[]{:S(2)}, u32[]{:S(2)}) %collective-permute-start.42) | collective-permute-done | bytes 786464 | tf_op jit(solution)/shard_map/ppermute | solution.py:28
  316.0 9.7 %mixer_back.2 = (bf16[512,1152]{1,0:T(8,128)(2,1)}, bf16[32,1152]{1,0:T(8,128)(2,1)}, f32[1,4,768]{2,1,0:T(4,128)}, f32[1,4,256]{2,1,0:T(4,128)}, f32[1,8,128]{2,1,0:T(8,128)}) custom-call(f32[544,1152]{1,0:T(8,128)} %fusion.58.proj_ref.tail_ref, f32[544,1152]{1,0:T(8,128)} %fusion.58.proj_ref.tail_ref, f32[4,768]{1,0:T(4,128)} %convert_element_type.346.tx_ref, ...), custom_call_target="tpu_custom_call" | custom-call | flops 900000000 | bytes 2700000 | tf_op jit(solution)/shard_map/mixer_back/pallas_call | solution.py:718
  333.5 7.4 %collective-permute-done.45.refs_6_ = bf16[64,3072]{1,0:T(8,128)(2,1)S(1)} collective-permute-done((bf16[64,3072]{1,0:T(8,128)(2,1)S(1)}, bf16[64,3072]{1,0:T(8,128)(2,1)S(1)}, u32[]{:S(2)}, u32[]{:S(2)}) %collective-permute-start.45) | collective-permute-done | bytes 393248 | tf_op jit(solution)/shard_map/ppermute | solution.py:28
  342.3 10.3 %mixer_back.3 = (bf16[512,1152]{1,0:T(8,128)(2,1)}, bf16[32,1152]{1,0:T(8,128)(2,1)}, f32[1,4,768]{2,1,0:T(4,128)}, f32[1,4,256]{2,1,0:T(4,128)}, f32[1,8,128]{2,1,0:T(8,128)}) custom-call(f32[544,1152]{1,0:T(8,128)} %fusion.58.proj_ref.tail_ref, f32[544,1152]{1,0:T(8,128)} %fusion.58.proj_ref.tail_ref, ...), custom_call_target="tpu_custom_call", output_to_operand_aliasing={{0}: (12, {}), {1}: (13, {})} | custom-call | flops 900000000 | bytes 2700000 | tf_op jit(solution)/shard_map/mixer_back/pallas_call | solution.py:718
  382.8 10.2 %collective-permute-done.63 = bf16[256,1152]{1,0:T(8,128)(2,1)} collective-permute-done((bf16[256,1152]{1,0:T(8,128)(2,1)}, bf16[256,1152]{1,0:T(8,128)(2,1)}, u32[]{:S(2)}, u32[]{:S(2)}) %collective-permute-start.63) | collective-permute-done | bytes 589856 | tf_op jit(solution)/shard_map/ppermute | solution.py:28
  404.5 5.6 %collective-permute-start.65 = (bf16[64,1152]{1,0:T(8,128)(2,1)S(1)}, bf16[64,1152]{1,0:T(8,128)(2,1)S(1)}, u32[]{:S(2)}, u32[]{:S(2)}) collective-permute-start(bf16[64,1152]{1,0:T(8,128)(2,1)S(1)} %get-tuple-element.175), channel_id=1, source_target_pairs={{0,2},{2,0},{4,6},{6,4},{1,3},{3,1},{5,7},{7,5},{8,10},{10,8},{12,... | collective-permute-start | bytes 442376 | tf_op jit(solution)/shard_map/ppermute | solution.py:28
  427.8 9.9 %collective-permute-done.60 = bf16[64,2176]{1,0:T(8,128)(2,1)} collective-permute-done((bf16[64,2176]{1,0:T(8,128)(2,1)S(1)}, bf16[64,2176]{1,0:T(8,128)(2,1)}, u32[]{:S(2)}, u32[]{:S(2)}) %collective-permute-start.60) | collective-permute-done | bytes 278560 | tf_op jit(solution)/shard_map/ppermute | solution.py:28
  (432 shorter events, 250.3 us)
Async XLA Ops:
  26.1 29.9 %collective-permute-start.4 = (bf16[256,1152]{1,0:T(8,128)(2,1)}, bf16[256,1152]{1,0:T(8,128)(2,1)S(1)}, u32[]{:S(2)}, u32[]{:S(2)}) collective-permute-start(bf16[256,1152]{1,0:T(8,128)(2,1)} %bitcast.273), channel_id=1, source_target_pairs={{0,8},{8,0},{16,24},{24,16},{1,9},{9,1},{17,25},{25,17},{2,10},{10... | collective-permute-start | bytes 1769480 | tf_op jit(solution)/shard_map/ppermute | solution.py:28
  27.6 28.4 %collective-permute-start.5 = (bf16[256,1152]{1,0:T(8,128)(2,1)}, bf16[256,1152]{1,0:T(8,128)(2,1)S(1)}, u32[]{:S(2)}, u32[]{:S(2)}) collective-permute-start(bf16[256,1152]{1,0:T(8,128)(2,1)} %bitcast.274), channel_id=1, source_target_pairs={{0,16},{8,24},{16,0},{24,8},{1,17},{9,25},{17,1},{25,9},{2,18},{10... | collective-permute-start | bytes 1769480 | tf_op jit(solution)/shard_map/ppermute | solution.py:28
  29.1 26.9 %collective-permute-start.6 = (bf16[256,1152]{1,0:T(8,128)(2,1)}, bf16[256,1152]{1,0:T(8,128)(2,1)S(1)}, u32[]{:S(2)}, u32[]{:S(2)}) collective-permute-start(bf16[256,1152]{1,0:T(8,128)(2,1)} %bitcast.275), channel_id=1, source_target_pairs={{0,24},{8,16},{16,8},{24,0},{1,25},{9,17},{17,9},{25,1},{2,26},{10... | collective-permute-start | bytes 1769480 | tf_op jit(solution)/shard_map/ppermute | solution.py:28
  70.9 45.4 %collective-permute-start.11 = (bf16[256,1152]{1,0:T(8,128)(2,1)}, bf16[256,1152]{1,0:T(8,128)(2,1)}, u32[]{:S(2)}, u32[]{:S(2)}) collective-permute-start(bf16[256,1152]{1,0:T(8,128)(2,1)} %bitcast.20.refs_0_), channel_id=1, source_target_pairs={{0,16},{8,24},{16,0},{24,8},{1,17},{9,25},{17,1},{25,9},{2,18},{10... | collective-permute-start | bytes 1769480 | tf_op jit(solution)/shard_map/ppermute | solution.py:28
  86.3 30.0 %collective-permute-start.15 = (bf16[256,1024]{1,0:T(8,128)(2,1)}, bf16[256,1024]{1,0:T(8,128)(2,1)}, u32[]{:S(2)}, u32[]{:S(2)}) collective-permute-start(bf16[256,1024]{1,0:T(8,128)(2,1)} %collective-permute-done.13.refs_5_), channel_id=1, source_target_pairs={{0,8},{8,0},{16,24},{24,16},{1,9},{9,1},{17,25},{25,17},{2,10},{10... | collective-permute-start | bytes 1572872 | tf_op jit(solution)/shard_map/ppermute | solution.py:28
  87.8 28.5 %collective-permute-start.12 = (bf16[256,1152]{1,0:T(8,128)(2,1)}, bf16[256,1152]{1,0:T(8,128)(2,1)S(1)}, u32[]{:S(2)}, u32[]{:S(2)}) collective-permute-start(bf16[256,1152]{1,0:T(8,128)(2,1)} %collective-permute-done.10.refs_1_), channel_id=1, source_target_pairs={{0,16},{8,24},{16,0},{24,8},{1,17},{9,25},{17,1},{25,9},{2,18},{10... | collective-permute-start | bytes 1769480 | tf_op jit(solution)/shard_map/ppermute | solution.py:28
  131.6 35.2 %collective-permute-start.25 = (bf16[256,1536]{1,0:T(8,128)(2,1)S(1)}, bf16[256,1536]{1,0:T(8,128)(2,1)S(1)}, u32[]{:S(2)}, u32[]{:S(2)}) collective-permute-start(bf16[256,1536]{1,0:T(8,128)(2,1)S(1)} %bitcast.268), channel_id=1, source_target_pairs={{0,8},{8,0},{16,24},{24,16},{1,9},{9,1},{17,25},{25,17},{2,10},{10... | collective-permute-start | bytes 2359304 | tf_op jit(solution)/shard_map/ppermute | solution.py:28
  132.2 34.6 %collective-permute-start.26 = (bf16[256,1536]{1,0:T(8,128)(2,1)S(1)}, bf16[256,1536]{1,0:T(8,128)(2,1)S(1)}, u32[]{:S(2)}, u32[]{:S(2)}) collective-permute-start(bf16[256,1536]{1,0:T(8,128)(2,1)S(1)} %bitcast.269), channel_id=1, source_target_pairs={{0,16},{8,24},{16,0},{24,8},{1,17},{9,25},{17,1},{25,9},{2,18},{10... | collective-permute-start | bytes 2359304 | tf_op jit(solution)/shard_map/ppermute | solution.py:28
  132.2 34.6 %collective-permute-start.27 = (bf16[256,1536]{1,0:T(8,128)(2,1)S(1)}, bf16[256,1536]{1,0:T(8,128)(2,1)S(1)}, u32[]{:S(2)}, u32[]{:S(2)}) collective-permute-start(bf16[256,1536]{1,0:T(8,128)(2,1)S(1)} %bitcast.271), channel_id=1, source_target_pairs={{0,16},{8,24},{16,0},{24,8},{1,17},{9,25},{17,1},{25,9},{2,18},{10... | collective-permute-start | bytes 2359304 | tf_op jit(solution)/shard_map/ppermute | solution.py:28
  134.3 32.6 %collective-permute-start.28 = (bf16[256,1536]{1,0:T(8,128)(2,1)S(1)}, bf16[256,1536]{1,0:T(8,128)(2,1)S(1)}, u32[]{:S(2)}, u32[]{:S(2)}) collective-permute-start(bf16[256,1536]{1,0:T(8,128)(2,1)S(1)} %bitcast.272), channel_id=1, source_target_pairs={{0,8},{8,0},{16,24},{24,16},{1,9},{9,1},{17,25},{25,17},{2,10},{10... | collective-permute-start | bytes 2359304 | tf_op jit(solution)/shard_map/ppermute | solution.py:28
  177.2 32.9 %collective-permute-start.29 = (bf16[512,1024]{1,0:T(8,128)(2,1)}, bf16[512,1024]{1,0:T(8,128)(2,1)}, u32[]{:S(2)}, u32[]{:S(2)}) collective-permute-start(bf16[512,1024]{1,0:T(8,128)(2,1)} %convolution_convert_fusion.4), channel_id=1, source_target_pairs={{0,1},{1,0},{2,3},{3,2},{4,5},{5,4},{6,7},{7,6},{8,9},{9,8},{10,11... | collective-permute-start | bytes 3145736 | tf_op jit(solution)/shard_map/ppermute | solution.py:28
  228.0 42.0 %collective-permute-start.37 = (bf16[2,256,1536]{2,1,0:T(8,128)(2,1)}, bf16[2,256,1536]{2,1,0:T(8,128)(2,1)S(1)}, u32[]{:S(2)}, u32[]{:S(2)}) collective-permute-start(bf16[2,256,1536]{2,1,0:T(8,128)(2,1)} %pad_maximum_fusion.2), channel_id=1, source_target_pairs={{0,16},{8,24},{16,0},{24,8},{1,17},{9,25},{17,1},{25,9},{2,18},{10... | collective-permute-start | bytes 4718600 | tf_op jit(solution)/shard_map/ppermute | solution.py:28
  229.9 36.4 %collective-permute-start.38 = (bf16[2,256,1536]{2,1,0:T(8,128)(2,1)}, bf16[2,256,1536]{2,1,0:T(8,128)(2,1)}, u32[]{:S(2)}, u32[]{:S(2)}) collective-permute-start(bf16[2,256,1536]{2,1,0:T(8,128)(2,1)} %pad_maximum_fusion.3), channel_id=1, source_target_pairs={{0,8},{8,0},{16,24},{24,16},{1,9},{9,1},{17,25},{25,17},{2,10},{10... | collective-permute-start | bytes 4718600 | tf_op jit(solution)/shard_map/ppermute | solution.py:28
  266.4 26.4 %collective-permute-start.48 = (bf16[2,256,1024]{2,1,0:T(8,128)(2,1)}, bf16[2,256,1024]{2,1,0:T(8,128)(2,1)}, u32[]{:S(2)}, u32[]{:S(2)}) collective-permute-start(bf16[2,256,1024]{2,1,0:T(8,128)(2,1)} %dynamic-slice_bitcast_fusion.1), channel_id=1, source_target_pairs={{0,8},{8,0},{16,24},{24,16},{1,9},{9,1},{17,25},{25,17},{2,10},{10... | collective-permute-start | bytes 3145736 | tf_op jit(solution)/shard_map/ppermute | solution.py:28
  273.5 37.5 %collective-permute-start.39 = (bf16[2,144,768]{2,1,0:T(8,128)(2,1)}, bf16[2,144,768]{2,1,0:T(8,128)(2,1)S(1)}, u32[]{:S(2)}, u32[]{:S(2)}) collective-permute-start(bf16[2,144,768]{2,1,0:T(8,128)(2,1)} %get-tuple-element.90), channel_id=1, source_target_pairs={{2,0},{4,2},{6,4},{3,1},{5,3},{7,5},{10,8},{12,10},{14,12},{11,9},... | collective-permute-start | bytes 1327112 | tf_op jit(solution)/shard_map/ppermute | solution.py:34
  274.8 36.3 %collective-permute-start.40 = (bf16[2,144,768]{2,1,0:T(8,128)(2,1)}, bf16[2,144,768]{2,1,0:T(8,128)(2,1)}, u32[]{:S(2)}, u32[]{:S(2)}) collective-permute-start(bf16[2,144,768]{2,1,0:T(8,128)(2,1)} %get-tuple-element.90), channel_id=1, source_target_pairs={{4,0},{6,2},{5,1},{7,3},{12,8},{14,10},{13,9},{15,11},{20,16},{22,... | collective-permute-start | bytes 1327112 | tf_op jit(solution)/shard_map/ppermute | solution.py:34
  276.1 31.4 %collective-permute-start.42 = (bf16[256,1536]{1,0:T(8,128)(2,1)}, bf16[256,1536]{1,0:T(8,128)(2,1)}, u32[]{:S(2)}, u32[]{:S(2)}) collective-permute-start(bf16[256,1536]{1,0:T(8,128)(2,1)} %fusion.29), channel_id=1, source_target_pairs={{0,8},{8,0},{16,24},{24,16},{1,9},{9,1},{17,25},{25,17},{2,10},{10... | collective-permute-start | bytes 2359304 | tf_op jit(solution)/shard_map/ppermute | solution.py:28
  295.7 45.2 %collective-permute-start.47 = (bf16[2,256,1152]{2,1,0:T(8,128)(2,1)}, bf16[2,256,1152]{2,1,0:T(8,128)(2,1)S(1)}, u32[]{:S(2)}, u32[]{:S(2)}) collective-permute-start(bf16[2,256,1152]{2,1,0:T(8,128)(2,1)} %dynamic-slice_bitcast_fusion), channel_id=1, source_target_pairs={{0,16},{8,24},{16,0},{24,8},{1,17},{9,25},{17,1},{25,9},{2,18},{10... | collective-permute-start | bytes 3538952 | tf_op jit(solution)/shard_map/ppermute | solution.py:28
  311.0 29.9 %collective-permute-start.45 = (bf16[64,3072]{1,0:T(8,128)(2,1)S(1)}, bf16[64,3072]{1,0:T(8,128)(2,1)S(1)}, u32[]{:S(2)}, u32[]{:S(2)}) collective-permute-start(bf16[64,3072]{1,0:T(8,128)(2,1)S(1)} %get-tuple-element.160), channel_id=1, source_target_pairs={{0,4},{2,6},{4,0},{6,2},{1,5},{3,7},{5,1},{7,3},{8,12},{10,14},{12... | collective-permute-start | bytes 1179656 | tf_op jit(solution)/shard_map/ppermute | solution.py:28
  314.0 26.9 %collective-permute-start.46 = (bf16[64,3072]{1,0:T(8,128)(2,1)S(1)}, bf16[64,3072]{1,0:T(8,128)(2,1)S(1)}, u32[]{:S(2)}, u32[]{:S(2)}) collective-permute-start(bf16[64,3072]{1,0:T(8,128)(2,1)S(1)} %get-tuple-element.159), channel_id=1, source_target_pairs={{0,6},{2,4},{4,2},{6,0},{1,7},{3,5},{5,3},{7,1},{8,14},{10,12},{12... | collective-permute-start | bytes 1179656 | tf_op jit(solution)/shard_map/ppermute | solution.py:28
  358.1 60.0 %collective-permute-start.49 = (bf16[512,1024]{1,0:T(8,128)(2,1)}, bf16[512,1024]{1,0:T(8,128)(2,1)}, u32[]{:S(2)}, u32[]{:S(2)}) collective-permute-start(bf16[512,1024]{1,0:T(8,128)(2,1)} %add_convert_fusion), channel_id=1, source_target_pairs={{0,1},{1,0},{2,3},{3,2},{4,5},{5,4},{6,7},{7,6},{8,9},{9,8},{10,11... | collective-permute-start | bytes 3145736 | tf_op jit(solution)/shard_map/ppermute | solution.py:28
  365.1 27.9 %collective-permute-start.63 = (bf16[256,1152]{1,0:T(8,128)(2,1)}, bf16[256,1152]{1,0:T(8,128)(2,1)}, u32[]{:S(2)}, u32[]{:S(2)}) collective-permute-start(bf16[256,1152]{1,0:T(8,128)(2,1)} %get-tuple-element.148), channel_id=1, source_target_pairs={{0,16},{8,24},{16,0},{24,8},{1,17},{9,25},{17,1},{25,9},{2,18},{10... | collective-permute-start | bytes 1769480 | tf_op jit(solution)/shard_map/ppermute | solution.py:28
  377.7 26.8 %collective-permute-start.57 = (bf16[256,1152]{1,0:T(8,128)(2,1)S(1)}, bf16[256,1152]{1,0:T(8,128)(2,1)S(1)}, u32[]{:S(2)}, u32[]{:S(2)}) collective-permute-start(bf16[256,1152]{1,0:T(8,128)(2,1)S(1)} %copy-done.40), channel_id=1, source_target_pairs={{0,8},{8,0},{16,24},{24,16},{1,9},{9,1},{17,25},{25,17},{2,10},{10... | collective-permute-start | bytes 1769480 | tf_op jit(solution)/shard_map/ppermute | solution.py:28
  381.4 38.7 %collective-permute-start.51 = (bf16[32,1024]{1,0:T(8,128)(2,1)}, bf16[32,1024]{1,0:T(8,128)(2,1)S(1)}, u32[]{:S(2)}, u32[]{:S(2)}) collective-permute-start(bf16[32,1024]{1,0:T(8,128)(2,1)} %add_convert_fusion.4), channel_id=1, source_target_pairs={{2,0},{4,2},{6,4},{3,1},{5,3},{7,5},{10,8},{12,10},{14,12},{11,9},... | collective-permute-start | bytes 196616 | tf_op jit(solution)/shard_map/ppermute | solution.py:34
  (133 other events, 1570.2 us)
